TPU v7x, 32 devices: a whole 2x2x4 slice. The times are simulated.
32 devices in a mesh: attn: 8 (over z, y), proj: 4 (over x, core).
Axes of the slice: x: 2, y: 2, z: 4, core: 2. Of those that a mesh axis runs over, the one named last changes fastest.
Arguments:
- tokens: bfloat16 [4096, 4096], P('attn', 'proj'), may hold values from -6 to 6
- norm_gain: float32 [4096], replicated, may hold values from 0.1 to 1.9
- w_query: bfloat16 [4096, 4096], P(None, 'proj')
- w_key: bfloat16 [4096, 1024], P(None, 'proj')
- value_matrix: bfloat16 [4096, 1024], P(None, 'proj'), may hold values from -0.09375 to 0.09375
- doc_lengths: int32 [32], replicated, may hold values from 1 to 512, 4096 in all
- block_server: int32 [32], P('attn'), may hold values from 0 to 7, as said below
Outputs:
- attn_out: bfloat16 [4096, 4096], P('attn', 'proj')
- served_lse: float32 [32, 32, 128], P('attn', 'proj')
Inputs may be any that keep to these rules, and one draw needn't show every extreme that they name: `doc_lengths`: the lengths sum to 4096. `block_server`: query block b belongs to the micro-batch b // 4; every index of attn serves exactly 4 blocks, and at most one block of any one micro-batch.
All inputs are finite; a program needn't handle non-finite values.
Results may differ from a plain program's by a relative error of at most 0.0074.
Values may be sent and summed in bfloat16 or wider, within the bound.
No kernel may reach another device: no remote copies, remote signals or barrier semaphores. Data moves between devices by JAX's collectives and lax.ppermute only.
A program may use at most 128 MiB of HBM per device.

v0:
```python
import jax
import jax.numpy as jnp
from jax import lax
from jax.sharding import PartitionSpec as P

HEAD_SIZE = 128
QUERY_BLOCK_ROWS = 128


big_value = 1e30
norm_eps = 1e-05


def passed_along(block, axis, distance):
    devices = range(lax.axis_size(axis))
    route = [(i - distance, i) for i in devices if i - distance in devices]
    return lax.ppermute(block, axis, route)


def row_first(starts, position):
    return jnp.max(jnp.where(starts[None, :] <= position[:, None], starts[None, :], 0), axis=1)


def empty_state(kv_heads, group):
    running = jnp.full((kv_heads, group, QUERY_BLOCK_ROWS), -big_value, jnp.float32)
    total = jnp.zeros((kv_heads, group, QUERY_BLOCK_ROWS), jnp.float32)
    summed = jnp.zeros((kv_heads, group, QUERY_BLOCK_ROWS, HEAD_SIZE), jnp.float32)
    return (running, total, summed)


def attend(state, query_block, first_row, keys_values, key_start, starts, window):
    width = keys_values.shape[1] // 2
    kv_heads = width // HEAD_SIZE
    group = query_block.shape[1] // (kv_heads * HEAD_SIZE)
    count = keys_values.shape[0]
    row_extent = min(window, count)
    lowest = row_first(starts, first_row[None])[0]
    touches = (lowest < key_start + count) & (first_row + QUERY_BLOCK_ROWS > key_start)

    def update(current):
        running, total, summed = current
        offset = jnp.clip(lowest - key_start, 0, count - row_extent)
        rows_kv = lax.dynamic_slice_in_dim(keys_values, offset, row_extent, 0)
        key_pos = key_start + offset + jnp.arange(row_extent, dtype=jnp.int32)
        query_pos = first_row + jnp.arange(QUERY_BLOCK_ROWS, dtype=jnp.int32)
        bounds = row_first(starts, query_pos)
        allowed = (key_pos[None, :] >= bounds[:, None]) & (key_pos[None, :] <= query_pos[:, None])
        query_vectors = query_block.reshape(QUERY_BLOCK_ROWS, kv_heads, group, HEAD_SIZE)
        keys = rows_kv[:, :width].reshape(row_extent, kv_heads, HEAD_SIZE)
        values = rows_kv[:, width:].reshape(row_extent, kv_heads, HEAD_SIZE)
        scores = jnp.einsum(
            "qngd,knd->ngqk", query_vectors, keys, preferred_element_type=jnp.float32
        ) * (1.0 / HEAD_SIZE**0.5)
        scores = jnp.where(allowed, scores, -big_value)
        highest = jnp.maximum(running, jnp.max(scores, axis=-1))
        weights = jnp.where(allowed, jnp.exp(scores - highest[..., None]), 0.0)
        total = jnp.sum(weights, axis=-1)
        summed = jnp.einsum(
            "ngqk,knd->ngqd",
            weights.astype(jnp.bfloat16),
            values,
            preferred_element_type=jnp.float32,
        )
        return (highest, total, summed)

    return lax.cond(touches, update, lambda current: current, state)


def finish(state):
    running, total, summed = state
    result = summed / total[..., None]
    kv_heads, group = (result.shape[0], result.shape[1])
    result = (
        jnp.transpose(result, (2, 0, 1, 3))
        .reshape(QUERY_BLOCK_ROWS, kv_heads * group * HEAD_SIZE)
        .astype(jnp.bfloat16)
    )
    lse = (running + jnp.log(total)).reshape(kv_heads * group, QUERY_BLOCK_ROWS)
    return (result, lse)


def shards(tokens, norm_gain, w_query, w_key, value_matrix, doc_lengths, block_server):
    rows = tokens.shape[0]
    model_width = w_query.shape[0]
    query_width = w_query.shape[1]
    key_width = w_key.shape[1]
    kv_heads = key_width // HEAD_SIZE
    group = query_width // key_width
    blocks = rows // QUERY_BLOCK_ROWS
    servers = lax.axis_size("attn")
    me_attn = lax.axis_index("attn")
    wide = lax.all_gather(tokens, "proj", axis=1, tiled=True).astype(jnp.float32)
    scaled = (wide * norm_gain[None, :]).astype(jnp.bfloat16)
    part_q = jnp.dot(scaled, w_query, preferred_element_type=jnp.float32)
    part_k = jnp.dot(scaled, w_key, preferred_element_type=jnp.float32)
    part_v = jnp.dot(scaled, value_matrix, preferred_element_type=jnp.float32)
    squares = jnp.sum(wide * wide, axis=1, keepdims=True)
    part_q, part_k, part_v, squares = (part_q, part_k, part_v, squares)
    inverse = lax.rsqrt(squares / model_width + norm_eps)
    query_vectors = (part_q * inverse).astype(jnp.bfloat16)
    keys_values = jnp.concatenate(
        [(part_k * inverse).astype(jnp.bfloat16), (part_v * inverse).astype(jnp.bfloat16)], axis=1
    )
    ends = jnp.cumsum(doc_lengths)
    starts = ends - doc_lengths
    window = rows + QUERY_BLOCK_ROWS
    slot_ids = jnp.arange(servers, dtype=jnp.int32)
    sending = block_server[None, :] == slot_ids[:, None]
    global_ids = me_attn * blocks + jnp.arange(blocks, dtype=jnp.int32)
    send_id = (jnp.sum(jnp.where(sending, global_ids[None, :] + 1, 0), axis=1) - 1).reshape(
        servers, 1
    )
    prior = passed_along(keys_values, "attn", 1)
    local_keys = jnp.concatenate([prior, keys_values], axis=0)
    key_start = (me_attn - 1) * rows
    finished = []
    for index in range(blocks):
        state = attend(
            empty_state(kv_heads, group),
            query_vectors[index * QUERY_BLOCK_ROWS : (index + 1) * QUERY_BLOCK_ROWS],
            global_ids[index] * QUERY_BLOCK_ROWS,
            local_keys,
            key_start,
            starts,
            window,
        )
        finished.append(finish(state))
    attn_out = jnp.concatenate([item[0] for item in finished], axis=0)
    lses = jnp.stack([item[1] for item in finished])
    send_lse = jnp.sum(jnp.where(sending[:, :, None, None], lses[None], 0.0), axis=1)
    recv_lse, recv_id = (
        lax.all_to_all(
            send_lse.astype(jnp.bfloat16), "attn", split_axis=0, concat_axis=0, tiled=True
        ).astype(send_lse.dtype),
        lax.all_to_all(send_id, "attn", split_axis=0, concat_axis=0, tiled=True),
    )
    valid = recv_id[:, 0] >= 0
    ranks = jnp.cumsum(valid.astype(jnp.int32)) - 1
    picking = (ranks[None, :] == jnp.arange(blocks, dtype=jnp.int32)[:, None]) & valid[None, :]
    served_lse = jnp.sum(jnp.where(picking[:, :, None, None], recv_lse[None], 0.0), axis=1)
    return (attn_out, served_lse)


def solution(mesh):
    return jax.shard_map(
        shards,
        mesh=mesh,
        in_specs=(
            P("attn", "proj"),
            P(),
            P(None, "proj"),
            P(None, "proj"),
            P(None, "proj"),
            P(),
            P("attn"),
        ),
        out_specs=(P("attn", "proj"), P("attn", "proj", None)),
        check_vma=False,
    )
```

profile of v0, /device:TPU:0, one launch (start us, length us, event | category | flops | bytes accessed | tf_op | source)
XLA Modules:
  0.0 144.8 jit_solution(17752934451589359826)
XLA Ops:
  9.4 7.3 %all-to-all-start = ((s32[8,1,1]{2,1,0:T(1,128)}), s32[8,1,1]{2,1,0:T(1,128)S(1)}, u32[]{:S(2)}, u32[]{:S(2)}) async-start(s32[8,1,1]{2,1,0:T(1,128)} %copy.124), calls=%async_computation | async-start | bytes 8192 | tf_op jit(solution)/shard_map/all_to_all | solution.py:135
  21.6 1.4 fusion.64
  26.4 20.4 %all-gather.2.cloned.1.call-done = bf16[512,4096]{1,0:T(8,128)(2,1)} async-done(((bf16[512,1024]{1,0:T(8,128)(2,1)}), bf16[512,4096]{1,0:T(8,128)(2,1)}) %all-gather.2.cloned.1.call-update) | async-done | bytes 4194320 | tf_op jit(solution)/shard_map/all_gather | solution.py:92
  46.8 3.2 %fusion.37 = f32[512]{0:T(512)S(1)} fusion(bf16[512,4096]{1,0:T(8,128)(2,1)} %all-gather.2.cloned.1.call-done), kind=kLoop, calls=%fused_computation.67 | loop fusion | flops 6290944 | bytes 4196352 | tf_op jit(solution)/shard_map/reduce_sum | solution.py:97
  50.3 1.4 fusion.52
  51.8 1.3 fusion.55
  53.2 3.5 %collective-permute-start = (bf16[512,512]{0,1:T(8,128)(2,1)S(1)}, bf16[512,512]{0,1:T(8,128)(2,1)S(1)}, u32[]{:S(2)}, u32[]{:S(2)}) collective-permute-start(bf16[512,512]{0,1:T(8,128)(2,1)S(1)} %pad_maximum_fusion.1), channel_id=1, source_target_pairs={{0,4},{4,8},{8,12},{12,16},{16,20},{20,24},{24,28},{1,5},{5,9},{9,... | collective-permute-start | bytes 1572872 | tf_op jit(solution)/shard_map/ppermute | solution.py:17
  56.8 4.6 %multiply_convert_fusion = bf16[512,1024]{1,0:T(8,128)(2,1)S(1)} fusion(bf16[4096,1024]{1,0:T(8,128)(2,1)S(1)} %bitcast.144, bf16[512,4096]{1,0:T(8,128)(2,1)S(1)} %copy-done.1, f32[4096]{0:T(1024)S(1)} %copy-done.4, f32[512]{0:T(512)S(1)} %add_rsqrt_fusion), kind=kOutput, calls=%fused_computation.71 | convolution fusion | flops 4302307328 | bytes 13649920 | tf_op jit(solution)/shard_map/dot_general | solution.py:94
  61.4 6.9 %collective-permute-done = bf16[512,512]{0,1:T(8,128)(2,1)S(1)} collective-permute-done((bf16[512,512]{0,1:T(8,128)(2,1)S(1)}, bf16[512,512]{0,1:T(8,128)(2,1)S(1)}, u32[]{:S(2)}, u32[]{:S(2)}) %collective-permute-start) | collective-permute-done | bytes 524320 | tf_op jit(solution)/shard_map/ppermute | solution.py:17
  69.4 10.9 %conditional.4 = (f32[2,4,128]{2,1,0:T(4,128)}, f32[2,4,128]{2,1,0:T(4,128)}, f32[2,4,128,128]{3,2,1,0:T(8,128)}, f32[2,4,128]{2,1,0:T(4,128)S(1)}) conditional(s32[]{:T(128)} %convert_element_type.96, () %tuple.48, (s32[]{:T(128)}, s32[]{:T(128)}, s32[32]{0:T(128)S(1)}, s32[]{:T(128)}, bf16[1024,512]{0,1:T(8,128)(2,1)}, ...), branch_computations={%region_3.4_spmd, %region_4.8_spmd} | conditional | flops 344321664 | bytes 13606636 | solution.py:66
  70.1 1.3 copy.116
  72.7 1.4 fusion.68
  75.3 1.9 %fusion.2 = f32[2,4,128]{2,1,0:T(4,128)} fusion(f32[2,640,128,4]{2,1,3,0:T(8,128)S(1)} %get-tuple-element.242, f32[2,4,128]{2,1,0:T(4,128)} %broadcast_maximum_fusion, pred[128,640]{0,1:T(8,128)(4,1)S(1)} %compare_and_fusion), kind=kLoop, calls=%fused_computation.4 | loop fusion | flops 3275776 | bytes 2711552 | tf_op jit(solution)/shard_map/cond/branch_1_fun/reduce_sum | solution.py:57
  77.2 2.4 %fusion.3 = f32[2,4,128,128]{3,2,1,0:T(8,128)} fusion(bf16[640,2,128,1]{0,2,3,1:T(8,128)(2,1)S(1)} %bitcast.133, f32[2,640,128,4]{2,1,3,0:T(8,128)S(1)} %get-tuple-element.242, f32[2,4,128]{2,1,0:T(4,128)} %broadcast_maximum_fusion, pred[128,640]{0,1:T(8,128)(4,1)S(1)} %compare_and_fusion), kind=kOutput, calls=%fused_computation.5 | convolution fusion | flops 171048960 | bytes 3559424 | tf_op jit(solution)/shard_map/cond/branch_1_fun/ngqk,knd->ngqd/dot_general | solution.py:58
  82.7 10.8 %conditional.5 = (f32[2,4,128]{2,1,0:T(4,128)}, f32[2,4,128]{2,1,0:T(4,128)}, f32[2,4,128,128]{3,2,1,0:T(8,128)}, f32[2,4,128]{2,1,0:T(4,128)S(1)}) conditional(s32[]{:T(128)} %convert_element_type.105, () %tuple.50, (s32[]{:T(128)}, s32[]{:T(128)}, s32[32]{0:T(128)S(1)}, s32[]{:T(128)}, bf16[1024,512]{0,1:T(8,128)(2,1)}, ...), branch_computations={%region_9.10_spmd, %region_10.14_spmd} | conditional | flops 344321664 | bytes 13606636 | solution.py:66
  83.3 1.3 copy.118
  85.9 1.4 fusion.69
  88.5 1.9 %fusion.11 = f32[2,4,128]{2,1,0:T(4,128)} fusion(f32[2,640,128,4]{2,1,3,0:T(8,128)S(1)} %get-tuple-element.246, f32[2,4,128]{2,1,0:T(4,128)} %broadcast_maximum_fusion.1, pred[128,640]{0,1:T(8,128)(4,1)S(1)} %compare_and_fusion.1), kind=kLoop, calls=%fused_computation.20 | loop fusion | flops 3275776 | bytes 2711552 | tf_op jit(solution)/shard_map/cond/branch_1_fun/reduce_sum | solution.py:57
  90.4 2.4 %fusion.12 = f32[2,4,128,128]{3,2,1,0:T(8,128)} fusion(bf16[640,2,128,1]{0,2,3,1:T(8,128)(2,1)S(1)} %bitcast.134, f32[2,640,128,4]{2,1,3,0:T(8,128)S(1)} %get-tuple-element.246, f32[2,4,128]{2,1,0:T(4,128)} %broadcast_maximum_fusion.1, pred[128,640]{0,1:T(8,128)(4,1)S(1)} %compare_and_fusion.1), kind=kOutput, calls=%fused_computation.21 | convolution fusion | flops 171048960 | bytes 3559424 | tf_op jit(solution)/shard_map/cond/branch_1_fun/ngqk,knd->ngqd/dot_general | solution.py:58
  95.8 10.9 %conditional.6 = (f32[2,4,128]{2,1,0:T(4,128)}, f32[2,4,128]{2,1,0:T(4,128)}, f32[2,4,128,128]{3,2,1,0:T(8,128)}, f32[2,4,128]{2,1,0:T(4,128)S(1)}) conditional(s32[]{:T(128)} %convert_element_type.109, () %tuple.52, (s32[]{:T(128)}, s32[]{:T(128)}, s32[32]{0:T(128)S(1)}, s32[]{:T(128)}, bf16[1024,512]{0,1:T(8,128)(2,1)}, ...), branch_computations={%region_15.16_spmd, %region_16.20_spmd} | conditional | flops 344321664 | bytes 13606636 | solution.py:66
  96.5 1.3 copy.120
  99.1 1.4 fusion.70
  101.7 1.9 %fusion.20 = f32[2,4,128]{2,1,0:T(4,128)} fusion(f32[2,640,128,4]{2,1,3,0:T(8,128)S(1)} %get-tuple-element.250, f32[2,4,128]{2,1,0:T(4,128)} %broadcast_maximum_fusion.2, pred[128,640]{0,1:T(8,128)(4,1)S(1)} %compare_and_fusion.2), kind=kLoop, calls=%fused_computation.36 | loop fusion | flops 3275776 | bytes 2711552 | tf_op jit(solution)/shard_map/cond/branch_1_fun/reduce_sum | solution.py:57
  103.6 2.4 %fusion.21 = f32[2,4,128,128]{3,2,1,0:T(8,128)} fusion(bf16[640,2,128,1]{0,2,3,1:T(8,128)(2,1)S(1)} %bitcast.135, f32[2,640,128,4]{2,1,3,0:T(8,128)S(1)} %get-tuple-element.250, f32[2,4,128]{2,1,0:T(4,128)} %broadcast_maximum_fusion.2, pred[128,640]{0,1:T(8,128)(4,1)S(1)} %compare_and_fusion.2), kind=kOutput, calls=%fused_computation.37 | convolution fusion | flops 171048960 | bytes 3559424 | tf_op jit(solution)/shard_map/cond/branch_1_fun/ngqk,knd->ngqd/dot_general | solution.py:58
  109.1 10.2 %conditional.7 = (f32[2,4,128]{2,1,0:T(4,128)}, f32[2,4,128]{2,1,0:T(4,128)}, f32[2,4,128,128]{3,2,1,0:T(8,128)S(1)}, f32[2,4,128]{2,1,0:T(4,128)S(1)}) conditional(s32[]{:T(128)} %convert_element_type.113, () %tuple.54, (s32[]{:T(128)}, s32[]{:T(128)}, s32[32]{0:T(128)S(1)}, s32[]{:T(128)}, bf16[1024,512]{0,1:T(8,128)(2,1)}, ...), branch_computations={%region_21.22_spmd, %region_22.26_spmd} | conditional | flops 344321664 | bytes 13606636 | solution.py:66
  109.8 1.3 copy.122
  112.4 1.4 fusion.71
  115.0 1.9 %fusion.29 = f32[2,4,128]{2,1,0:T(4,128)} fusion(f32[2,640,128,4]{2,1,3,0:T(8,128)S(1)} %get-tuple-element.254, f32[2,4,128]{2,1,0:T(4,128)} %broadcast_maximum_fusion.3, pred[128,640]{0,1:T(8,128)(4,1)S(1)} %compare_and_fusion.3), kind=kLoop, calls=%fused_computation.52 | loop fusion | flops 3275776 | bytes 2711552 | tf_op jit(solution)/shard_map/cond/branch_1_fun/reduce_sum | solution.py:57
  116.9 1.6 %fusion.30 = f32[2,4,128,128]{3,2,1,0:T(8,128)S(1)} fusion(bf16[640,2,128,1]{0,2,3,1:T(8,128)(2,1)S(1)} %bitcast.136, f32[2,640,128,4]{2,1,3,0:T(8,128)S(1)} %get-tuple-element.254, f32[2,4,128]{2,1,0:T(4,128)} %broadcast_maximum_fusion.3, pred[128,640]{0,1:T(8,128)(4,1)S(1)} %compare_and_fusion.3), kind=kOutput, calls=%fused_computation.53 | convolution fusion | flops 171048960 | bytes 3559424 | tf_op jit(solution)/shard_map/cond/branch_1_fun/ngqk,knd->ngqd/dot_general | solution.py:58
  124.0 6.6 %all-to-all-start.1 = ((bf16[8,8,128]{2,1,0:T(8,128)(2,1)}), bf16[8,8,128]{2,1,0:T(8,128)(2,1)S(1)}, u32[]{:S(2)}, u32[]{:S(2)}) async-start(bf16[8,8,128]{2,1,0:T(8,128)(2,1)} %select_reduce_fusion.5), calls=%async_computation.1 | async-start | bytes 32768 | tf_op jit(solution)/shard_map/all_to_all | solution.py:132
  130.6 2.1 %pad_maximum_fusion = bf16[512,1024]{1,0:T(8,128)(2,1)} fusion(bf16[128,1024]{1,0:T(8,128)(2,1)S(1)} %convert_element_type.116, bf16[128,1024]{1,0:T(8,128)(2,1)} %convert_element_type.112, bf16[128,1024]{1,0:T(8,128)(2,1)} %convert_element_type.108, bf16[128,1024]{1,0:T(8,128)(2,1)S(1)} %copy-done.2), kind=kLoop, calls=%fused_computation.77 | loop fusion | flops 4194304 | bytes 2097152 | tf_op jit(solution)/shard_map/concatenate | solution.py:128
  132.7 4.5 %all-to-all-done.1 = bf16[8,8,128]{2,1,0:T(8,128)(2,1)S(1)} async-done(((bf16[8,8,128]{2,1,0:T(8,128)(2,1)}), bf16[8,8,128]{2,1,0:T(8,128)(2,1)S(1)}, u32[]{:S(2)}, u32[]{:S(2)}) %all-to-all-start.1) | async-done | bytes 16416 | tf_op jit(solution)/shard_map/all_to_all | solution.py:132
  (88 shorter events, 31.7 us)
Async XLA Ops:
  7.2 42.9 %copy-start = (bf16[4096,256]{1,0:T(8,128)(2,1)S(1)}, bf16[4096,256]{1,0:T(8,128)(2,1)}, u32[]{:S(2)}) copy-start(bf16[4096,256]{1,0:T(8,128)(2,1)} %param.19) | copy-start | bytes 6291460
  7.2 42.9 %copy-start.4 = (f32[4096]{0:T(1024)S(1)}, f32[4096]{0:T(1024)}, u32[]{:S(2)}) copy-start(f32[4096]{0:T(1024)} %param.16) | copy-start | bytes 49156
  7.2 39.6 %all-gather.2.cloned.1.call-start = ((), (), s32[]{:S(2)}) async-start(), calls=%async_computation.2 | async-start | bytes 5242880 | tf_op jit(solution)/shard_map/all_gather | solution.py:92
  9.4 16.3 %all-to-all-start = ((s32[8,1,1]{2,1,0:T(1,128)}), s32[8,1,1]{2,1,0:T(1,128)S(1)}, u32[]{:S(2)}, u32[]{:S(2)}) async-start(s32[8,1,1]{2,1,0:T(1,128)} %copy.124), calls=%async_computation | async-start | bytes 8192 | tf_op jit(solution)/shard_map/all_to_all | solution.py:135
  46.8 3.4 %copy-start.1 = (bf16[512,4096]{1,0:T(8,128)(2,1)S(1)}, bf16[512,4096]{1,0:T(8,128)(2,1)}, u32[]{:S(2)}) copy-start(bf16[512,4096]{1,0:T(8,128)(2,1)} %all-gather.2.cloned.1.call-done) | copy-start | bytes 12582916
  50.2 1.6 %copy-start.3 = (bf16[4096,256]{1,0:T(8,128)(2,1)S(1)}, bf16[4096,256]{1,0:T(8,128)(2,1)}, u32[]{:S(2)}) copy-start(bf16[4096,256]{1,0:T(8,128)(2,1)} %param.18) | copy-start | bytes 6291460
  50.2 6.5 %slice-start = ((s8[8388608]{0:T(1024)(128)(4,1)}), s8[4194304]{0:T(1024)(128)(4,1)S(1)}, s32[]{:S(2)}) async-start(s8[8388608]{0:T(1024)(128)(4,1)} %bitcast.143), calls=%async_computation.3 | async-start | bytes 8388608
  51.8 4.9 %slice-start.1 = ((s8[8388608]{0:T(1024)(128)(4,1)}), s8[4194304]{0:T(1024)(128)(4,1)S(1)}, s32[]{:S(2)}) async-start(s8[8388608]{0:T(1024)(128)(4,1)} %bitcast.143), calls=%async_computation.4 | async-start | bytes 8388608
  53.2 15.1 %collective-permute-start = (bf16[512,512]{0,1:T(8,128)(2,1)S(1)}, bf16[512,512]{0,1:T(8,128)(2,1)S(1)}, u32[]{:S(2)}, u32[]{:S(2)}) collective-permute-start(bf16[512,512]{0,1:T(8,128)(2,1)S(1)} %pad_maximum_fusion.1), channel_id=1, source_target_pairs={{0,4},{4,8},{8,12},{12,16},{16,20},{20,24},{24,28},{1,5},{5,9},{9,... | collective-permute-start | bytes 1572872 | tf_op jit(solution)/shard_map/ppermute | solution.py:17
  109.1 21.6 %copy-start.2 = (bf16[128,1024]{1,0:T(8,128)(2,1)S(1)}, bf16[128,1024]{1,0:T(8,128)(2,1)}, u32[]{:S(2)}) copy-start(bf16[128,1024]{1,0:T(8,128)(2,1)} %convert_element_type.104) | copy-start | bytes 786436
  124.0 13.2 %all-to-all-start.1 = ((bf16[8,8,128]{2,1,0:T(8,128)(2,1)}), bf16[8,8,128]{2,1,0:T(8,128)(2,1)S(1)}, u32[]{:S(2)}, u32[]{:S(2)}) async-start(bf16[8,8,128]{2,1,0:T(8,128)(2,1)} %select_reduce_fusion.5), calls=%async_computation.1 | async-start | bytes 32768 | tf_op jit(solution)/shard_map/all_to_all | solution.py:132
Sparse Core Ops, SparseCore 0:
  9.6 37.1 all-gather.1
where the time goes:
time: 146 us; the launch traced here: 145 us
  waiting for transfers between devices  32.5 us (22%)
  other arithmetic  30.1 us (21%)
  local copies, waits for them, and re-layouts  23.8 us (16%)
  between operations  19.5 us (13%)
  matrix products  18.5 us (13%)
  starting transfers between devices  17.5 us (12%)
  loops' own time  2.86 us (2%)
    all_gather x1, waiting for transfers between devices, shards(): lax.all_gather(tokens, 'proj', axis=1, tiled=True).astype(jnp.float32)  20.4 us
    dot_general x4, matrix products, update(): jnp.einsum('ngqk,knd->ngqd', weights.astype(jnp.bfloat16), values, prefer...  8.91 us
    reduce_sum x4, other arithmetic, update(): total = jnp.sum(weights, axis=-1)  7.64 us
    all_to_all x1, starting transfers between devices, shards(): lax.all_to_all(send_id, 'attn', split_axis=0, concat_axis=0, tiled=True)  7.28 us
    ppermute x1, waiting for transfers between devices, passed_along(): return lax.ppermute(block, axis, route)  6.92 us
    all_to_all x1, starting transfers between devices, shards(): lax.all_to_all(send_lse.astype(jnp.bfloat16), 'attn', split_axis=0, conca...  6.64 us
    another operation x5, local copies, waits for them, and re-layouts  6.12 us
    slice x4, local copies, waits for them, and re-layouts, update(): values = rows_kv[:, width:].reshape(row_extent, kv_heads, HEAD_SIZE)  5.59 us
  transfers between devices with their start and end apart: 4, of which 3 were waited for; matrix products, arithmetic and copies ran while one was open for 9% of the time, Pallas kernels for 0%

commit v1 on v0

v1 whole, which is shorter than its diff:
```python
import functools
import math

import jax
import jax.numpy as jnp
from jax import lax
from jax.experimental import pallas as pl
from jax.experimental.pallas import tpu as pltpu
from jax.sharding import PartitionSpec as P

HEAD_SIZE = 128
QUERY_BLOCK_ROWS = 128
CORES = 2

masked_value = -1e30
norm_eps = 1e-05
score_scale = 1.0 / HEAD_SIZE**0.5
log2_scale = score_scale * math.log2(math.e)

VMEM = pl.BlockSpec(memory_space=pltpu.VMEM)
SMEM = pl.BlockSpec(memory_space=pltpu.SMEM)
HBM = pl.BlockSpec(memory_space=pltpu.HBM)


def params(limit=16 << 20):
    return pltpu.CompilerParams(vmem_limit_bytes=limit)


def part_terms(x, gain):
    values = x.astype(jnp.float32)
    scaled = (values * gain).astype(jnp.bfloat16)
    return scaled, jnp.sum(values * values, axis=1, keepdims=True)


def cost():
    return pl.CostEstimate(flops=1 << 10, bytes_accessed=1 << 10, transcendentals=0)


class Weights:
    def __init__(self, order_ref, slots, features, hbm, vmem, sems):
        self.copies = {}
        for kind, (src, dst) in enumerate(zip(hbm, vmem)):
            for i, slot in enumerate(slots):
                start = pl.multiple_of(order_ref[slot] * features, features)
                rows = pl.ds(i * features, features)
                copy = pltpu.make_async_copy(
                    src.at[pl.ds(start, features), :], dst.at[rows, :], sems.at[kind, i]
                )
                copy.start()
                self.copies[kind, i] = copy
        self.vmem = vmem

    def product(self, scaled, kind):
        for (k, _), copy in self.copies.items():
            if k == kind:
                copy.wait()
        return jnp.dot(scaled, self.vmem[kind][...], preferred_element_type=jnp.float32)


def weight_scratch(count, features, weights):
    return [pltpu.VMEM((count * features, w.shape[1]), jnp.bfloat16) for w in weights] + [
        pltpu.SemaphoreType.DMA((len(weights), count))
    ]


def local_kernel(order_ref, docs_ref, x_ref, other_ref, gain_ref, wk, wv, wq, q_ref, kv_ref, sq_ref, bound_ref, *scratch):
    features = x_ref.shape[1]
    shape = bound_ref.shape
    base = order_ref[order_ref.shape[0] - 1]
    position = lax.broadcasted_iota(jnp.int32, shape, 0) * shape[1] + lax.broadcasted_iota(jnp.int32, shape, 1)
    start = -base
    bounds = jnp.full(shape, start, jnp.int32)
    for d in range(docs_ref.shape[0]):
        bounds = jnp.where(position >= start, start, bounds)
        start = start + docs_ref[d]
    bound_ref[...] = bounds
    width = wk.shape[1]
    weights = Weights(order_ref, range(CORES), features, (wk, wv, wq), scratch[:3], scratch[3])
    parts = [
        part_terms(ref[...], gain_ref[pl.ds(order_ref[slot], 1), :]) for slot, ref in enumerate((x_ref, other_ref))
    ]
    sq_ref[...] = parts[0][1] + parts[1][1]
    scaled = jnp.concatenate([part[0] for part in parts], axis=1)
    kv_ref[:, :width] = weights.product(scaled, 0)
    kv_ref[:, width:] = weights.product(scaled, 1)
    q_ref[...] = weights.product(scaled, 2)


def local_part(order, docs, x, other, gains, wk, wv, wq):
    rows, features = x.shape
    q_width, kv_width = wq.shape[1], 2 * wk.shape[1]
    return pl.pallas_call(
        local_kernel,
        out_shape=(
            jax.ShapeDtypeStruct((rows, q_width), jnp.float32),
            jax.ShapeDtypeStruct((rows, kv_width), jnp.float32),
            jax.ShapeDtypeStruct((rows, 1), jnp.float32),
            jax.ShapeDtypeStruct((rows // QUERY_BLOCK_ROWS, QUERY_BLOCK_ROWS), jnp.int32),
        ),
        in_specs=[SMEM, SMEM, VMEM, VMEM, VMEM, HBM, HBM, HBM],
        out_specs=(VMEM,) * 4,
        scratch_shapes=weight_scratch(CORES, features, (wk, wv, wq)),
        compiler_params=params(24 << 20),
        cost_estimate=cost(),
    )(order, docs, x, other, gains, wk, wv, wq)


def chunk_kernel(count, halves, row, want_kv, want_q, order_ref, *refs):
    it = iter(refs)
    groups = [[next(it) for _ in range(halves if i % CORES else 1)] for i in range(count)]
    gain_ref = next(it)
    hbm = [next(it) for _ in range(2 * want_kv + want_q)]
    kva_ref, sq_ref = (next(it), next(it)) if want_kv else (None, None)
    inv_ref = None if want_kv else next(it)
    qa_ref = next(it) if want_q else None
    kv_ref, inv_out = (next(it), next(it)) if want_kv else (None, None)
    q_ref = next(it) if want_q else None
    *vmem, sems = it
    features = groups[0][0].shape[1]
    weights = Weights(order_ref, [CORES + i for i in range(count)], features, hbm, vmem, sems)
    scaled, squares = [], []
    for i, group in enumerate(groups):
        x = jnp.concatenate([ref[...] for ref in group], axis=0)
        part, square = part_terms(x, gain_ref[pl.ds(order_ref[CORES + i], 1), :])
        scaled.append(part)
        squares.append(square)
    scaled = jnp.concatenate(scaled, axis=1)
    rows = scaled.shape[0]
    here = slice(row, row + rows)
    if want_kv:
        width = hbm[0].shape[1]
        inverse = lax.rsqrt((sq_ref[here, :] + sum(squares)) / (features * (count + CORES)) + norm_eps)
        inv_out[...] = inverse
        for kind in range(2):
            columns = slice(kind * width, (kind + 1) * width)
            total = kva_ref[here, columns] + weights.product(scaled, kind)
            kv_ref[:, columns] = (total * inverse).astype(jnp.bfloat16)
    else:
        inverse = inv_ref[...]
    if want_q:
        total = qa_ref[here, :] + weights.product(scaled, len(hbm) - 1)
        q_ref[...] = (total * inverse).astype(jnp.bfloat16)


def project(row, order, groups, gains, wk=None, wv=None, wq=None, kv_acc=None, squares=None, inverse=None, q_acc=None):
    want_kv, want_q = wk is not None, wq is not None
    count, (rows, features) = len(groups), groups[0][0].shape
    weights = ([wk, wv] if want_kv else []) + ([wq] if want_q else [])
    pieces = [piece for group in groups for piece in group]
    accs = ([kv_acc, squares] if want_kv else [inverse]) + ([q_acc] if want_q else [])
    shapes = []
    if want_kv:
        shapes += [jax.ShapeDtypeStruct((rows, 2 * wk.shape[1]), jnp.bfloat16), jax.ShapeDtypeStruct((rows, 1), jnp.float32)]
    if want_q:
        shapes += [jax.ShapeDtypeStruct((rows, wq.shape[1]), jnp.bfloat16)]
    return pl.pallas_call(
        functools.partial(chunk_kernel, count, len(groups[1]), row, want_kv, want_q),
        out_shape=tuple(shapes),
        in_specs=[SMEM] + [VMEM] * (len(pieces) + 1) + [HBM] * len(weights) + [VMEM] * len(accs),
        out_specs=(VMEM,) * len(shapes),
        scratch_shapes=weight_scratch(count, features, weights),
        compiler_params=params(24 << 20),
        cost_estimate=cost(),
    )(order, *pieces, gains, *weights, *accs)


def block_attention(q, bounds, keys_values, key_starts, row_start, store):
    rows = q.shape[0]
    width = keys_values[0].shape[1] // 2
    kv_heads = width // HEAD_SIZE
    group = q.shape[1] // width
    bounds = jnp.transpose(jnp.broadcast_to(bounds, (QUERY_BLOCK_ROWS, rows)))
    query_pos = row_start + lax.broadcasted_iota(jnp.int32, (rows, QUERY_BLOCK_ROWS), 0)
    allowed = []
    for start in key_starts:
        key_pos = start + lax.broadcasted_iota(jnp.int32, (rows, QUERY_BLOCK_ROWS), 1)
        ok = key_pos >= bounds
        if start == row_start:
            ok = ok & (key_pos <= query_pos)
        allowed.append(jnp.concatenate([ok] * group, axis=0))
    lse_rows = []
    for n in range(kv_heads):
        stacked = jnp.concatenate(
            [q[:, (n * group + g) * HEAD_SIZE : (n * group + g + 1) * HEAD_SIZE] for g in range(group)],
            axis=0,
        )
        scores = []
        highest = None
        for ok, ref in zip(allowed, keys_values):
            s = lax.dot_general(
                stacked,
                ref[:, n * HEAD_SIZE : (n + 1) * HEAD_SIZE],
                (((1,), (1,)), ((), ())),
                preferred_element_type=jnp.float32,
            )
            s = jnp.where(ok, s, masked_value)
            scores.append(s)
            highest = s if highest is None else jnp.maximum(highest, s)
        highest = jnp.max(highest, axis=1, keepdims=True)
        total = None
        summed = None
        for s, ref in zip(scores, keys_values):
            weights = jnp.exp2((s - highest) * log2_scale)
            total = weights if total is None else total + weights
            product = jnp.dot(
                weights.astype(jnp.bfloat16),
                ref[:, width + n * HEAD_SIZE : width + (n + 1) * HEAD_SIZE],
                preferred_element_type=jnp.float32,
            )
            summed = product if summed is None else summed + product
        total = jnp.sum(total, axis=1, keepdims=True)
        result = (summed / total).astype(jnp.bfloat16)
        lse = highest * score_scale + jnp.log(total)
        for g in range(group):
            store(n * group + g, result[g * rows : (g + 1) * rows])
            lse_rows.append(lse[g * rows : (g + 1) * rows])
    lane = lax.broadcasted_iota(jnp.int32, (rows, HEAD_SIZE), 1)
    table = jnp.zeros((rows, HEAD_SIZE), jnp.float32)
    for h, column in enumerate(lse_rows):
        table = jnp.where(lane == h, column, table)
    return jnp.transpose(table)[: len(lse_rows), :]


def main_attention_kernel(blocks, *refs):
    qs, owns, priors = refs[: blocks - 1], refs[blocks - 1 : 2 * blocks - 1], refs[2 * blocks - 1 : 3 * blocks - 2]
    bounds_ref, out_ref, lse_ref = refs[3 * blocks - 2 :]
    rows = QUERY_BLOCK_ROWS
    for block in range(1, blocks):
        def store(head, value, block=block):
            out_ref[block * rows : (block + 1) * rows, head * HEAD_SIZE : (head + 1) * HEAD_SIZE] = value

        lse_ref[block - 1] = block_attention(
            qs[block - 1][...],
            bounds_ref[block : block + 1, :],
            [*priors[block - 1 :], *owns[: block + 1]],
            [(i - blocks) * rows for i in range(block, blocks)] + [i * rows for i in range(block + 1)],
            block * rows,
            store,
        )


def last_attention_kernel(blocks, servers, *refs):
    server_ref, q_ref, own_ref = refs[:3]
    priors = refs[3 : 3 + blocks]
    bounds_ref, lse_ref, _, out_ref, send_ref = refs[3 + blocks :]
    rows = QUERY_BLOCK_ROWS

    def store(head, value):
        out_ref[:, head * HEAD_SIZE : (head + 1) * HEAD_SIZE] = value

    lses = [
        block_attention(
            q_ref[...],
            bounds_ref[:1, :],
            [*priors, own_ref],
            [(i - blocks) * rows for i in range(blocks)] + [0],
            0,
            store,
        )
    ]
    lses += [lse_ref[i] for i in range(blocks - 1)]
    for s in range(servers):
        value = jnp.full(lses[0].shape, jnp.inf, jnp.float32)
        for i in range(blocks):
            value = jnp.where(server_ref[i] == s, lses[i], value)
        send_ref[s] = value.astype(jnp.bfloat16)


def pick_kernel(blocks, recv_ref, out_ref):
    shape = recv_ref.shape[1:]
    rank = jnp.zeros(shape, jnp.int32)
    picked = [jnp.zeros(shape, jnp.float32) for _ in range(blocks)]
    for i in range(recv_ref.shape[0]):
        value = recv_ref[i].astype(jnp.float32)
        valid = value < jnp.inf
        for k in range(blocks):
            picked[k] = jnp.where(valid & (rank == k), value, picked[k])
        rank = rank + valid.astype(jnp.int32)
    for k in range(blocks):
        out_ref[k] = picked[k]


def shards(tokens, norm_gain, w_query, w_key, value_matrix, doc_lengths, block_server):
    rows, features = tokens.shape
    width = w_key.shape[1]
    heads = w_query.shape[1] // HEAD_SIZE
    block = QUERY_BLOCK_ROWS
    blocks = rows // block
    servers = lax.axis_size("attn")
    sharers = lax.axis_size("proj")
    chips = sharers // CORES
    me_attn = lax.axis_index("attn")
    me_proj = lax.axis_index("proj")
    sibling = [(i, i ^ 1) for i in range(sharers)]

    def across(distance):
        return [(i, (i + distance * CORES) % sharers) for i in range(sharers)]

    chunks = list(range(blocks))[::-1]
    arrived = {}
    rest = tokens
    for c in chunks:
        piece = rest[c * block : (c + 1) * block]
        if c == chunks[0]:
            piece, rest = lax.optimization_barrier((piece, rest))
        arrived[c] = [lax.ppermute(piece, "proj", across(d)) for d in range(1, chips)]
    other = lax.ppermute(tokens, "proj", sibling)

    order = [me_proj, me_proj ^ 1]
    for d in range(1, chips):
        source = (me_proj + sharers - d * CORES) % sharers
        order += [source, source ^ 1]
    order = jnp.stack([*order, me_attn * rows]).astype(jnp.int32)
    gains = norm_gain.reshape(sharers, features)

    w_key, value_matrix, w_query = [
        pltpu.with_memory_space_constraint(w, pltpu.HBM) for w in (w_key, value_matrix, w_query)
    ]
    q_acc, kv_acc, squares, bounds = local_part(
        order, doc_lengths, tokens, other, gains, w_key, value_matrix, w_query
    )

    onward = [(i, (i + 1) % servers) for i in range(servers)]
    own, prior, queries = [None] * blocks, [None] * blocks, [None] * blocks
    tie = kv_acc
    halves = 2
    for c in chunks:
        pieces, tie = lax.optimization_barrier((arrived[c], tie))
        groups = []
        for piece in pieces:
            part = block // halves
            groups += [
                [piece],
                [lax.ppermute(piece[i * part : (i + 1) * part], "proj", sibling) for i in range(halves)],
            ]
        if c:
            own[c], inverse, queries[c] = project(
                c * block, order, groups, gains, w_key, value_matrix, w_query, kv_acc, squares, None, q_acc
            )
            prior[c] = lax.ppermute(own[c], "attn", onward)
        else:
            own[c], inverse = project(c * block, order, groups, gains, w_key, value_matrix, None, kv_acc, squares)
            prior[c] = lax.ppermute(own[c], "attn", onward)
            (queries[c],) = project(c * block, order, groups, gains, None, None, w_query, None, None, inverse, q_acc)
        tie = (queries[c], prior[c + 1]) if c + 1 < blocks else queries[c]

    out, lse = pl.pallas_call(
        functools.partial(main_attention_kernel, blocks),
        out_shape=(
            jax.ShapeDtypeStruct((rows, heads * HEAD_SIZE), jnp.bfloat16),
            jax.ShapeDtypeStruct((blocks - 1, heads, block), jnp.float32),
        ),
        in_specs=[VMEM] * (3 * blocks - 1),
        out_specs=(VMEM, VMEM),
        compiler_params=params(24 << 20),
        cost_estimate=cost(),
    )(*queries[1:], *own, *prior[1:], bounds)
    out, send = pl.pallas_call(
        functools.partial(last_attention_kernel, blocks, servers),
        grid=(1,),
        out_shape=(
            jax.ShapeDtypeStruct((rows, heads * HEAD_SIZE), jnp.bfloat16),
            jax.ShapeDtypeStruct((servers, heads, block), jnp.bfloat16),
        ),
        in_specs=[SMEM] + [VMEM] * (blocks + 4) + [pl.BlockSpec(memory_space=pl.ANY)],
        out_specs=(pl.BlockSpec((block, heads * HEAD_SIZE), lambda i: (0, 0)), VMEM),
        input_output_aliases={blocks + 5: 0},
        compiler_params=params(),
        cost_estimate=cost(),
    )(block_server, queries[0], own[0], *prior, bounds, lse, out)
    recv = lax.all_to_all(send, "attn", split_axis=0, concat_axis=0, tiled=True)
    served = pl.pallas_call(
        functools.partial(pick_kernel, blocks),
        out_shape=jax.ShapeDtypeStruct((blocks, heads, block), jnp.float32),
        in_specs=[VMEM],
        out_specs=VMEM,
        compiler_params=params(),
    )(recv)
    return (out, served)


def solution(mesh):
    return jax.shard_map(
        shards,
        mesh=mesh,
        in_specs=(
            P("attn", "proj"),
            P(),
            P(None, "proj"),
            P(None, "proj"),
            P(None, "proj"),
            P(),
            P("attn"),
        ),
        out_specs=(P("attn", "proj"), P("attn", "proj", None)),
        check_vma=False,
    )
```

time: 146 us -> 67.7 us (0.46)
  Pallas kernels: 0 us -> 34.8 us
  other arithmetic: 30.1 us -> 0 us
  waiting for transfers between devices: 32.5 us -> 6.71 us
  local copies, waits for them, and re-layouts: 23.8 us -> 3.02 us
  between operations: 19.5 us -> 0.83 us
  matrix products: 18.5 us -> 0 us
  blocking collectives: 0 us -> 11.7 us
  starting transfers between devices: 17.5 us -> 10.4 us
  loops' own time: 2.86 us -> 0 us
    pallas_call x0 -> x9, Pallas kernels: none -> 34.8 us  [the longest x5 19.3 us: project(): pl.pallas_call(functools.partial(chunk_kernel, count, len(groups[1]), row...]
    all_gather x1 -> x0, waiting for transfers between devices: 20.4 us -> none  [shards(): lax.all_gather(tokens, 'proj', axis=1, tiled=True).astype(jnp.float32)]
    dot_general x11 -> x0, matrix products: 18.5 us -> none  [the longest x4 8.91 us: update(): jnp.einsum('ngqk,knd->ngqd', weights.astype(jnp.bfloat16), values, prefer...]
    all_to_all x2 -> x0, starting transfers between devices: 13.9 us -> none  [the longest x1 7.28 us: shards(): lax.all_to_all(send_id, 'attn', split_axis=0, concat_axis=0, tiled=True)]
    reduce_sum x8 -> x0, other arithmetic: 13 us -> none  [the longest x4 7.64 us: update(): total = jnp.sum(weights, axis=-1)]
    all_to_all x0 -> x1, blocking collectives: none -> 11.7 us  [shards(): recv = lax.all_to_all(send, 'attn', split_axis=0, concat_axis=0, tiled=True)]
    slice x9 -> x6, local copies, waits for them, and re-layouts: 10.1 us -> 2.9 us  [the longest x2 2.83 us: shards(): piece = rest[c * block:(c + 1) * block]]
    ppermute x1 -> x17, starting transfers between devices: 3.54 us -> 10.4 us  [the longest x4 5.69 us: shards(): lax.ppermute(piece, 'proj', across(d))]
  transfers between devices with their start and end apart: 4 -> 17, of which waited for: 3 -> 7; matrix products, arithmetic and copies ran while one was open for 9% -> 4% of each run, Pallas kernels for 0% -> 46%
where the time goes in v1:
time: 67.7 us; the launch traced here: 67.5 us
  Pallas kernels  34.8 us (51%)
  blocking collectives  11.7 us (17%)
  starting transfers between devices  10.4 us (15%)
  waiting for transfers between devices  6.71 us (10%)
  local copies, waits for them, and re-layouts  3.02 us (4%)
  between operations  0.83 us (1%)
    pallas_call x5, Pallas kernels, project(): pl.pallas_call(functools.partial(chunk_kernel, count, len(groups[1]), row...  19.3 us
    all_to_all x1, blocking collectives, shards(): recv = lax.all_to_all(send, 'attn', split_axis=0, concat_axis=0, tiled=True)  11.7 us
    pallas_call x1, Pallas kernels, local_part(): pl.pallas_call(local_kernel, out_shape=(jax.ShapeDtypeStruct((rows, q_wid...  7.21 us
    ppermute x4, starting transfers between devices, shards(): lax.ppermute(piece, 'proj', across(d))  5.69 us
    ppermute x4, waiting for transfers between devices, shards(): prior[c] = lax.ppermute(own[c], 'attn', onward)  4.79 us
    pallas_call x1, Pallas kernels, shards(): pl.pallas_call(functools.partial(main_attention_kernel, blocks), out_shap...  4.74 us
    pallas_call x1, Pallas kernels, shards(): pl.pallas_call(functools.partial(last_attention_kernel, blocks, servers),...  2.91 us
    slice x2, local copies, waits for them, and re-layouts, shards(): piece = rest[c * block:(c + 1) * block]  2.83 us
  transfers between devices with their start and end apart: 17, of which 7 were waited for; matrix products, arithmetic and copies ran while one was open for 4% of the time, Pallas kernels for 46%

profile of v1, /device:TPU:0, one launch (start us, length us, event | category | flops | bytes accessed | tf_op | source)
XLA Modules:
  0.0 67.5 jit_solution(15821684939376227272)
XLA Ops:
  0.7 0.5 collective-permute-start.4
  1.2 1.0 %slice.36 = bf16[128,1024]{1,0:T(8,128)(2,1)S(1)} slice(bf16[512,1024]{1,0:T(8,128)(2,1)} %x_ref.1), slice={[384:512], [0:1024]} | slice | bytes 524288 | tf_op jit(solution)/shard_map/slice | solution.py:303
  2.1 2.6 %collective-permute-start.3 = (bf16[128,1024]{1,0:T(8,128)(2,1)S(1)}, bf16[128,1024]{1,0:T(8,128)(2,1)S(1)}, u32[]{:S(2)}, u32[]{:S(2)}) collective-permute-start(bf16[128,1024]{1,0:T(8,128)(2,1)S(1)} %slice.36), channel_id=1, source_target_pairs={{0,2},{1,3},{2,0},{3,1},{4,6},{5,7},{6,4},{7,5},{8,10},{9,11},{10,... | collective-permute-start | bytes 786440 | tf_op jit(solution)/shard_map/ppermute | solution.py:306
  4.8 1.9 %fusion = (bf16[128,1024]{1,0:T(8,128)(2,1)}, bf16[128,1024]{1,0:T(8,128)(2,1)S(1)}, bf16[128,1024]{1,0:T(8,128)(2,1)S(1)}) fusion(bf16[512,1024]{1,0:T(8,128)(2,1)} %x_ref.1), kind=kLoop, calls=%fused_computation | loop fusion | bytes 1572864 | tf_op jit(solution)/shard_map/slice | solution.py:303
  6.7 0.1 stack.23.order_ref
  6.8 7.2 %shard_map.86 = (f32[512,1024]{1,0:T(8,128)S(1)}, f32[512,512]{1,0:T(8,128)S(1)}, f32[512,1]{1,0:T(8,128)S(1)}, s32[4,128]{1,0:T(4,128)S(1)}) custom-call(s32[5]{0:T(128)S(1)} %stack.23.order_ref, s32[32]{0:T(128)S(1)} %copy-done.1, bf16[512,1024]{1,0:T(8,128)(2,1)S(1)} %copy-done, bf16[512,1024]{1,0:T(8,128)(2,1)S(1)} %collective-permute-done.4.other_ref, ...), custom_call_target="tpu_custom_call" | custom-call | flops 1024 | bytes 1024 | tf_op jit(solution)/shard_map/pallas_call | solution.py:92
  14.0 0.2 collective-permute-start.5
  14.3 0.4 collective-permute-start.6
  14.6 2.0 %collective-permute-start.1 = (bf16[128,1024]{1,0:T(8,128)(2,1)S(1)}, bf16[128,1024]{1,0:T(8,128)(2,1)S(1)}, u32[]{:S(2)}, u32[]{:S(2)}) collective-permute-start(bf16[128,1024]{1,0:T(8,128)(2,1)S(1)} %get-tuple-element.47), channel_id=1, source_target_pairs={{0,2},{1,3},{2,0},{3,1},{4,6},{5,7},{6,4},{7,5},{8,10},{9,11},{10,... | collective-permute-start | bytes 786440 | tf_op jit(solution)/shard_map/ppermute | solution.py:306
  16.6 4.3 %shard_map.87 = (bf16[128,512]{1,0:T(8,128)(2,1)S(1)}, f32[128,1]{1,0:T(8,128)}, bf16[128,1024]{1,0:T(8,128)(2,1)S(1)}) custom-call(s32[5]{0:T(128)S(1)} %stack.23.order_ref, bf16[128,1024]{1,0:T(8,128)(2,1)S(1)} %collective-permute-done.3.refs_0_, bf16[64,1024]{1,0:T(8,128)(2,1)S(1)} %collective-permute-done.5.refs_1_, ...), custom_call_target="tpu_custom_call" | custom-call | flops 1024 | bytes 1024 | tf_op jit(solution)/shard_map/pallas_call | solution.py:156
  21.1 0.5 collective-permute-start.8
  21.6 1.5 %collective-permute-start.9 = (bf16[128,512]{1,0:T(8,128)(2,1)S(1)}, bf16[128,512]{1,0:T(8,128)(2,1)S(1)}, u32[]{:S(2)}, u32[]{:S(2)}) collective-permute-start(bf16[128,512]{1,0:T(8,128)(2,1)S(1)} %get-tuple-element.33.refs_6_), channel_id=1, source_target_pairs={{0,4},{4,8},{8,12},{12,16},{16,20},{20,24},{24,28},{28,0},{1,5},{5... | collective-permute-start | bytes 393224 | tf_op jit(solution)/shard_map/ppermute | solution.py:340
  23.1 1.0 %collective-permute-start = (bf16[128,1024]{1,0:T(8,128)(2,1)S(1)}, bf16[128,1024]{1,0:T(8,128)(2,1)S(1)}, u32[]{:S(2)}, u32[]{:S(2)}) collective-permute-start(bf16[128,1024]{1,0:T(8,128)(2,1)S(1)} %get-tuple-element.48), channel_id=1, source_target_pairs={{0,2},{1,3},{2,0},{3,1},{4,6},{5,7},{6,4},{7,5},{8,10},{9,11},{10,... | collective-permute-start | bytes 786440 | tf_op jit(solution)/shard_map/ppermute | solution.py:306
  24.1 4.3 %shard_map.88 = (bf16[128,512]{1,0:T(8,128)(2,1)S(1)}, f32[128,1]{1,0:T(8,128)}, bf16[128,1024]{1,0:T(8,128)(2,1)S(1)}) custom-call(s32[5]{0:T(128)S(1)} %stack.23.order_ref, bf16[128,1024]{1,0:T(8,128)(2,1)S(1)} %collective-permute-done.2.refs_0_, bf16[64,1024]{1,0:T(8,128)(2,1)S(1)} %collective-permute-done.7.refs_1_, ...), custom_call_target="tpu_custom_call" | custom-call | flops 1024 | bytes 1024 | tf_op jit(solution)/shard_map/pallas_call | solution.py:156
  28.5 1.4 %collective-permute-done.9.refs_9_.refs_6_ = bf16[128,512]{1,0:T(8,128)(2,1)S(1)} collective-permute-done((bf16[128,512]{1,0:T(8,128)(2,1)S(1)}, bf16[128,512]{1,0:T(8,128)(2,1)S(1)}, u32[]{:S(2)}, u32[]{:S(2)}) %collective-permute-start.9) | collective-permute-done | bytes 131104 | tf_op jit(solution)/shard_map/ppermute | solution.py:340
  30.0 0.5 collective-permute-start.11
  30.5 0.1 collective-permute-start.12
  30.7 0.7 %collective-permute-done.10.refs_1_ = bf16[64,1024]{1,0:T(8,128)(2,1)S(1)} collective-permute-done((bf16[64,1024]{1,0:T(8,128)(2,1)S(1)}, bf16[64,1024]{1,0:T(8,128)(2,1)S(1)}, u32[]{:S(2)}, u32[]{:S(2)}) %collective-permute-start.10) | collective-permute-done | bytes 131104 | tf_op jit(solution)/shard_map/ppermute | solution.py:334
  31.3 0.2 collective-permute-done.11.refs_2_
  31.5 4.3 %shard_map.89 = (bf16[128,512]{1,0:T(8,128)(2,1)S(1)}, f32[128,1]{1,0:T(8,128)}, bf16[128,1024]{1,0:T(8,128)(2,1)S(1)}) custom-call(s32[5]{0:T(128)S(1)} %stack.23.order_ref, bf16[128,1024]{1,0:T(8,128)(2,1)S(1)} %collective-permute-done.1.refs_0_, bf16[64,1024]{1,0:T(8,128)(2,1)S(1)} %collective-permute-done.10.refs_1_, ...), custom_call_target="tpu_custom_call" | custom-call | flops 1024 | bytes 1024 | tf_op jit(solution)/shard_map/pallas_call | solution.py:156
  35.9 2.8 %collective-permute-done.12.refs_8_.refs_5_ = bf16[128,512]{1,0:T(8,128)(2,1)S(1)} collective-permute-done((bf16[128,512]{1,0:T(8,128)(2,1)S(1)}, bf16[128,512]{1,0:T(8,128)(2,1)S(1)}, u32[]{:S(2)}, u32[]{:S(2)}) %collective-permute-start.12) | collective-permute-done | bytes 131104 | tf_op jit(solution)/shard_map/ppermute | solution.py:340
  38.8 0.5 collective-permute-start.14
  39.3 0.8 %collective-permute-done.13.refs_1_ = bf16[64,1024]{1,0:T(8,128)(2,1)S(1)} collective-permute-done((bf16[64,1024]{1,0:T(8,128)(2,1)S(1)}, bf16[64,1024]{1,0:T(8,128)(2,1)S(1)}, u32[]{:S(2)}, u32[]{:S(2)}) %collective-permute-start.13) | collective-permute-done | bytes 131104 | tf_op jit(solution)/shard_map/ppermute | solution.py:334
  40.1 0.2 collective-permute-done.14.refs_2_
  40.3 2.8 %shard_map.90 = (bf16[128,512]{1,0:T(8,128)(2,1)S(1)}, f32[128,1]{1,0:T(8,128)S(1)}) custom-call(s32[5]{0:T(128)S(1)} %stack.23.order_ref, bf16[128,1024]{1,0:T(8,128)(2,1)S(1)} %collective-permute-done.refs_0_, bf16[64,1024]{1,0:T(8,128)(2,1)S(1)} %collective-permute-done.13.refs_1_, bf16[64,1024]{1,0:T(8,128)(2,1)S(1)} %collective-permute-done.14.refs_2_, ...), custom_call_target="tpu_custom_call" | custom-call | flops 1024 | bytes 1024 | tf_op jit(solution)/shard_map/pallas_call | solution.py:156
  43.1 0.2 collective-permute-start.15
  43.3 3.5 %shard_map.91.refs_1_ = bf16[128,1024]{1,0:T(8,128)(2,1)S(1)} custom-call(s32[5]{0:T(128)S(1)} %stack.23.order_ref, bf16[128,1024]{1,0:T(8,128)(2,1)S(1)} %collective-permute-done.refs_0_, bf16[64,1024]{1,0:T(8,128)(2,1)S(1)} %collective-permute-done.13.refs_1_, bf16[64,1024]{1,0:T(8,128)(2,1)S(1)} %collective-permute-done.14.refs_2_, ...), custom_call_target="tpu_custom_call" | custom-call | flops 1024 | bytes 1024 | tf_op jit(solution)/shard_map/pallas_call | solution.py:156
  46.9 0.6 collective-permute-done.16.refs_7_.refs_4_
  47.5 4.7 %shard_map.92 = (bf16[512,1024]{1,0:T(8,128)(2,1)}, f32[3,8,128]{2,1,0:T(8,128)S(1)}) custom-call(bf16[128,1024]{1,0:T(8,128)(2,1)S(1)} %get-tuple-element.35.refs_0_, bf16[128,1024]{1,0:T(8,128)(2,1)S(1)} %get-tuple-element.32.refs_1_, bf16[128,1024]{1,0:T(8,128)(2,1)S(1)} %get-tuple-element.30.refs_2_, ...), custom_call_target="tpu_custom_call" | custom-call | flops 1024 | bytes 1024 | tf_op jit(solution)/shard_map/pallas_call | solution.py:347
  52.2 2.9 %shard_map.93 = (bf16[512,1024]{1,0:T(8,128)(2,1)}, bf16[8,8,128]{2,1,0:T(8,128)(2,1)S(1)}) custom-call(s32[4]{0:T(128)S(1)} %copy-done.2, bf16[128,1024]{1,0:T(8,128)(2,1)S(1)} %shard_map.91.refs_1_, bf16[128,512]{1,0:T(8,128)(2,1)S(1)} %get-tuple-element.39.refs_3_.refs_2_, ...), custom_call_target="tpu_custom_call", output_to_operand_aliasing={{0}: (9, {})} | custom-call | flops 1024 | bytes 1024 | tf_op jit(solution)/shard_map/pallas_call | solution.py:358
  55.1 11.7 %all_to_all.5.recv_ref = bf16[8,8,128]{2,1,0:T(8,128)(2,1)S(1)} all-to-all(bf16[8,8,128]{2,1,0:T(8,128)(2,1)S(1)} %get-tuple-element.45), channel_id=1, replica_groups=mesh['attn'=8,'proj'=4] {'attn'}, dimensions={0} | all-to-all | bytes 32768 | tf_op jit(solution)/shard_map/all_to_all | solution.py:371
  66.9 0.6 shard_map.94
  (28 shorter events, 0.4 us)
Async XLA Ops:
  0.6 6.2 %copy-start = (bf16[512,1024]{1,0:T(8,128)(2,1)S(1)}, bf16[512,1024]{1,0:T(8,128)(2,1)}, u32[]{:S(2)}) copy-start(bf16[512,1024]{1,0:T(8,128)(2,1)} %x_ref.1) | copy-start | bytes 3145732
  0.6 6.0 %copy-start.3 = (f32[4096]{0:T(1024)S(1)}, f32[4096]{0:T(1024)}, u32[]{:S(2)}) copy-start(f32[4096]{0:T(1024)} %param.8) | copy-start | bytes 49156
  0.7 6.1 %copy-start.1 = (s32[32]{0:T(128)S(1)}, s32[32]{0:T(128)}, u32[]{:S(2)}) copy-start(s32[32]{0:T(128)} %docs_ref.1) | copy-start | bytes 388
  0.7 6.1 %collective-permute-start.4 = (bf16[512,1024]{1,0:T(8,128)(2,1)}, bf16[512,1024]{1,0:T(8,128)(2,1)S(1)}, u32[]{:S(2)}, u32[]{:S(2)}) collective-permute-start(bf16[512,1024]{1,0:T(8,128)(2,1)} %x_ref.1), channel_id=1, source_target_pairs={{0,1},{1,0},{2,3},{3,2},{4,5},{5,4},{6,7},{7,6},{8,9},{9,8},{10,11... | collective-permute-start | bytes 3145736 | tf_op jit(solution)/shard_map/ppermute | solution.py:307
  2.1 11.9 %collective-permute-start.3 = (bf16[128,1024]{1,0:T(8,128)(2,1)S(1)}, bf16[128,1024]{1,0:T(8,128)(2,1)S(1)}, u32[]{:S(2)}, u32[]{:S(2)}) collective-permute-start(bf16[128,1024]{1,0:T(8,128)(2,1)S(1)} %slice.36), channel_id=1, source_target_pairs={{0,2},{1,3},{2,0},{3,1},{4,6},{5,7},{6,4},{7,5},{8,10},{9,11},{10,... | collective-permute-start | bytes 786440 | tf_op jit(solution)/shard_map/ppermute | solution.py:306
  6.7 14.3 %collective-permute-start.2 = (bf16[128,1024]{1,0:T(8,128)(2,1)}, bf16[128,1024]{1,0:T(8,128)(2,1)S(1)}, u32[]{:S(2)}, u32[]{:S(2)}) collective-permute-start(bf16[128,1024]{1,0:T(8,128)(2,1)} %get-tuple-element.46), channel_id=1, source_target_pairs={{0,2},{1,3},{2,0},{3,1},{4,6},{5,7},{6,4},{7,5},{8,10},{9,11},{10,... | collective-permute-start | bytes 786440 | tf_op jit(solution)/shard_map/ppermute | solution.py:306
  14.0 2.6 %collective-permute-start.5 = (bf16[64,1024]{1,0:T(8,128)(2,1)S(1)}, bf16[64,1024]{1,0:T(8,128)(2,1)S(1)}, u32[]{:S(2)}, u32[]{:S(2)}) collective-permute-start(bf16[64,1024]{1,0:T(8,128)(2,1)S(1)} %get-tuple-element.56), channel_id=1, source_target_pairs={{0,1},{1,0},{2,3},{3,2},{4,5},{5,4},{6,7},{7,6},{8,9},{9,8},{10,11... | collective-permute-start | bytes 393224 | tf_op jit(solution)/shard_map/ppermute | solution.py:334
  14.3 2.4 %collective-permute-start.6 = (bf16[64,1024]{1,0:T(8,128)(2,1)S(1)}, bf16[64,1024]{1,0:T(8,128)(2,1)S(1)}, u32[]{:S(2)}, u32[]{:S(2)}) collective-permute-start(bf16[64,1024]{1,0:T(8,128)(2,1)S(1)} %get-tuple-element.55), channel_id=1, source_target_pairs={{0,1},{1,0},{2,3},{3,2},{4,5},{5,4},{6,7},{7,6},{8,9},{9,8},{10,11... | collective-permute-start | bytes 393224 | tf_op jit(solution)/shard_map/ppermute | solution.py:334
  14.6 13.9 %collective-permute-start.1 = (bf16[128,1024]{1,0:T(8,128)(2,1)S(1)}, bf16[128,1024]{1,0:T(8,128)(2,1)S(1)}, u32[]{:S(2)}, u32[]{:S(2)}) collective-permute-start(bf16[128,1024]{1,0:T(8,128)(2,1)S(1)} %get-tuple-element.47), channel_id=1, source_target_pairs={{0,2},{1,3},{2,0},{3,1},{4,6},{5,7},{6,4},{7,5},{8,10},{9,11},{10,... | collective-permute-start | bytes 786440 | tf_op jit(solution)/shard_map/ppermute | solution.py:306
  21.0 3.1 %collective-permute-start.7 = (bf16[64,1024]{1,0:T(8,128)(2,1)S(1)}, bf16[64,1024]{1,0:T(8,128)(2,1)S(1)}, u32[]{:S(2)}, u32[]{:S(2)}) collective-permute-start(bf16[64,1024]{1,0:T(8,128)(2,1)S(1)} %get-tuple-element.54), channel_id=1, source_target_pairs={{0,1},{1,0},{2,3},{3,2},{4,5},{5,4},{6,7},{7,6},{8,9},{9,8},{10,11... | collective-permute-start | bytes 393224 | tf_op jit(solution)/shard_map/ppermute | solution.py:334
  21.1 3.0 %collective-permute-start.8 = (bf16[64,1024]{1,0:T(8,128)(2,1)S(1)}, bf16[64,1024]{1,0:T(8,128)(2,1)S(1)}, u32[]{:S(2)}, u32[]{:S(2)}) collective-permute-start(bf16[64,1024]{1,0:T(8,128)(2,1)S(1)} %get-tuple-element.53), channel_id=1, source_target_pairs={{0,1},{1,0},{2,3},{3,2},{4,5},{5,4},{6,7},{7,6},{8,9},{9,8},{10,11... | collective-permute-start | bytes 393224 | tf_op jit(solution)/shard_map/ppermute | solution.py:334
  21.6 8.3 %collective-permute-start.9 = (bf16[128,512]{1,0:T(8,128)(2,1)S(1)}, bf16[128,512]{1,0:T(8,128)(2,1)S(1)}, u32[]{:S(2)}, u32[]{:S(2)}) collective-permute-start(bf16[128,512]{1,0:T(8,128)(2,1)S(1)} %get-tuple-element.33.refs_6_), channel_id=1, source_target_pairs={{0,4},{4,8},{8,12},{12,16},{16,20},{20,24},{24,28},{28,0},{1,5},{5... | collective-permute-start | bytes 393224 | tf_op jit(solution)/shard_map/ppermute | solution.py:340
  23.1 12.8 %collective-permute-start = (bf16[128,1024]{1,0:T(8,128)(2,1)S(1)}, bf16[128,1024]{1,0:T(8,128)(2,1)S(1)}, u32[]{:S(2)}, u32[]{:S(2)}) collective-permute-start(bf16[128,1024]{1,0:T(8,128)(2,1)S(1)} %get-tuple-element.48), channel_id=1, source_target_pairs={{0,2},{1,3},{2,0},{3,1},{4,6},{5,7},{6,4},{7,5},{8,10},{9,11},{10,... | collective-permute-start | bytes 786440 | tf_op jit(solution)/shard_map/ppermute | solution.py:306
  29.9 1.4 %collective-permute-start.10 = (bf16[64,1024]{1,0:T(8,128)(2,1)S(1)}, bf16[64,1024]{1,0:T(8,128)(2,1)S(1)}, u32[]{:S(2)}, u32[]{:S(2)}) collective-permute-start(bf16[64,1024]{1,0:T(8,128)(2,1)S(1)} %get-tuple-element.52), channel_id=1, source_target_pairs={{0,1},{1,0},{2,3},{3,2},{4,5},{5,4},{6,7},{7,6},{8,9},{9,8},{10,11... | collective-permute-start | bytes 393224 | tf_op jit(solution)/shard_map/ppermute | solution.py:334
  30.0 1.5 %collective-permute-start.11 = (bf16[64,1024]{1,0:T(8,128)(2,1)S(1)}, bf16[64,1024]{1,0:T(8,128)(2,1)S(1)}, u32[]{:S(2)}, u32[]{:S(2)}) collective-permute-start(bf16[64,1024]{1,0:T(8,128)(2,1)S(1)} %get-tuple-element.51), channel_id=1, source_target_pairs={{0,1},{1,0},{2,3},{3,2},{4,5},{5,4},{6,7},{7,6},{8,9},{9,8},{10,11... | collective-permute-start | bytes 393224 | tf_op jit(solution)/shard_map/ppermute | solution.py:334
  30.5 8.2 %collective-permute-start.12 = (bf16[128,512]{1,0:T(8,128)(2,1)S(1)}, bf16[128,512]{1,0:T(8,128)(2,1)S(1)}, u32[]{:S(2)}, u32[]{:S(2)}) collective-permute-start(bf16[128,512]{1,0:T(8,128)(2,1)S(1)} %get-tuple-element.36.refs_5_), channel_id=1, source_target_pairs={{0,4},{4,8},{8,12},{12,16},{16,20},{20,24},{24,28},{28,0},{1,5},{5... | collective-permute-start | bytes 393224 | tf_op jit(solution)/shard_map/ppermute | solution.py:340
  38.7 1.4 %collective-permute-start.13 = (bf16[64,1024]{1,0:T(8,128)(2,1)S(1)}, bf16[64,1024]{1,0:T(8,128)(2,1)S(1)}, u32[]{:S(2)}, u32[]{:S(2)}) collective-permute-start(bf16[64,1024]{1,0:T(8,128)(2,1)S(1)} %get-tuple-element.50), channel_id=1, source_target_pairs={{0,1},{1,0},{2,3},{3,2},{4,5},{5,4},{6,7},{7,6},{8,9},{9,8},{10,11... | collective-permute-start | bytes 393224 | tf_op jit(solution)/shard_map/ppermute | solution.py:334
  38.8 1.5 %collective-permute-start.14 = (bf16[64,1024]{1,0:T(8,128)(2,1)S(1)}, bf16[64,1024]{1,0:T(8,128)(2,1)S(1)}, u32[]{:S(2)}, u32[]{:S(2)}) collective-permute-start(bf16[64,1024]{1,0:T(8,128)(2,1)S(1)} %get-tuple-element.49), channel_id=1, source_target_pairs={{0,1},{1,0},{2,3},{3,2},{4,5},{5,4},{6,7},{7,6},{8,9},{9,8},{10,11... | collective-permute-start | bytes 393224 | tf_op jit(solution)/shard_map/ppermute | solution.py:334
  39.3 8.2 %collective-permute-start.16 = (bf16[128,512]{1,0:T(8,128)(2,1)S(1)}, bf16[128,512]{1,0:T(8,128)(2,1)S(1)}, u32[]{:S(2)}, u32[]{:S(2)}) collective-permute-start(bf16[128,512]{1,0:T(8,128)(2,1)S(1)} %get-tuple-element.40.refs_4_), channel_id=1, source_target_pairs={{0,4},{4,8},{8,12},{12,16},{16,20},{20,24},{24,28},{28,0},{1,5},{5... | collective-permute-start | bytes 393224 | tf_op jit(solution)/shard_map/ppermute | solution.py:340
  43.1 9.1 %collective-permute-start.15 = (bf16[128,512]{1,0:T(8,128)(2,1)S(1)}, bf16[128,512]{1,0:T(8,128)(2,1)S(1)}, u32[]{:S(2)}, u32[]{:S(2)}) collective-permute-start(bf16[128,512]{1,0:T(8,128)(2,1)S(1)} %get-tuple-element.39.refs_3_.refs_2_), channel_id=1, source_target_pairs={{0,4},{4,8},{8,12},{12,16},{16,20},{20,24},{24,28},{28,0},{1,5},{5... | collective-permute-start | bytes 393224 | tf_op jit(solution)/shard_map/ppermute | solution.py:343
  43.3 8.9 %copy-start.2 = (s32[4]{0:T(128)S(1)}, s32[4]{0:T(128)}, u32[]{:S(2)}) copy-start(s32[4]{0:T(128)} %refs_0_.1) | copy-start | bytes 52

commit v2 on v1

v2 whole, which is shorter than its diff:
```python
import functools
import math

import jax
import jax.numpy as jnp
from jax import lax
from jax.experimental import pallas as pl
from jax.experimental.pallas import tpu as pltpu
from jax.sharding import PartitionSpec as P

HEAD_SIZE = 128
QUERY_BLOCK_ROWS = 128
CORES = 2

masked_value = -1e30
norm_eps = 1e-05
score_scale = 1.0 / HEAD_SIZE**0.5
log2_scale = score_scale * math.log2(math.e)

VMEM = pl.BlockSpec(memory_space=pltpu.VMEM)
SMEM = pl.BlockSpec(memory_space=pltpu.SMEM)
HBM = pl.BlockSpec(memory_space=pltpu.HBM)


def params(limit=16 << 20):
    return pltpu.CompilerParams(vmem_limit_bytes=limit)


def part_terms(x, gain):
    values = x.astype(jnp.float32)
    scaled = (values * gain).astype(jnp.bfloat16)
    return scaled, jnp.sum(values * values, axis=1, keepdims=True)


def cost():
    return pl.CostEstimate(flops=1 << 10, bytes_accessed=1 << 10, transcendentals=0)


def local_kernel(order_ref, docs_ref, x_ref, other_ref, gain_ref, wk, wv, wq, *refs):
    q_ref, kv_ref, sq_ref, bound_ref, kv_rest, q_rest, kv_own, q_own, sems = refs
    features, width = x_ref.shape[1], wk.shape[1]

    def fetch(slot, kv_to, q_to, place):
        rows = pl.ds(pl.multiple_of(order_ref[slot] * features, features), features)
        here = pl.ds(place * features, features)
        copies = (
            pltpu.make_async_copy(wk.at[rows, :], kv_to.at[here, pl.ds(0, width)], sems.at[slot, 0]),
            pltpu.make_async_copy(wv.at[rows, :], kv_to.at[here, pl.ds(width, width)], sems.at[slot, 1]),
            pltpu.make_async_copy(wq.at[rows, :], q_to.at[here, :], sems.at[slot, 2]),
        )
        for copy in copies:
            copy.start()
        return copies

    mine = [fetch(slot, kv_own, q_own, slot) for slot in range(CORES)]
    rest = [fetch(CORES + i, kv_rest, q_rest, i) for i in range(q_rest.shape[0] // features)]

    shape = bound_ref.shape
    base = order_ref[order_ref.shape[0] - 1]
    position = lax.broadcasted_iota(jnp.int32, shape, 0) * shape[1] + lax.broadcasted_iota(jnp.int32, shape, 1)
    start = -base
    bounds = jnp.full(shape, start, jnp.int32)
    for d in range(docs_ref.shape[0]):
        bounds = jnp.where(position >= start, start, bounds)
        start = start + docs_ref[d]
    bound_ref[...] = bounds

    parts = [
        part_terms(ref[...], gain_ref[pl.ds(order_ref[slot], 1), :]) for slot, ref in enumerate((x_ref, other_ref))
    ]
    sq_ref[...] = parts[0][1] + parts[1][1]
    scaled = jnp.concatenate([part[0] for part in parts], axis=1)
    for k, v, _ in mine:
        k.wait()
        v.wait()
    kv_ref[...] = jnp.dot(scaled, kv_own[...], preferred_element_type=jnp.float32)
    for _, _, q in mine:
        q.wait()
    q_ref[...] = jnp.dot(scaled, q_own[...], preferred_element_type=jnp.float32)
    for copies in rest:
        for copy in copies:
            copy.wait()


def local_part(order, docs, x, other, gains, wk, wv, wq):
    rows, features = x.shape
    q_width, kv_width = wq.shape[1], 2 * wk.shape[1]
    rest = wq.shape[0] - CORES * features
    return pl.pallas_call(
        local_kernel,
        out_shape=(
            pltpu.VMEM((rows, q_width), jnp.float32),
            pltpu.VMEM((rows, kv_width), jnp.float32),
            pltpu.VMEM((rows, 1), jnp.float32),
            pltpu.VMEM((rows // QUERY_BLOCK_ROWS, QUERY_BLOCK_ROWS), jnp.int32),
            pltpu.VMEM((rest, kv_width), jnp.bfloat16),
            pltpu.VMEM((rest, q_width), jnp.bfloat16),
        ),
        in_specs=[SMEM, SMEM, VMEM, VMEM, VMEM, HBM, HBM, HBM],
        out_specs=(VMEM,) * 6,
        scratch_shapes=[
            pltpu.VMEM((CORES * features, kv_width), jnp.bfloat16),
            pltpu.VMEM((CORES * features, q_width), jnp.bfloat16),
            pltpu.SemaphoreType.DMA((wq.shape[0] // features, 3)),
        ],
        compiler_params=params(32 << 20),
        cost_estimate=cost(),
    )(order, docs, x, other, gains, wk, wv, wq)


def chunk_kernel(count, halves, row, want_kv, want_q, order_ref, *refs):
    it = iter(refs)
    groups = [[next(it) for _ in range(halves if i % CORES else 1)] for i in range(count)]
    gain_ref = next(it)
    wkv_ref, kva_ref, sq_ref = (next(it), next(it), next(it)) if want_kv else (None,) * 3
    inv_ref = None if want_kv else next(it)
    wq_ref, qa_ref = (next(it), next(it)) if want_q else (None, None)
    kv_ref, inv_out = (next(it), next(it)) if want_kv else (None, None)
    q_ref = next(it) if want_q else None
    features = groups[0][0].shape[1]
    scaled, squares = [], []
    for i, group in enumerate(groups):
        x = jnp.concatenate([ref[...] for ref in group], axis=0)
        part, square = part_terms(x, gain_ref[pl.ds(order_ref[CORES + i], 1), :])
        scaled.append(part)
        squares.append(square)
    scaled = jnp.concatenate(scaled, axis=1)
    here = slice(row, row + scaled.shape[0])
    if want_kv:
        inverse = lax.rsqrt((sq_ref[here, :] + sum(squares)) / (features * (count + CORES)) + norm_eps)
        inv_out[...] = inverse
        total = kva_ref[here, :] + jnp.dot(scaled, wkv_ref[...], preferred_element_type=jnp.float32)
        kv_ref[...] = (total * inverse).astype(jnp.bfloat16)
    else:
        inverse = inv_ref[...]
    if want_q:
        total = qa_ref[here, :] + jnp.dot(scaled, wq_ref[...], preferred_element_type=jnp.float32)
        q_ref[...] = (total * inverse).astype(jnp.bfloat16)


def project(row, order, groups, gains, kv=(), inverse=None, q=()):
    count, halves, rows = len(groups), len(groups[1]), groups[0][0].shape[0]
    pieces = [piece for group in groups for piece in group]
    operands = [*kv] + ([] if kv else [inverse]) + [*q]
    shapes = []
    if kv:
        shapes += [
            jax.ShapeDtypeStruct((rows, kv[0].shape[1]), jnp.bfloat16),
            jax.ShapeDtypeStruct((rows, 1), jnp.float32),
        ]
    if q:
        shapes += [jax.ShapeDtypeStruct((rows, q[0].shape[1]), jnp.bfloat16)]
    return pl.pallas_call(
        functools.partial(chunk_kernel, count, halves, row, bool(kv), bool(q)),
        out_shape=tuple(shapes),
        in_specs=[SMEM] + [VMEM] * (len(pieces) + 1 + len(operands)),
        out_specs=(VMEM,) * len(shapes),
        compiler_params=params(),
        cost_estimate=cost(),
    )(order, *pieces, gains, *operands)


def block_attention(q, bounds, keys_values, key_starts, row_start, store):
    rows = q.shape[0]
    width = keys_values[0][0].shape[1] // 2
    kv_heads = width // HEAD_SIZE
    group = q.shape[1] // width
    bounds = jnp.transpose(jnp.broadcast_to(bounds, (QUERY_BLOCK_ROWS, rows)))
    query_pos = row_start + lax.broadcasted_iota(jnp.int32, (rows, QUERY_BLOCK_ROWS), 0)
    allowed = []
    for start in key_starts:
        key_pos = start + lax.broadcasted_iota(jnp.int32, (rows, QUERY_BLOCK_ROWS), 1)
        ok = key_pos >= bounds
        if start == row_start:
            ok = ok & (key_pos <= query_pos)
        allowed.append(jnp.concatenate([ok] * group, axis=0))
    lse_rows = []
    for n in range(kv_heads):
        stacked = jnp.concatenate(
            [q[:, (n * group + g) * HEAD_SIZE : (n * group + g + 1) * HEAD_SIZE] for g in range(group)],
            axis=0,
        )
        scores = []
        highest = None
        for ok, (ref, at) in zip(allowed, keys_values):
            s = lax.dot_general(
                stacked,
                ref[at : at + QUERY_BLOCK_ROWS, n * HEAD_SIZE : (n + 1) * HEAD_SIZE],
                (((1,), (1,)), ((), ())),
                preferred_element_type=jnp.float32,
            )
            s = jnp.where(ok, s, masked_value)
            scores.append(s)
            highest = s if highest is None else jnp.maximum(highest, s)
        highest = jnp.max(highest, axis=1, keepdims=True)
        total = None
        summed = None
        for s, (ref, at) in zip(scores, keys_values):
            weights = jnp.exp2((s - highest) * log2_scale)
            total = weights if total is None else total + weights
            product = jnp.dot(
                weights.astype(jnp.bfloat16),
                ref[at : at + QUERY_BLOCK_ROWS, width + n * HEAD_SIZE : width + (n + 1) * HEAD_SIZE],
                preferred_element_type=jnp.float32,
            )
            summed = product if summed is None else summed + product
        total = jnp.sum(total, axis=1, keepdims=True)
        result = (summed / total).astype(jnp.bfloat16)
        lse = highest * score_scale + jnp.log(total)
        for g in range(group):
            store(n * group + g, result[g * rows : (g + 1) * rows])
            lse_rows.append(lse[g * rows : (g + 1) * rows])
    lane = lax.broadcasted_iota(jnp.int32, (rows, HEAD_SIZE), 1)
    table = jnp.zeros((rows, HEAD_SIZE), jnp.float32)
    for h, column in enumerate(lse_rows):
        table = jnp.where(lane == h, column, table)
    return jnp.transpose(table)[: len(lse_rows), :]


def block_refs(refs, chunks):
    found = {}
    for ref, (low, high) in zip(refs, chunks):
        for i in range(low, high):
            found[i] = (ref, (i - low) * QUERY_BLOCK_ROWS)
    return found


def attend_blocks(wanted, blocks, queries, owns, priors, bounds_ref, out_ref, base):
    rows = QUERY_BLOCK_ROWS
    lses = {}
    for block in wanted:
        def store(head, value, at=(block - base) * rows):
            out_ref[at : at + rows, head * HEAD_SIZE : (head + 1) * HEAD_SIZE] = value

        ref, at = queries[block]
        lses[block] = block_attention(
            ref[at : at + rows, :],
            bounds_ref[block : block + 1, :],
            [priors[i] for i in range(block, blocks)] + [owns[i] for i in range(block + 1)],
            [(i - blocks) * rows for i in range(block, blocks)] + [i * rows for i in range(block + 1)],
            block * rows,
            store,
        )
    return lses


def main_attention_kernel(chunks, *refs):
    count, (low, blocks) = len(chunks), chunks[0]
    queries = block_refs(refs[:1], chunks[:1])
    owns = block_refs(refs[1 : 1 + count], chunks)
    priors = block_refs(refs[1 + count : 2 + count], chunks[:1])
    bounds_ref, out_ref, lse_ref = refs[2 + count :]
    lses = attend_blocks(range(low, blocks), blocks, queries, owns, priors, bounds_ref, out_ref, low)
    for block, lse in lses.items():
        lse_ref[block - low] = lse


def last_attention_kernel(chunks, servers, *refs):
    count, (low, blocks) = len(chunks), chunks[0]
    server_ref, *refs = refs
    queries = block_refs(refs[: count - 1], chunks[1:])
    owns = block_refs(refs[count - 1 : 2 * count - 2], chunks[1:])
    priors = block_refs(refs[2 * count - 2 : 3 * count - 2], chunks)
    bounds_ref, lse_ref, _, out_ref, send_ref = refs[3 * count - 2 :]
    lses = attend_blocks(reversed(range(low)), blocks, queries, owns, priors, bounds_ref, out_ref, 0)
    for block in range(low, blocks):
        lses[block] = lse_ref[block - low]
    for s in range(servers):
        value = jnp.full(lses[0].shape, jnp.inf, jnp.float32)
        for block, lse in lses.items():
            value = jnp.where(server_ref[block] == s, lse, value)
        send_ref[s] = value.astype(jnp.bfloat16)


def pick_kernel(blocks, recv_ref, out_ref):
    shape = recv_ref.shape[1:]
    rank = jnp.zeros(shape, jnp.int32)
    picked = [jnp.zeros(shape, jnp.float32) for _ in range(blocks)]
    for i in range(recv_ref.shape[0]):
        value = recv_ref[i].astype(jnp.float32)
        valid = value < jnp.inf
        for k in range(blocks):
            picked[k] = jnp.where(valid & (rank == k), value, picked[k])
        rank = rank + valid.astype(jnp.int32)
    for k in range(blocks):
        out_ref[k] = picked[k]


def shards(tokens, norm_gain, w_query, w_key, value_matrix, doc_lengths, block_server):
    rows, features = tokens.shape
    width = w_key.shape[1]
    heads = w_query.shape[1] // HEAD_SIZE
    block = QUERY_BLOCK_ROWS
    blocks = rows // block
    servers = lax.axis_size("attn")
    sharers = lax.axis_size("proj")
    chips = sharers // CORES
    me_attn = lax.axis_index("attn")
    me_proj = lax.axis_index("proj")
    sibling = [(i, i ^ 1) for i in range(sharers)]

    def across(distance):
        return [(i, (i + distance * CORES) % sharers) for i in range(sharers)]

    middle = blocks // 2
    chunks = [(middle, blocks)] + [(i, i + 1) for i in reversed(range(middle))]
    arrived = []
    rest = tokens
    for low, high in chunks:
        piece = rest[low * block : high * block]
        if not arrived:
            piece, rest = lax.optimization_barrier((piece, rest))
        arrived.append([lax.ppermute(piece, "proj", across(d)) for d in range(1, chips)])
    other = lax.ppermute(tokens, "proj", sibling)

    order = [me_proj, me_proj ^ 1]
    for d in range(1, chips):
        source = (me_proj + sharers - d * CORES) % sharers
        order += [source, source ^ 1]
    order = jnp.stack([*order, me_attn * rows]).astype(jnp.int32)
    gains = norm_gain.reshape(sharers, features)

    w_key, value_matrix, w_query = [
        pltpu.with_memory_space_constraint(w, pltpu.HBM) for w in (w_key, value_matrix, w_query)
    ]
    q_acc, kv_acc, squares, bounds, wkv_rest, wq_rest = local_part(
        order, doc_lengths, tokens, other, gains, w_key, value_matrix, w_query
    )

    onward = [(i, (i + 1) % servers) for i in range(servers)]
    own, prior, queries = [], [], []
    tie = kv_acc
    for (low, high), pieces in zip(chunks, arrived):
        pieces, tie = lax.optimization_barrier((pieces, tie))
        part = 64 if high == blocks else 32
        groups = []
        for piece in pieces:
            groups += [
                [piece],
                [lax.ppermute(piece[i : i + part], "proj", sibling) for i in range(0, piece.shape[0], part)],
            ]
        if low:
            kv, _, q = project(
                low * block, order, groups, gains, (wkv_rest, kv_acc, squares), None, (wq_rest, q_acc)
            )
            tie = q
            prior.append(lax.ppermute(kv, "attn", onward))
        else:
            kv, inverse = project(0, order, groups, gains, (wkv_rest, kv_acc, squares))
            prior.append(lax.ppermute(kv, "attn", onward))
            (q,) = project(0, order, groups, gains, (), inverse, (wq_rest, q_acc))
        own.append(kv)
        queries.append(q)

    count = len(chunks)
    queries = list(lax.optimization_barrier(tuple(queries)))
    half = (blocks - middle) * block
    out, lse = pl.pallas_call(
        functools.partial(main_attention_kernel, chunks),
        grid=(1,),
        out_shape=(
            jax.ShapeDtypeStruct((rows, heads * HEAD_SIZE), jnp.bfloat16),
            jax.ShapeDtypeStruct((blocks - middle, heads, block), jnp.float32),
        ),
        in_specs=[VMEM] * (count + 3),
        out_specs=(pl.BlockSpec((half, heads * HEAD_SIZE), lambda i: (rows // half - 1, 0)), VMEM),
        compiler_params=params(24 << 20),
        cost_estimate=cost(),
    )(queries[0], *own, prior[0], bounds)
    out, send = pl.pallas_call(
        functools.partial(last_attention_kernel, chunks, servers),
        grid=(1,),
        out_shape=(
            jax.ShapeDtypeStruct((rows, heads * HEAD_SIZE), jnp.bfloat16),
            jax.ShapeDtypeStruct((servers, heads, block), jnp.bfloat16),
        ),
        in_specs=[SMEM] + [VMEM] * (3 * count) + [pl.BlockSpec(memory_space=pl.ANY)],
        out_specs=(pl.BlockSpec((rows - half, heads * HEAD_SIZE), lambda i: (0, 0)), VMEM),
        input_output_aliases={3 * count + 1: 0},
        compiler_params=params(24 << 20),
        cost_estimate=cost(),
    )(block_server, *queries[1:], *own[1:], *prior, bounds, lse, out)
    recv = lax.all_to_all(send, "attn", split_axis=0, concat_axis=0, tiled=True)
    served = pl.pallas_call(
        functools.partial(pick_kernel, blocks),
        out_shape=jax.ShapeDtypeStruct((blocks, heads, block), jnp.float32),
        in_specs=[VMEM],
        out_specs=VMEM,
        compiler_params=params(),
    )(recv)
    return (out, served)


def solution(mesh):
    return jax.shard_map(
        shards,
        mesh=mesh,
        in_specs=(
            P("attn", "proj"),
            P(),
            P(None, "proj"),
            P(None, "proj"),
            P(None, "proj"),
            P(),
            P("attn"),
        ),
        out_specs=(P("attn", "proj"), P("attn", "proj", None)),
        check_vma=False,
    )
```

time: 67.7 us -> 56.1 us (0.83)
  Pallas kernels: 34.8 us -> 22.1 us
  starting transfers between devices: 10.4 us -> 13.4 us
  blocking collectives: 11.7 us -> 9.38 us
    pallas_call x8 -> x7, Pallas kernels: 34.2 us -> 21.5 us  [the longest x4 7.06 us: project(): pl.pallas_call(functools.partial(chunk_kernel, count, halves, row, bool(k...]
    ppermute x12 -> x15, starting transfers between devices: 4.19 us -> 8.24 us  [the longest x3 5.01 us: shards(): prior.append(lax.ppermute(kv, 'attn', onward))]
    ppermute x4 -> x3, waiting for transfers between devices: 0.01 us -> 3.81 us  [shards(): lax.ppermute(piece, 'proj', across(d))]
    ppermute x12 -> x15, waiting for transfers between devices: 6.69 us -> 3.33 us  [the longest x3 2.51 us: shards(): prior.append(lax.ppermute(kv, 'attn', onward))]
    all_to_all x1, blocking collectives: 11.7 us -> 9.38 us  [shards(): recv = lax.all_to_all(send, 'attn', split_axis=0, concat_axis=0, tiled=True)]
    ppermute x4 -> x3, starting transfers between devices: 5.69 us -> 4.61 us  [shards(): lax.ppermute(piece, 'proj', across(d))]
    slice x6 -> x5, local copies, waits for them, and re-layouts: 2.9 us -> 2.98 us  [the longest x2 2.91 us: shards(): piece = rest[low * block:high * block]]
  transfers between devices with their start and end apart: 17 -> 19, of which waited for: 7 -> 6; matrix products, arithmetic and copies ran while one was open for 4% -> 6% of each run, Pallas kernels for 46% -> 31%
where the time goes in v2:
time: 56.1 us; the launch traced here: 55.9 us
  Pallas kernels  22.1 us (39%)
  starting transfers between devices  13.4 us (24%)
  blocking collectives  9.38 us (17%)
  waiting for transfers between devices  7.14 us (13%)
  local copies, waits for them, and re-layouts  3.11 us (6%)
  between operations  0.78 us (1%)
    all_to_all x1, blocking collectives, shards(): recv = lax.all_to_all(send, 'attn', split_axis=0, concat_axis=0, tiled=True)  9.38 us
    pallas_call x4, Pallas kernels, project(): pl.pallas_call(functools.partial(chunk_kernel, count, halves, row, bool(k...  7.06 us
    pallas_call x1, Pallas kernels, local_part(): pl.pallas_call(local_kernel, out_shape=(pltpu.VMEM((rows, q_width), jnp.f...  6.98 us
    ppermute x3, starting transfers between devices, shards(): prior.append(lax.ppermute(kv, 'attn', onward))  5.01 us
    ppermute x3, starting transfers between devices, shards(): lax.ppermute(piece, 'proj', across(d))  4.61 us
    pallas_call x1, Pallas kernels, shards(): pl.pallas_call(functools.partial(last_attention_kernel, chunks, servers),...  3.96 us
    ppermute x3, waiting for transfers between devices, shards(): lax.ppermute(piece, 'proj', across(d))  3.81 us
    pallas_call x1, Pallas kernels, shards(): pl.pallas_call(functools.partial(main_attention_kernel, chunks), grid=(1,...  3.46 us
  transfers between devices with their start and end apart: 19, of which 6 were waited for; matrix products, arithmetic and copies ran while one was open for 6% of the time, Pallas kernels for 31%

profile of v2, /device:TPU:0, one launch (start us, length us, event | category | flops | bytes accessed | tf_op | source)
XLA Modules:
  0.0 55.9 jit_solution(15323478701137324725)
XLA Ops:
  0.7 0.5 collective-permute-start.1
  1.2 1.1 %slice.45 = bf16[256,1024]{1,0:T(8,128)(2,1)S(1)} slice(bf16[512,1024]{1,0:T(8,128)(2,1)} %x_ref.1), slice={[256:512], [0:1024]} | slice | bytes 1048576 | tf_op jit(solution)/shard_map/slice | solution.py:310
  2.3 2.6 %collective-permute-start = (bf16[256,1024]{1,0:T(8,128)(2,1)S(1)}, bf16[256,1024]{1,0:T(8,128)(2,1)S(1)}, u32[]{:S(2)}, u32[]{:S(2)}) collective-permute-start(bf16[256,1024]{1,0:T(8,128)(2,1)S(1)} %slice.45), channel_id=1, source_target_pairs={{0,2},{1,3},{2,0},{3,1},{4,6},{5,7},{6,4},{7,5},{8,10},{9,11},{10,... | collective-permute-start | bytes 1572872 | tf_op jit(solution)/shard_map/ppermute | solution.py:313
  4.9 1.8 %fusion = (bf16[128,1024]{1,0:T(8,128)(2,1)}, bf16[128,1024]{1,0:T(8,128)(2,1)}) fusion(bf16[512,1024]{1,0:T(8,128)(2,1)} %x_ref.1), kind=kLoop, calls=%fused_computation | loop fusion | bytes 1048576 | tf_op jit(solution)/shard_map/slice | solution.py:310
  6.8 0.1 stack.23.order_ref
  6.9 7.0 %shard_map.86 = (f32[512,1024]{1,0:T(8,128)S(1)}, f32[512,512]{1,0:T(8,128)S(1)}, f32[512,1]{1,0:T(8,128)S(1)}, s32[4,128]{1,0:T(4,128)S(1)}, bf16[2048,512]{1,0...) custom-call(s32[5]{0:T(128)S(1)} %stack.23.order_ref, s32[32]{0:T(128)S(1)} %copy-done.1, bf16[512,1024]{1,0:T(8,128)(2,1)S(1)} %copy-done, ...), custom_call_target="tpu_custom_call" | custom-call | flops 1024 | bytes 1024 | tf_op jit(solution)/shard_map/pallas_call | solution.py:89
  13.9 3.8 %collective-permute-done.refs_0_ = bf16[256,1024]{1,0:T(8,128)(2,1)S(1)} collective-permute-done((bf16[256,1024]{1,0:T(8,128)(2,1)S(1)}, bf16[256,1024]{1,0:T(8,128)(2,1)S(1)}, u32[]{:S(2)}, u32[]{:S(2)}) %collective-permute-start) | collective-permute-done | bytes 524320 | tf_op jit(solution)/shard_map/ppermute | solution.py:313
  17.8 0.5 collective-permute-start.3
  18.3 0.1 collective-permute-start.4
  18.4 0.4 collective-permute-start.5
  18.8 0.3 collective-permute-done.2.refs_1_
  19.1 2.0 %collective-permute-start.11 = (bf16[128,1024]{1,0:T(8,128)(2,1)S(1)}, bf16[128,1024]{1,0:T(8,128)(2,1)S(1)}, u32[]{:S(2)}, u32[]{:S(2)}) collective-permute-start(bf16[128,1024]{1,0:T(8,128)(2,1)S(1)} %copy-done.3), channel_id=1, source_target_pairs={{0,2},{1,3},{2,0},{3,1},{4,6},{5,7},{6,4},{7,5},{8,10},{9,11},{10,... | collective-permute-start | bytes 786440 | tf_op jit(solution)/shard_map/ppermute | solution.py:313
  21.1 2.5 %shard_map.87 = (bf16[256,512]{1,0:T(8,128)(2,1)S(1)}, f32[256,1]{1,0:T(8,128)}, bf16[256,1024]{1,0:T(8,128)(2,1)S(1)}) custom-call(s32[5]{0:T(128)S(1)} %stack.23.order_ref, bf16[256,1024]{1,0:T(8,128)(2,1)S(1)} %collective-permute-done.refs_0_, bf16[64,1024]{1,0:T(8,128)(2,1)S(1)} %collective-permute-done.2.refs_1_, ...), custom_call_target="tpu_custom_call" | custom-call | flops 1024 | bytes 1024 | tf_op jit(solution)/shard_map/pallas_call | solution.py:153
  23.8 0.5 collective-permute-start.7
  24.3 0.1 collective-permute-start.8
  24.3 0.4 collective-permute-start.9
  24.8 0.2 collective-permute-done.10.refs_4_
  25.0 1.6 %collective-permute-start.16 = (bf16[256,512]{1,0:T(8,128)(2,1)S(1)}, bf16[256,512]{1,0:T(8,128)(2,1)S(1)}, u32[]{:S(2)}, u32[]{:S(2)}) collective-permute-start(bf16[256,512]{1,0:T(8,128)(2,1)S(1)} %get-tuple-element.43.refs_1_), channel_id=1, source_target_pairs={{0,4},{4,8},{8,12},{12,16},{16,20},{20,24},{24,28},{28,0},{1,5},{5... | collective-permute-start | bytes 786440 | tf_op jit(solution)/shard_map/ppermute | solution.py:347
  26.6 2.1 %shard_map.88 = (bf16[128,512]{1,0:T(8,128)(2,1)S(1)}, f32[128,1]{1,0:T(8,128)}, bf16[128,1024]{1,0:T(8,128)(2,1)S(1)}) custom-call(s32[5]{0:T(128)S(1)} %stack.23.order_ref, bf16[128,1024]{1,0:T(8,128)(2,1)S(1)} %collective-permute-done.6.refs_0_, bf16[32,1024]{1,0:T(8,128)(2,1)S(1)} %collective-permute-done.7.refs_1_, ...), custom_call_target="tpu_custom_call" | custom-call | flops 1024 | bytes 1024 | tf_op jit(solution)/shard_map/pallas_call | solution.py:153
  28.9 0.5 collective-permute-start.13
  29.5 0.4 collective-permute-start.15
  29.9 0.2 collective-permute-done.12.refs_1_
  30.1 1.6 %collective-permute-start.17 = (bf16[128,512]{1,0:T(8,128)(2,1)S(1)}, bf16[128,512]{1,0:T(8,128)(2,1)S(1)}, u32[]{:S(2)}, u32[]{:S(2)}) collective-permute-start(bf16[128,512]{1,0:T(8,128)(2,1)S(1)} %get-tuple-element.41.refs_2_.refs_3_), channel_id=1, source_target_pairs={{0,4},{4,8},{8,12},{12,16},{16,20},{20,24},{24,28},{28,0},{1,5},{5... | collective-permute-start | bytes 393224 | tf_op jit(solution)/shard_map/ppermute | solution.py:347
  31.8 1.1 %shard_map.89 = (bf16[128,512]{1,0:T(8,128)(2,1)S(1)}, f32[128,1]{1,0:T(8,128)S(1)}) custom-call(s32[5]{0:T(128)S(1)} %stack.23.order_ref, bf16[128,1024]{1,0:T(8,128)(2,1)S(1)} %collective-permute-done.11.refs_0_, bf16[32,1024]{1,0:T(8,128)(2,1)S(1)} %collective-permute-done.12.refs_1_, bf16[32,1024]{1,0:T(8,128)(2,1)S(1)} %collective-permute-done.13.refs_2_, ...), custom_call_target="tpu_custom_call" | custom-call | flops 1024 | bytes 1024 | tf_op jit(solution)/shard_map/pallas_call | solution.py:153
  32.9 1.8 %collective-permute-start.18 = (bf16[128,512]{1,0:T(8,128)(2,1)S(1)}, bf16[128,512]{1,0:T(8,128)(2,1)S(1)}, u32[]{:S(2)}, u32[]{:S(2)}) collective-permute-start(bf16[128,512]{1,0:T(8,128)(2,1)S(1)} %get-tuple-element.42.refs_3_.refs_4_), channel_id=1, source_target_pairs={{0,4},{4,8},{8,12},{12,16},{16,20},{20,24},{24,28},{28,0},{1,5},{5... | collective-permute-start | bytes 393224 | tf_op jit(solution)/shard_map/ppermute | solution.py:350
  34.6 1.3 %shard_map.90.refs_2_ = bf16[128,1024]{1,0:T(8,128)(2,1)S(1)} custom-call(s32[5]{0:T(128)S(1)} %stack.23.order_ref, bf16[128,1024]{1,0:T(8,128)(2,1)S(1)} %collective-permute-done.11.refs_0_, bf16[32,1024]{1,0:T(8,128)(2,1)S(1)} %collective-permute-done.12.refs_1_, bf16[32,1024]{1,0:T(8,128)(2,1)S(1)} %collective-permute-done.13.refs_2_, ...), custom_call_target="tpu_custom_call" | custom-call | flops 1024 | bytes 1024 | tf_op jit(solution)/shard_map/pallas_call | solution.py:153
  35.9 0.8 %collective-permute-done.16.refs_4_.refs_5_ = bf16[256,512]{1,0:T(8,128)(2,1)S(1)} collective-permute-done((bf16[256,512]{1,0:T(8,128)(2,1)S(1)}, bf16[256,512]{1,0:T(8,128)(2,1)S(1)}, u32[]{:S(2)}, u32[]{:S(2)}) %collective-permute-start.16) | collective-permute-done | bytes 262176 | tf_op jit(solution)/shard_map/ppermute | solution.py:347
  36.7 3.5 %shard_map.91 = (bf16[512,1024]{1,0:T(8,128)(2,1)}, f32[2,8,128]{2,1,0:T(8,128)S(1)}) custom-call(bf16[256,1024]{1,0:T(8,128)(2,1)S(1)} %get-tuple-element.45.refs_0_, bf16[256,512]{1,0:T(8,128)(2,1)S(1)} %get-tuple-element.43.refs_1_, bf16[128,512]{1,0:T(8,128)(2,1)S(1)} %get-tuple-element.41.refs_2_.refs_3_, ...), custom_call_target="tpu_custom_call" | custom-call | flops 1024 | bytes 1024 | tf_op jit(solution)/shard_map/pallas_call | solution.py:358
  40.1 1.8 %collective-permute-done.18.refs_7_ = bf16[128,512]{1,0:T(8,128)(2,1)S(1)} collective-permute-done((bf16[128,512]{1,0:T(8,128)(2,1)S(1)}, bf16[128,512]{1,0:T(8,128)(2,1)S(1)}, u32[]{:S(2)}, u32[]{:S(2)}) %collective-permute-start.18) | collective-permute-done | bytes 131104 | tf_op jit(solution)/shard_map/ppermute | solution.py:350
  41.9 4.0 %shard_map.92 = (bf16[512,1024]{1,0:T(8,128)(2,1)}, bf16[8,8,128]{2,1,0:T(8,128)(2,1)S(1)}) custom-call(s32[4]{0:T(128)S(1)} %copy-done.2, bf16[128,1024]{1,0:T(8,128)(2,1)S(1)} %get-tuple-element.39.refs_1_, bf16[128,1024]{1,0:T(8,128)(2,1)S(1)} %shard_map.90.refs_2_, ...), custom_call_target="tpu_custom_call", output_to_operand_aliasing={{0}: (10, {})} | custom-call | flops 1024 | bytes 1024 | tf_op jit(solution)/shard_map/pallas_call | solution.py:370
  45.9 9.4 %all_to_all.5.recv_ref = bf16[8,8,128]{2,1,0:T(8,128)(2,1)S(1)} all-to-all(bf16[8,8,128]{2,1,0:T(8,128)(2,1)S(1)} %get-tuple-element.49), channel_id=1, replica_groups=mesh['attn'=8,'proj'=4] {'attn'}, dimensions={0} | all-to-all | bytes 32768 | tf_op jit(solution)/shard_map/all_to_all | solution.py:383
  55.2 0.6 %shard_map.93 = f32[4,8,128]{2,1,0:T(8,128)} custom-call(bf16[8,8,128]{2,1,0:T(8,128)(2,1)S(1)} %all_to_all.5.recv_ref), custom_call_target="tpu_custom_call" | custom-call | tf_op jit(solution)/shard_map/pallas_call | solution.py:384
  (32 shorter events, 0.4 us)
Async XLA Ops:
  0.6 6.2 %copy-start = (bf16[512,1024]{1,0:T(8,128)(2,1)S(1)}, bf16[512,1024]{1,0:T(8,128)(2,1)}, u32[]{:S(2)}) copy-start(bf16[512,1024]{1,0:T(8,128)(2,1)} %x_ref.1) | copy-start | bytes 3145732
  0.6 6.1 %copy-start.4 = (f32[4096]{0:T(1024)S(1)}, f32[4096]{0:T(1024)}, u32[]{:S(2)}) copy-start(f32[4096]{0:T(1024)} %param.8) | copy-start | bytes 49156
  0.7 6.2 %copy-start.1 = (s32[32]{0:T(128)S(1)}, s32[32]{0:T(128)}, u32[]{:S(2)}) copy-start(s32[32]{0:T(128)} %docs_ref.1) | copy-start | bytes 388
  0.7 6.2 %collective-permute-start.1 = (bf16[512,1024]{1,0:T(8,128)(2,1)}, bf16[512,1024]{1,0:T(8,128)(2,1)S(1)}, u32[]{:S(2)}, u32[]{:S(2)}) collective-permute-start(bf16[512,1024]{1,0:T(8,128)(2,1)} %x_ref.1), channel_id=1, source_target_pairs={{0,1},{1,0},{2,3},{3,2},{4,5},{5,4},{6,7},{7,6},{8,9},{9,8},{10,11... | collective-permute-start | bytes 3145736 | tf_op jit(solution)/shard_map/ppermute | solution.py:314
  2.3 15.4 %collective-permute-start = (bf16[256,1024]{1,0:T(8,128)(2,1)S(1)}, bf16[256,1024]{1,0:T(8,128)(2,1)S(1)}, u32[]{:S(2)}, u32[]{:S(2)}) collective-permute-start(bf16[256,1024]{1,0:T(8,128)(2,1)S(1)} %slice.45), channel_id=1, source_target_pairs={{0,2},{1,3},{2,0},{3,1},{4,6},{5,7},{6,4},{7,5},{8,10},{9,11},{10,... | collective-permute-start | bytes 1572872 | tf_op jit(solution)/shard_map/ppermute | solution.py:313
  6.7 16.9 %collective-permute-start.6 = (bf16[128,1024]{1,0:T(8,128)(2,1)}, bf16[128,1024]{1,0:T(8,128)(2,1)S(1)}, u32[]{:S(2)}, u32[]{:S(2)}) collective-permute-start(bf16[128,1024]{1,0:T(8,128)(2,1)} %get-tuple-element.51), channel_id=1, source_target_pairs={{0,2},{1,3},{2,0},{3,1},{4,6},{5,7},{6,4},{7,5},{8,10},{9,11},{10,... | collective-permute-start | bytes 786440 | tf_op jit(solution)/shard_map/ppermute | solution.py:313
  6.9 12.3 %copy-start.3 = (bf16[128,1024]{1,0:T(8,128)(2,1)S(1)}, bf16[128,1024]{1,0:T(8,128)(2,1)}, u32[]{:S(2)}) copy-start(bf16[128,1024]{1,0:T(8,128)(2,1)} %get-tuple-element.50) | copy-start | bytes 786436
  17.7 1.4 %collective-permute-start.2 = (bf16[64,1024]{1,0:T(8,128)(2,1)S(1)}, bf16[64,1024]{1,0:T(8,128)(2,1)S(1)}, u32[]{:S(2)}, u32[]{:S(2)}) collective-permute-start(bf16[64,1024]{1,0:T(8,128)(2,1)S(1)} %get-tuple-element.55), channel_id=1, source_target_pairs={{0,1},{1,0},{2,3},{3,2},{4,5},{5,4},{6,7},{7,6},{8,9},{9,8},{10,11... | collective-permute-start | bytes 393224 | tf_op jit(solution)/shard_map/ppermute | solution.py:340
  17.8 3.3 %collective-permute-start.3 = (bf16[64,1024]{1,0:T(8,128)(2,1)S(1)}, bf16[64,1024]{1,0:T(8,128)(2,1)S(1)}, u32[]{:S(2)}, u32[]{:S(2)}) collective-permute-start(bf16[64,1024]{1,0:T(8,128)(2,1)S(1)} %get-tuple-element.54), channel_id=1, source_target_pairs={{0,1},{1,0},{2,3},{3,2},{4,5},{5,4},{6,7},{7,6},{8,9},{9,8},{10,11... | collective-permute-start | bytes 393224 | tf_op jit(solution)/shard_map/ppermute | solution.py:340
  18.3 2.8 %collective-permute-start.4 = (bf16[64,1024]{1,0:T(8,128)(2,1)S(1)}, bf16[64,1024]{1,0:T(8,128)(2,1)S(1)}, u32[]{:S(2)}, u32[]{:S(2)}) collective-permute-start(bf16[64,1024]{1,0:T(8,128)(2,1)S(1)} %get-tuple-element.53), channel_id=1, source_target_pairs={{0,1},{1,0},{2,3},{3,2},{4,5},{5,4},{6,7},{7,6},{8,9},{9,8},{10,11... | collective-permute-start | bytes 393224 | tf_op jit(solution)/shard_map/ppermute | solution.py:340
  18.4 2.7 %collective-permute-start.5 = (bf16[64,1024]{1,0:T(8,128)(2,1)S(1)}, bf16[64,1024]{1,0:T(8,128)(2,1)S(1)}, u32[]{:S(2)}, u32[]{:S(2)}) collective-permute-start(bf16[64,1024]{1,0:T(8,128)(2,1)S(1)} %get-tuple-element.52), channel_id=1, source_target_pairs={{0,1},{1,0},{2,3},{3,2},{4,5},{5,4},{6,7},{7,6},{8,9},{9,8},{10,11... | collective-permute-start | bytes 393224 | tf_op jit(solution)/shard_map/ppermute | solution.py:340
  19.1 9.7 %collective-permute-start.11 = (bf16[128,1024]{1,0:T(8,128)(2,1)S(1)}, bf16[128,1024]{1,0:T(8,128)(2,1)S(1)}, u32[]{:S(2)}, u32[]{:S(2)}) collective-permute-start(bf16[128,1024]{1,0:T(8,128)(2,1)S(1)} %copy-done.3), channel_id=1, source_target_pairs={{0,2},{1,3},{2,0},{3,1},{4,6},{5,7},{6,4},{7,5},{8,10},{9,11},{10,... | collective-permute-start | bytes 786440 | tf_op jit(solution)/shard_map/ppermute | solution.py:313
  23.7 1.3 %collective-permute-start.10 = (bf16[32,1024]{1,0:T(8,128)(2,1)S(1)}, bf16[32,1024]{1,0:T(8,128)(2,1)S(1)}, u32[]{:S(2)}, u32[]{:S(2)}) collective-permute-start(bf16[32,1024]{1,0:T(8,128)(2,1)S(1)} %get-tuple-element.60), channel_id=1, source_target_pairs={{0,1},{1,0},{2,3},{3,2},{4,5},{5,4},{6,7},{7,6},{8,9},{9,8},{10,11... | collective-permute-start | bytes 196616 | tf_op jit(solution)/shard_map/ppermute | solution.py:340
  23.8 2.9 %collective-permute-start.7 = (bf16[32,1024]{1,0:T(8,128)(2,1)S(1)}, bf16[32,1024]{1,0:T(8,128)(2,1)S(1)}, u32[]{:S(2)}, u32[]{:S(2)}) collective-permute-start(bf16[32,1024]{1,0:T(8,128)(2,1)S(1)} %get-tuple-element.63), channel_id=1, source_target_pairs={{0,1},{1,0},{2,3},{3,2},{4,5},{5,4},{6,7},{7,6},{8,9},{9,8},{10,11... | collective-permute-start | bytes 196616 | tf_op jit(solution)/shard_map/ppermute | solution.py:340
  24.3 2.4 %collective-permute-start.8 = (bf16[32,1024]{1,0:T(8,128)(2,1)S(1)}, bf16[32,1024]{1,0:T(8,128)(2,1)S(1)}, u32[]{:S(2)}, u32[]{:S(2)}) collective-permute-start(bf16[32,1024]{1,0:T(8,128)(2,1)S(1)} %get-tuple-element.62), channel_id=1, source_target_pairs={{0,1},{1,0},{2,3},{3,2},{4,5},{5,4},{6,7},{7,6},{8,9},{9,8},{10,11... | collective-permute-start | bytes 196616 | tf_op jit(solution)/shard_map/ppermute | solution.py:340
  24.3 2.3 %collective-permute-start.9 = (bf16[32,1024]{1,0:T(8,128)(2,1)S(1)}, bf16[32,1024]{1,0:T(8,128)(2,1)S(1)}, u32[]{:S(2)}, u32[]{:S(2)}) collective-permute-start(bf16[32,1024]{1,0:T(8,128)(2,1)S(1)} %get-tuple-element.61), channel_id=1, source_target_pairs={{0,1},{1,0},{2,3},{3,2},{4,5},{5,4},{6,7},{7,6},{8,9},{9,8},{10,11... | collective-permute-start | bytes 196616 | tf_op jit(solution)/shard_map/ppermute | solution.py:340
  25.0 11.7 %collective-permute-start.16 = (bf16[256,512]{1,0:T(8,128)(2,1)S(1)}, bf16[256,512]{1,0:T(8,128)(2,1)S(1)}, u32[]{:S(2)}, u32[]{:S(2)}) collective-permute-start(bf16[256,512]{1,0:T(8,128)(2,1)S(1)} %get-tuple-element.43.refs_1_), channel_id=1, source_target_pairs={{0,4},{4,8},{8,12},{12,16},{16,20},{20,24},{24,28},{28,0},{1,5},{5... | collective-permute-start | bytes 786440 | tf_op jit(solution)/shard_map/ppermute | solution.py:347
  28.8 1.3 %collective-permute-start.12 = (bf16[32,1024]{1,0:T(8,128)(2,1)S(1)}, bf16[32,1024]{1,0:T(8,128)(2,1)S(1)}, u32[]{:S(2)}, u32[]{:S(2)}) collective-permute-start(bf16[32,1024]{1,0:T(8,128)(2,1)S(1)} %get-tuple-element.59), channel_id=1, source_target_pairs={{0,1},{1,0},{2,3},{3,2},{4,5},{5,4},{6,7},{7,6},{8,9},{9,8},{10,11... | collective-permute-start | bytes 196616 | tf_op jit(solution)/shard_map/ppermute | solution.py:340
  28.9 2.9 %collective-permute-start.13 = (bf16[32,1024]{1,0:T(8,128)(2,1)S(1)}, bf16[32,1024]{1,0:T(8,128)(2,1)S(1)}, u32[]{:S(2)}, u32[]{:S(2)}) collective-permute-start(bf16[32,1024]{1,0:T(8,128)(2,1)S(1)} %get-tuple-element.58), channel_id=1, source_target_pairs={{0,1},{1,0},{2,3},{3,2},{4,5},{5,4},{6,7},{7,6},{8,9},{9,8},{10,11... | collective-permute-start | bytes 196616 | tf_op jit(solution)/shard_map/ppermute | solution.py:340
  29.4 2.4 %collective-permute-start.14 = (bf16[32,1024]{1,0:T(8,128)(2,1)S(1)}, bf16[32,1024]{1,0:T(8,128)(2,1)S(1)}, u32[]{:S(2)}, u32[]{:S(2)}) collective-permute-start(bf16[32,1024]{1,0:T(8,128)(2,1)S(1)} %get-tuple-element.57), channel_id=1, source_target_pairs={{0,1},{1,0},{2,3},{3,2},{4,5},{5,4},{6,7},{7,6},{8,9},{9,8},{10,11... | collective-permute-start | bytes 196616 | tf_op jit(solution)/shard_map/ppermute | solution.py:340
  29.5 2.3 %collective-permute-start.15 = (bf16[32,1024]{1,0:T(8,128)(2,1)S(1)}, bf16[32,1024]{1,0:T(8,128)(2,1)S(1)}, u32[]{:S(2)}, u32[]{:S(2)}) collective-permute-start(bf16[32,1024]{1,0:T(8,128)(2,1)S(1)} %get-tuple-element.56), channel_id=1, source_target_pairs={{0,1},{1,0},{2,3},{3,2},{4,5},{5,4},{6,7},{7,6},{8,9},{9,8},{10,11... | collective-permute-start | bytes 196616 | tf_op jit(solution)/shard_map/ppermute | solution.py:340
  30.1 10.0 %collective-permute-start.17 = (bf16[128,512]{1,0:T(8,128)(2,1)S(1)}, bf16[128,512]{1,0:T(8,128)(2,1)S(1)}, u32[]{:S(2)}, u32[]{:S(2)}) collective-permute-start(bf16[128,512]{1,0:T(8,128)(2,1)S(1)} %get-tuple-element.41.refs_2_.refs_3_), channel_id=1, source_target_pairs={{0,4},{4,8},{8,12},{12,16},{16,20},{20,24},{24,28},{28,0},{1,5},{5... | collective-permute-start | bytes 393224 | tf_op jit(solution)/shard_map/ppermute | solution.py:347
  32.9 9.0 %collective-permute-start.18 = (bf16[128,512]{1,0:T(8,128)(2,1)S(1)}, bf16[128,512]{1,0:T(8,128)(2,1)S(1)}, u32[]{:S(2)}, u32[]{:S(2)}) collective-permute-start(bf16[128,512]{1,0:T(8,128)(2,1)S(1)} %get-tuple-element.42.refs_3_.refs_4_), channel_id=1, source_target_pairs={{0,4},{4,8},{8,12},{12,16},{16,20},{20,24},{24,28},{28,0},{1,5},{5... | collective-permute-start | bytes 393224 | tf_op jit(solution)/shard_map/ppermute | solution.py:350
  34.6 7.3 %copy-start.2 = (s32[4]{0:T(128)S(1)}, s32[4]{0:T(128)}, u32[]{:S(2)}) copy-start(s32[4]{0:T(128)} %refs_0_.1) | copy-start | bytes 52

commit v3 on v2

v3 whole, which is shorter than its diff:
```python
import functools
import math

import jax
import jax.numpy as jnp
from jax import lax
from jax.experimental import pallas as pl
from jax.experimental.pallas import tpu as pltpu
from jax.sharding import PartitionSpec as P

HEAD_SIZE = 128
QUERY_BLOCK_ROWS = 128
CORES = 2
LAST_ROWS = 128

masked_value = -1e30
norm_eps = 1e-05
score_scale = 1.0 / HEAD_SIZE**0.5
log2_scale = score_scale * math.log2(math.e)

VMEM = pl.BlockSpec(memory_space=pltpu.VMEM)
SMEM = pl.BlockSpec(memory_space=pltpu.SMEM)
HBM = pl.BlockSpec(memory_space=pltpu.HBM)


def params(limit=16 << 20):
    return pltpu.CompilerParams(vmem_limit_bytes=limit)


def part_terms(x, gain):
    values = x.astype(jnp.float32)
    scaled = (values * gain).astype(jnp.bfloat16)
    return scaled, jnp.sum(values * values, axis=1, keepdims=True)


def cost():
    return pl.CostEstimate(flops=1 << 10, bytes_accessed=1 << 10, transcendentals=0)


def local_kernel(order_ref, docs_ref, x_ref, other_ref, gain_ref, wk, wv, wq, *refs):
    q_ref, kv_ref, sq_ref, bound_ref, kv_rest, q_rest, kv_own, q_own, sems = refs
    features, width = x_ref.shape[1], wk.shape[1]

    def fetch(slot, kv_to, q_to, place):
        rows = pl.ds(pl.multiple_of(order_ref[slot] * features, features), features)
        here = pl.ds(place * features, features)
        copies = (
            pltpu.make_async_copy(wk.at[rows, :], kv_to.at[here, pl.ds(0, width)], sems.at[slot, 0]),
            pltpu.make_async_copy(wv.at[rows, :], kv_to.at[here, pl.ds(width, width)], sems.at[slot, 1]),
            pltpu.make_async_copy(wq.at[rows, :], q_to.at[here, :], sems.at[slot, 2]),
        )
        for copy in copies:
            copy.start()
        return copies

    mine = [fetch(slot, kv_own, q_own, slot) for slot in range(CORES)]
    rest = [fetch(CORES + i, kv_rest, q_rest, i) for i in range(q_rest.shape[0] // features)]

    shape = bound_ref.shape
    base = order_ref[order_ref.shape[0] - 1]
    position = lax.broadcasted_iota(jnp.int32, shape, 0) * shape[1] + lax.broadcasted_iota(jnp.int32, shape, 1)
    start = -base
    bounds = jnp.full(shape, start, jnp.int32)
    for d in range(docs_ref.shape[0]):
        bounds = jnp.where(position >= start, start, bounds)
        start = start + docs_ref[d]
    bound_ref[...] = bounds

    parts = [
        part_terms(ref[...], gain_ref[pl.ds(order_ref[slot], 1), :]) for slot, ref in enumerate((x_ref, other_ref))
    ]
    sq_ref[...] = parts[0][1] + parts[1][1]
    scaled = jnp.concatenate([part[0] for part in parts], axis=1)
    for k, v, _ in mine:
        k.wait()
        v.wait()
    kv_ref[...] = jnp.dot(scaled, kv_own[...], preferred_element_type=jnp.float32)
    for _, _, q in mine:
        q.wait()
    q_ref[...] = jnp.dot(scaled, q_own[...], preferred_element_type=jnp.float32)
    for copies in rest:
        for copy in copies:
            copy.wait()


def local_part(order, docs, x, other, gains, wk, wv, wq):
    rows, features = x.shape
    q_width, kv_width = wq.shape[1], 2 * wk.shape[1]
    rest = wq.shape[0] - CORES * features
    return pl.pallas_call(
        local_kernel,
        out_shape=(
            pltpu.VMEM((rows, q_width), jnp.float32),
            pltpu.VMEM((rows, kv_width), jnp.float32),
            pltpu.VMEM((rows, 1), jnp.float32),
            pltpu.VMEM((rows // QUERY_BLOCK_ROWS, QUERY_BLOCK_ROWS), jnp.int32),
            pltpu.VMEM((rest, kv_width), jnp.bfloat16),
            pltpu.VMEM((rest, q_width), jnp.bfloat16),
        ),
        in_specs=[SMEM, SMEM, VMEM, VMEM, VMEM, HBM, HBM, HBM],
        out_specs=(VMEM,) * 6,
        scratch_shapes=[
            pltpu.VMEM((CORES * features, kv_width), jnp.bfloat16),
            pltpu.VMEM((CORES * features, q_width), jnp.bfloat16),
            pltpu.SemaphoreType.DMA((wq.shape[0] // features, 3)),
        ],
        compiler_params=params(32 << 20),
        cost_estimate=cost(),
    )(order, docs, x, other, gains, wk, wv, wq)


def chunk_kernel(sizes, row, order_ref, *refs):
    pieces, refs = refs[: sum(sizes)], refs[sum(sizes) :]
    gain_ref, wkv_ref, kva_ref, sq_ref, wq_ref, qa_ref, kv_ref, q_ref = refs
    terms = []
    for i, size in enumerate(sizes):
        x = jnp.concatenate([ref[...] for ref in pieces[:size]], axis=0)
        pieces = pieces[size:]
        terms.append(part_terms(x, gain_ref[pl.ds(order_ref[CORES + i], 1), :]))
    scaled = jnp.concatenate([x for x, _ in terms], axis=1)
    squares = sum(square for _, square in terms)
    here = slice(row, row + scaled.shape[0])
    features = scaled.shape[1] // len(sizes)
    inverse = lax.rsqrt((sq_ref[here, :] + squares) / (features * (len(sizes) + CORES)) + norm_eps)
    total = kva_ref[here, :] + jnp.dot(scaled, wkv_ref[...], preferred_element_type=jnp.float32)
    kv_ref[...] = (total * inverse).astype(jnp.bfloat16)
    total = qa_ref[here, :] + jnp.dot(scaled, wq_ref[...], preferred_element_type=jnp.float32)
    q_ref[...] = (total * (inverse * log2_scale)).astype(jnp.bfloat16)


def project(rows, row, order, groups, gains, wkv, kv_acc, squares, wq, q_acc):
    operands = [piece for group in groups for piece in group] + [gains, wkv, kv_acc, squares, wq, q_acc]
    return pl.pallas_call(
        functools.partial(chunk_kernel, [len(group) for group in groups], row),
        out_shape=(
            jax.ShapeDtypeStruct((rows, wkv.shape[1]), jnp.bfloat16),
            jax.ShapeDtypeStruct((rows, wq.shape[1]), jnp.bfloat16),
        ),
        in_specs=[SMEM] + [VMEM] * len(operands),
        out_specs=(VMEM, VMEM),
        compiler_params=params(),
        cost_estimate=cost(),
    )(order, *operands)


def block_parts(refs, chunks):
    found = {}
    block = QUERY_BLOCK_ROWS
    for i in range(chunks[0][1] // block):
        parts = []
        for ref, (low, high) in zip(refs, chunks):
            first, last = max(low, i * block), min(high, (i + 1) * block)
            if first < last:
                parts.insert(0, (ref, first - low, last - low))
        if sum(last - first for _, first, last in parts) == block:
            found[i] = parts
    return found


def key_bias(bounds, key_starts, row_start):
    rows = QUERY_BLOCK_ROWS
    bounds = jnp.transpose(jnp.broadcast_to(bounds, (rows, rows)))
    query_pos = row_start + lax.broadcasted_iota(jnp.int32, (rows, rows), 0)
    bias = []
    for start in key_starts:
        key_pos = start + lax.broadcasted_iota(jnp.int32, (rows, rows), 1)
        ok = key_pos >= bounds
        if start == row_start:
            ok = ok & (key_pos <= query_pos)
        bias.append(jnp.where(ok, 0.0, masked_value))
    return jnp.concatenate(bias, axis=1)


def attend_blocks(wanted, blocks, queries, owns, priors, bounds_ref, outs, finished=None):
    rows = QUERY_BLOCK_ROWS
    width = owns[wanted[0]][0][0].shape[1] // 2
    kv_heads, group = width // HEAD_SIZE, outs[wanted[0]][0].shape[1] // width
    keys = {
        b: [part for i in range(b, blocks) for part in priors[i]] + [part for i in range(b + 1) for part in owns[i]]
        for b in wanted
    }
    bias = {
        b: key_bias(
            bounds_ref[b : b + 1, :],
            [(i - blocks) * rows for i in range(b, blocks)] + [i * rows for i in range(b + 1)],
            b * rows,
        )
        for b in wanted
    }
    steps = [(b, n) for b in wanted for n in range(kv_heads)]
    lane = lax.broadcasted_iota(jnp.int32, (rows, HEAD_SIZE), 1)
    highests = {b: jnp.zeros((rows, HEAD_SIZE), jnp.float32) for b in wanted}
    totals = {b: jnp.ones((rows, HEAD_SIZE), jnp.float32) for b in wanted}

    def columns(parts, first):
        return jnp.concatenate([ref[i:j, first : first + HEAD_SIZE] for ref, i, j in parts], axis=0)

    def score(b, n):
        heads = range(n * group, (n + 1) * group)
        stacked = jnp.concatenate([columns(queries[b], h * HEAD_SIZE) for h in heads], axis=0)
        return lax.dot_general(
            stacked, columns(keys[b], n * HEAD_SIZE), (((1,), (1,)), ((), ())), preferred_element_type=jnp.float32
        )

    def weigh(b, scores):
        shape = scores.shape
        scores = (scores.reshape(group, rows, shape[1]) + bias[b][None]).reshape(shape)
        highest = jnp.max(scores, axis=1, keepdims=True)
        return highest, jnp.exp2(scores - highest)

    def finish(b, n, highest, weights):
        total = jnp.sum(weights, axis=1, keepdims=True)
        summed = jnp.dot(
            weights.astype(jnp.bfloat16),
            columns(keys[b], width + n * HEAD_SIZE),
            preferred_element_type=jnp.float32,
        )
        result = (summed / total).astype(jnp.bfloat16)
        for g in range(group):
            h, part = n * group + g, slice(g * rows, (g + 1) * rows)
            ref, at = outs[b]
            ref[at : at + rows, h * HEAD_SIZE : (h + 1) * HEAD_SIZE] = result[part]
            highests[b] = jnp.where(lane == h, highest[part], highests[b])
            totals[b] = jnp.where(lane == h, total[part], totals[b])
        if finished is not None and n == kv_heads - 1:
            finished(b)

    scores, pending = score(*steps[0]), None
    for i, (b, n) in enumerate(steps):
        ahead = score(*steps[i + 1]) if i + 1 < len(steps) else None
        highest, weights = weigh(b, scores)
        if pending is not None:
            finish(*pending)
        pending, scores = (b, n, highest, weights), ahead
    finish(*pending)
    return {
        b: jnp.transpose((highests[b] + jnp.log2(totals[b])) * math.log(2.0))[: kv_heads * group, :] for b in wanted
    }


def attention_kernel(chunks, wanted, *refs):
    count = len(chunks)
    prior_count = len(refs) - 2 * count - 3
    queries = block_parts(refs[:count], chunks)
    owns = block_parts(refs[count : 2 * count], chunks)
    priors = block_parts(refs[2 * count : -3], chunks[:prior_count])
    bounds_ref, out_ref, lse_ref = refs[-3:]
    outs = {b: (out_ref, (b - wanted[0]) * QUERY_BLOCK_ROWS) for b in wanted}
    lses = attend_blocks(wanted, chunks[0][1] // QUERY_BLOCK_ROWS, queries, owns, priors, bounds_ref, outs)
    for b in wanted:
        lse_ref[b - wanted[0]] = lses[b]


def last_attention_kernel(chunks, servers, server_ref, *refs):
    count, rows = len(chunks), QUERY_BLOCK_ROWS
    blocks = chunks[0][1] // rows
    queries = block_parts(refs[:count], chunks)
    owns = block_parts(refs[count : 2 * count], chunks)
    priors = block_parts(refs[2 * count : 3 * count], chunks)
    bounds_ref, *ready, out_hbm, send_ref, here, sems = refs[3 * count :]
    lses, copies = {}, []
    for i in range(0, len(ready), 2):
        out_ref, lse_ref = ready[i : i + 2]
        low = 1 + len(lses)
        lses.update({low + j: lse_ref[j] for j in range(lse_ref.shape[0])})
        place = out_hbm.at[pl.ds(low * rows, out_ref.shape[0]), :]
        copies.append(pltpu.make_async_copy(out_ref, place, sems.at[len(copies)]))
        copies[-1].start()

    def finished(block):
        copies.append(pltpu.make_async_copy(here, out_hbm.at[pl.ds(0, rows), :], sems.at[len(copies)]))
        copies[-1].start()

    lses.update(attend_blocks([0], blocks, queries, owns, priors, bounds_ref, {0: (here, 0)}, finished))
    for s in range(servers):
        value = jnp.full(lses[0].shape, jnp.inf, jnp.float32)
        for block, lse in lses.items():
            value = jnp.where(server_ref[block] == s, lse, value)
        send_ref[s] = value.astype(jnp.bfloat16)
    for copy in copies:
        copy.wait()


def pick_kernel(blocks, recv_ref, out_ref):
    shape = recv_ref.shape[1:]
    rank = jnp.zeros(shape, jnp.int32)
    picked = [jnp.zeros(shape, jnp.float32) for _ in range(blocks)]
    for i in range(recv_ref.shape[0]):
        value = recv_ref[i].astype(jnp.float32)
        valid = value < jnp.inf
        for k in range(blocks):
            picked[k] = jnp.where(valid & (rank == k), value, picked[k])
        rank = rank + valid.astype(jnp.int32)
    for k in range(blocks):
        out_ref[k] = picked[k]


def shards(tokens, norm_gain, w_query, w_key, value_matrix, doc_lengths, block_server):
    rows, features = tokens.shape
    width = w_key.shape[1]
    heads = w_query.shape[1] // HEAD_SIZE
    block = QUERY_BLOCK_ROWS
    blocks = rows // block
    servers = lax.axis_size("attn")
    sharers = lax.axis_size("proj")
    chips = sharers // CORES
    me_attn = lax.axis_index("attn")
    me_proj = lax.axis_index("proj")
    sibling = [(i, i ^ 1) for i in range(sharers)]

    def across(distance):
        return [(i, (i + distance * CORES) % sharers) for i in range(sharers)]

    middle = rows // 2
    chunks = [(middle, rows), (LAST_ROWS, middle), (0, LAST_ROWS)]
    arrived = []
    rest = tokens
    for low, high in chunks:
        piece = rest[low:high]
        if not arrived:
            piece, rest = lax.optimization_barrier((piece, rest))
        arrived.append([lax.ppermute(piece, "proj", across(d)) for d in range(1, chips)])
    other = lax.ppermute(tokens, "proj", sibling)

    order = [me_proj, me_proj ^ 1]
    for d in range(1, chips):
        source = (me_proj + sharers - d * CORES) % sharers
        order += [source, source ^ 1]
    order = jnp.stack([*order, me_attn * rows]).astype(jnp.int32)
    gains = norm_gain.reshape(sharers, features)

    w_key, value_matrix, w_query = [
        pltpu.with_memory_space_constraint(w, pltpu.HBM) for w in (w_key, value_matrix, w_query)
    ]
    q_acc, kv_acc, squares, bounds, wkv_rest, wq_rest = local_part(
        order, doc_lengths, tokens, other, gains, w_key, value_matrix, w_query
    )

    onward = [(i, (i + 1) % servers) for i in range(servers)]
    own, prior, queries = [], [], []
    tie = kv_acc
    for (low, high), sources in zip(chunks, arrived):
        sources, tie = lax.optimization_barrier((sources, tie))
        cuts = range(0, high - low, 64)
        groups = []
        for piece in sources:
            pieces = [piece[i:j] for i, j in zip(cuts, [*cuts[1:], piece.shape[0]])]
            groups += [[piece], [lax.ppermute(part, "proj", sibling) for part in pieces]]
        kv, q = project(high - low, low, order, groups, gains, wkv_rest, kv_acc, squares, wq_rest, q_acc)
        tie = q
        prior.append(lax.ppermute(kv, "attn", onward))
        own.append(kv)
        queries.append(q)

    queries = list(lax.optimization_barrier(tuple(queries)))

    def attend(wanted, priors):
        return pl.pallas_call(
            functools.partial(attention_kernel, chunks, wanted),
            out_shape=(
                jax.ShapeDtypeStruct((len(wanted) * block, heads * HEAD_SIZE), jnp.bfloat16),
                jax.ShapeDtypeStruct((len(wanted), heads, block), jnp.float32),
            ),
            in_specs=[VMEM] * (2 * len(chunks) + len(priors) + 1),
            out_specs=(VMEM, VMEM),
            compiler_params=params(24 << 20),
            cost_estimate=cost(),
        )(*queries, *own, *priors, bounds)

    above = attend(list(range(blocks // 2, blocks)), prior[:1])
    below = attend(list(range(1, blocks // 2)), prior[:2])
    out, send = pl.pallas_call(
        functools.partial(last_attention_kernel, chunks, servers),
        out_shape=(
            jax.ShapeDtypeStruct((rows, heads * HEAD_SIZE), jnp.bfloat16),
            jax.ShapeDtypeStruct((servers, heads, block), jnp.bfloat16),
        ),
        in_specs=[SMEM] + [VMEM] * (3 * len(chunks) + 5),
        out_specs=(HBM, VMEM),
        scratch_shapes=[pltpu.VMEM((block, heads * HEAD_SIZE), jnp.bfloat16), pltpu.SemaphoreType.DMA((3,))],
        compiler_params=params(24 << 20),
        cost_estimate=cost(),
    )(block_server, *queries, *own, *prior, bounds, *below, *above)
    recv = lax.all_to_all(send, "attn", split_axis=0, concat_axis=0, tiled=True)
    served = pl.pallas_call(
        functools.partial(pick_kernel, blocks),
        out_shape=jax.ShapeDtypeStruct((blocks, heads, block), jnp.float32),
        in_specs=[VMEM],
        out_specs=VMEM,
        compiler_params=params(),
    )(recv)
    return (out, served)


def solution(mesh):
    return jax.shard_map(
        shards,
        mesh=mesh,
        in_specs=(
            P("attn", "proj"),
            P(),
            P(None, "proj"),
            P(None, "proj"),
            P(None, "proj"),
            P(),
            P("attn"),
        ),
        out_specs=(P("attn", "proj"), P("attn", "proj", None)),
        check_vma=False,
    )
```

time: 56.1 us -> 53.8 us (0.959)
  Pallas kernels: 22.1 us -> 19.5 us
  waiting for transfers between devices: 7.14 us -> 8.35 us
  starting transfers between devices: 13.4 us -> 12.5 us
    pallas_call x1, Pallas kernels: 3.96 us -> 2.54 us  [shards(): pl.pallas_call(functools.partial(last_attention_kernel, chunks, servers),...]
    pallas_call x5, Pallas kernels: 10.5 us -> 9.35 us  [the longest x3 5.85 us: project(): pl.pallas_call(functools.partial(chunk_kernel, [len(group) for group in g...]
    ppermute x3, waiting for transfers between devices: 3.81 us -> 4.89 us  [shards(): lax.ppermute(piece, 'proj', across(d))]
    ppermute x12 -> x8, starting transfers between devices: 3.23 us -> 2.21 us  [shards(): lax.ppermute(part, 'proj', sibling)]
    ppermute x3, waiting for transfers between devices: 2.51 us -> 3.11 us  [shards(): prior.append(lax.ppermute(kv, 'attn', onward))]
  transfers between devices with their start and end apart: 19 -> 15, of which waited for: 6 -> 6; matrix products, arithmetic and copies ran while one was open for 6% -> 6% of each run, Pallas kernels for 31% -> 30%
where the time goes in v3:
time: 53.8 us; the launch traced here: 53.6 us
  Pallas kernels  19.5 us (36%)
  starting transfers between devices  12.5 us (23%)
  blocking collectives  9.39 us (17%)
  waiting for transfers between devices  8.35 us (16%)
  local copies, waits for them, and re-layouts  3.13 us (6%)
  between operations  0.79 us (1%)
    all_to_all x1, blocking collectives, shards(): recv = lax.all_to_all(send, 'attn', split_axis=0, concat_axis=0, tiled=True)  9.39 us
    pallas_call x1, Pallas kernels, local_part(): pl.pallas_call(local_kernel, out_shape=(pltpu.VMEM((rows, q_width), jnp.f...  6.98 us
    pallas_call x3, Pallas kernels, project(): pl.pallas_call(functools.partial(chunk_kernel, [len(group) for group in g...  5.85 us
    ppermute x3, starting transfers between devices, shards(): prior.append(lax.ppermute(kv, 'attn', onward))  5.15 us
    ppermute x3, waiting for transfers between devices, shards(): lax.ppermute(piece, 'proj', across(d))  4.89 us
    ppermute x3, starting transfers between devices, shards(): lax.ppermute(piece, 'proj', across(d))  4.61 us
    pallas_call x2, Pallas kernels, attend(): pl.pallas_call(functools.partial(attention_kernel, chunks, wanted), out_s...  3.5 us
    ppermute x3, waiting for transfers between devices, shards(): prior.append(lax.ppermute(kv, 'attn', onward))  3.11 us
  transfers between devices with their start and end apart: 15, of which 6 were waited for; matrix products, arithmetic and copies ran while one was open for 6% of the time, Pallas kernels for 30%

profile of v3, /device:TPU:0, one launch (start us, length us, event | category | flops | bytes accessed | tf_op | source)
XLA Modules:
  0.0 53.6 jit_solution(12952550964907892076)
XLA Ops:
  0.7 0.5 collective-permute-start.1
  1.2 1.1 %slice.33 = bf16[256,1024]{1,0:T(8,128)(2,1)S(1)} slice(bf16[512,1024]{1,0:T(8,128)(2,1)} %x_ref.1), slice={[256:512], [0:1024]} | slice | bytes 1048576 | tf_op jit(solution)/shard_map/slice | solution.py:319
  2.3 2.6 %collective-permute-start = (bf16[256,1024]{1,0:T(8,128)(2,1)S(1)}, bf16[256,1024]{1,0:T(8,128)(2,1)S(1)}, u32[]{:S(2)}, u32[]{:S(2)}) collective-permute-start(bf16[256,1024]{1,0:T(8,128)(2,1)S(1)} %slice.33), channel_id=1, source_target_pairs={{0,2},{1,3},{2,0},{3,1},{4,6},{5,7},{6,4},{7,5},{8,10},{9,11},{10,... | collective-permute-start | bytes 1572872 | tf_op jit(solution)/shard_map/ppermute | solution.py:322
  4.9 1.9 %fusion = (bf16[128,1024]{1,0:T(8,128)(2,1)}, bf16[128,1024]{1,0:T(8,128)(2,1)}) fusion(bf16[512,1024]{1,0:T(8,128)(2,1)} %x_ref.1), kind=kLoop, calls=%fused_computation | loop fusion | bytes 1048576 | tf_op jit(solution)/shard_map/slice | solution.py:319
  6.8 0.1 stack.23.order_ref
  6.9 7.0 %shard_map.86 = (f32[512,1024]{1,0:T(8,128)S(1)}, f32[512,512]{1,0:T(8,128)S(1)}, f32[512,1]{1,0:T(8,128)S(1)}, s32[4,128]{1,0:T(4,128)S(1)}, bf16[2048,512]{1,0...) custom-call(s32[5]{0:T(128)S(1)} %stack.23.order_ref, s32[32]{0:T(128)S(1)} %copy-done.1, bf16[512,1024]{1,0:T(8,128)(2,1)S(1)} %copy-done, ...), custom_call_target="tpu_custom_call" | custom-call | flops 1024 | bytes 1024 | tf_op jit(solution)/shard_map/pallas_call | solution.py:90
  13.9 3.8 %collective-permute-done.refs_0_ = bf16[256,1024]{1,0:T(8,128)(2,1)S(1)} collective-permute-done((bf16[256,1024]{1,0:T(8,128)(2,1)S(1)}, bf16[256,1024]{1,0:T(8,128)(2,1)S(1)}, u32[]{:S(2)}, u32[]{:S(2)}) %collective-permute-start) | collective-permute-done | bytes 524320 | tf_op jit(solution)/shard_map/ppermute | solution.py:322
  17.7 0.1 collective-permute-start.2
  17.8 0.5 collective-permute-start.3
  18.3 0.1 collective-permute-start.4
  18.4 0.4 collective-permute-start.5
  18.8 0.3 collective-permute-done.2.refs_1_
  19.1 2.0 %collective-permute-start.9 = (bf16[128,1024]{1,0:T(8,128)(2,1)S(1)}, bf16[128,1024]{1,0:T(8,128)(2,1)S(1)}, u32[]{:S(2)}, u32[]{:S(2)}) collective-permute-start(bf16[128,1024]{1,0:T(8,128)(2,1)S(1)} %copy-done.3), channel_id=1, source_target_pairs={{0,2},{1,3},{2,0},{3,1},{4,6},{5,7},{6,4},{7,5},{8,10},{9,11},{10,... | collective-permute-start | bytes 786440 | tf_op jit(solution)/shard_map/ppermute | solution.py:322
  21.1 2.5 %shard_map.87 = (bf16[256,512]{1,0:T(8,128)(2,1)S(1)}, bf16[256,1024]{1,0:T(8,128)(2,1)S(1)}) custom-call(s32[5]{0:T(128)S(1)} %stack.23.order_ref, bf16[256,1024]{1,0:T(8,128)(2,1)S(1)} %collective-permute-done.refs_0_, bf16[64,1024]{1,0:T(8,128)(2,1)S(1)} %collective-permute-done.2.refs_1_, bf16[64,1024]{1,0:T(8,128)(2,1)S(1)} %collective-permute-done.3.refs_2_, ...), custom_call_target="tpu_custom_call" | custom-call | flops 1024 | bytes 1024 | tf_op jit(solution)/shard_map/pallas_call | solution.py:133
  23.7 0.1 collective-permute-start.7
  23.8 0.5 collective-permute-start.8
  24.3 1.6 %collective-permute-start.12 = (bf16[256,512]{1,0:T(8,128)(2,1)S(1)}, bf16[256,512]{1,0:T(8,128)(2,1)S(1)}, u32[]{:S(2)}, u32[]{:S(2)}) collective-permute-start(bf16[256,512]{1,0:T(8,128)(2,1)S(1)} %get-tuple-element.44.refs_3_), channel_id=1, source_target_pairs={{0,4},{4,8},{8,12},{12,16},{16,20},{20,24},{24,28},{28,0},{1,5},{5... | collective-permute-start | bytes 786440 | tf_op jit(solution)/shard_map/ppermute | solution.py:351
  25.9 1.7 %shard_map.88 = (bf16[128,512]{1,0:T(8,128)(2,1)S(1)}, bf16[128,1024]{1,0:T(8,128)(2,1)S(1)}) custom-call(s32[5]{0:T(128)S(1)} %stack.23.order_ref, bf16[128,1024]{1,0:T(8,128)(2,1)S(1)} %collective-permute-done.6.refs_0_, bf16[64,1024]{1,0:T(8,128)(2,1)S(1)} %collective-permute-done.7.refs_1_, bf16[64,1024]{1,0:T(8,128)(2,1)S(1)} %collective-permute-done.8.refs_2_, ...), custom_call_target="tpu_custom_call" | custom-call | flops 1024 | bytes 1024 | tf_op jit(solution)/shard_map/pallas_call | solution.py:133
  27.5 1.1 %collective-permute-done.9.refs_0_ = bf16[128,1024]{1,0:T(8,128)(2,1)S(1)} collective-permute-done((bf16[128,1024]{1,0:T(8,128)(2,1)S(1)}, bf16[128,1024]{1,0:T(8,128)(2,1)S(1)}, u32[]{:S(2)}, u32[]{:S(2)}) %collective-permute-start.9) | collective-permute-done | bytes 262176 | tf_op jit(solution)/shard_map/ppermute | solution.py:322
  28.7 0.1 collective-permute-start.10
  28.7 0.5 collective-permute-start.11
  29.2 1.8 %collective-permute-start.13 = (bf16[128,512]{1,0:T(8,128)(2,1)S(1)}, bf16[128,512]{1,0:T(8,128)(2,1)S(1)}, u32[]{:S(2)}, u32[]{:S(2)}) collective-permute-start(bf16[128,512]{1,0:T(8,128)(2,1)S(1)} %get-tuple-element.45.refs_4_), channel_id=1, source_target_pairs={{0,4},{4,8},{8,12},{12,16},{16,20},{20,24},{24,28},{28,0},{1,5},{5... | collective-permute-start | bytes 393224 | tf_op jit(solution)/shard_map/ppermute | solution.py:351
  31.0 1.6 %shard_map.89 = (bf16[128,512]{1,0:T(8,128)(2,1)S(1)}, bf16[128,1024]{1,0:T(8,128)(2,1)S(1)}) custom-call(s32[5]{0:T(128)S(1)} %stack.23.order_ref, bf16[128,1024]{1,0:T(8,128)(2,1)S(1)} %collective-permute-done.9.refs_0_, bf16[64,1024]{1,0:T(8,128)(2,1)S(1)} %collective-permute-done.10.refs_1_, bf16[64,1024]{1,0:T(8,128)(2,1)S(1)} %collective-permute-done.11.refs_2_, ...), custom_call_target="tpu_custom_call" | custom-call | flops 1024 | bytes 1024 | tf_op jit(solution)/shard_map/pallas_call | solution.py:133
  32.7 1.8 %collective-permute-start.14 = (bf16[128,512]{1,0:T(8,128)(2,1)S(1)}, bf16[128,512]{1,0:T(8,128)(2,1)S(1)}, u32[]{:S(2)}, u32[]{:S(2)}) collective-permute-start(bf16[128,512]{1,0:T(8,128)(2,1)S(1)} %get-tuple-element.46.refs_5_), channel_id=1, source_target_pairs={{0,4},{4,8},{8,12},{12,16},{16,20},{20,24},{24,28},{28,0},{1,5},{5... | collective-permute-start | bytes 393224 | tf_op jit(solution)/shard_map/ppermute | solution.py:351
  34.5 1.4 %collective-permute-done.12.refs_6_ = bf16[256,512]{1,0:T(8,128)(2,1)S(1)} collective-permute-done((bf16[256,512]{1,0:T(8,128)(2,1)S(1)}, bf16[256,512]{1,0:T(8,128)(2,1)S(1)}, u32[]{:S(2)}, u32[]{:S(2)}) %collective-permute-start.12) | collective-permute-done | bytes 262176 | tf_op jit(solution)/shard_map/ppermute | solution.py:351
  35.9 2.2 %shard_map.91 = (bf16[256,1024]{1,0:T(8,128)(2,1)S(1)}, f32[2,8,128]{2,1,0:T(8,128)S(1)}) custom-call(bf16[256,1024]{1,0:T(8,128)(2,1)S(1)} %get-tuple-element.41.refs_0_, bf16[128,1024]{1,0:T(8,128)(2,1)S(1)} %get-tuple-element.42.refs_1_, bf16[128,1024]{1,0:T(8,128)(2,1)S(1)} %get-tuple-element.43.refs_2_, bf16[256,512]{1,0:T(8,128)(2,1)S(1)} %get-tuple-element.44.refs_3_, ...), custom_call_target="tpu_custom_call" | custom-call | flops 1024 | bytes 1024 | tf_op jit(solution)/shard_map/pallas_call | solution.py:358
  38.1 0.2 collective-permute-done.13.refs_7_
  38.3 1.3 %shard_map.90 = (bf16[128,1024]{1,0:T(8,128)(2,1)S(1)}, f32[1,8,128]{2,1,0:T(8,128)S(1)}) custom-call(bf16[256,1024]{1,0:T(8,128)(2,1)S(1)} %get-tuple-element.41.refs_0_, bf16[128,1024]{1,0:T(8,128)(2,1)S(1)} %get-tuple-element.42.refs_1_, bf16[128,1024]{1,0:T(8,128)(2,1)S(1)} %get-tuple-element.43.refs_2_, bf16[256,512]{1,0:T(8,128)(2,1)S(1)} %get-tuple-element.44.refs_3_, ...), custom_call_target="tpu_custom_call" | custom-call | flops 1024 | bytes 1024 | tf_op jit(solution)/shard_map/pallas_call | solution.py:358
  39.6 1.5 %collective-permute-done.14.refs_8_ = bf16[128,512]{1,0:T(8,128)(2,1)S(1)} collective-permute-done((bf16[128,512]{1,0:T(8,128)(2,1)S(1)}, bf16[128,512]{1,0:T(8,128)(2,1)S(1)}, u32[]{:S(2)}, u32[]{:S(2)}) %collective-permute-start.14) | collective-permute-done | bytes 131104 | tf_op jit(solution)/shard_map/ppermute | solution.py:351
  41.1 2.5 %shard_map.92 = (bf16[512,1024]{1,0:T(8,128)(2,1)}, bf16[8,8,128]{2,1,0:T(8,128)(2,1)S(1)}) custom-call(s32[4]{0:T(128)S(1)} %copy-done.2, bf16[256,1024]{1,0:T(8,128)(2,1)S(1)} %get-tuple-element.41.refs_0_, bf16[128,1024]{1,0:T(8,128)(2,1)S(1)} %get-tuple-element.42.refs_1_, bf16[128,1024]{1,0:T(8,128)(2,1)S(1)} %get-tuple-element.43.refs_2_, ...), custom_call_target="tpu_custom_call" | custom-call | flops 1024 | bytes 1024 | tf_op jit(solution)/shard_map/pallas_call | solution.py:372
  43.6 9.4 %all_to_all.5.recv_ref = bf16[8,8,128]{2,1,0:T(8,128)(2,1)S(1)} all-to-all(bf16[8,8,128]{2,1,0:T(8,128)(2,1)S(1)} %get-tuple-element.53), channel_id=1, replica_groups=mesh['attn'=8,'proj'=4] {'attn'}, dimensions={0} | all-to-all | bytes 32768 | tf_op jit(solution)/shard_map/all_to_all | solution.py:384
  53.0 0.6 %shard_map.93 = f32[4,8,128]{2,1,0:T(8,128)} custom-call(bf16[8,8,128]{2,1,0:T(8,128)(2,1)S(1)} %all_to_all.5.recv_ref), custom_call_target="tpu_custom_call" | custom-call | tf_op jit(solution)/shard_map/pallas_call | solution.py:385
  (24 shorter events, 0.1 us)
Async XLA Ops:
  0.6 6.3 %copy-start = (bf16[512,1024]{1,0:T(8,128)(2,1)S(1)}, bf16[512,1024]{1,0:T(8,128)(2,1)}, u32[]{:S(2)}) copy-start(bf16[512,1024]{1,0:T(8,128)(2,1)} %x_ref.1) | copy-start | bytes 3145732
  0.6 6.1 %copy-start.4 = (f32[4096]{0:T(1024)S(1)}, f32[4096]{0:T(1024)}, u32[]{:S(2)}) copy-start(f32[4096]{0:T(1024)} %param.8) | copy-start | bytes 49156
  0.7 6.2 %copy-start.1 = (s32[32]{0:T(128)S(1)}, s32[32]{0:T(128)}, u32[]{:S(2)}) copy-start(s32[32]{0:T(128)} %docs_ref.1) | copy-start | bytes 388
  0.7 6.2 %collective-permute-start.1 = (bf16[512,1024]{1,0:T(8,128)(2,1)}, bf16[512,1024]{1,0:T(8,128)(2,1)S(1)}, u32[]{:S(2)}, u32[]{:S(2)}) collective-permute-start(bf16[512,1024]{1,0:T(8,128)(2,1)} %x_ref.1), channel_id=1, source_target_pairs={{0,1},{1,0},{2,3},{3,2},{4,5},{5,4},{6,7},{7,6},{8,9},{9,8},{10,11... | collective-permute-start | bytes 3145736 | tf_op jit(solution)/shard_map/ppermute | solution.py:323
  2.3 15.4 %collective-permute-start = (bf16[256,1024]{1,0:T(8,128)(2,1)S(1)}, bf16[256,1024]{1,0:T(8,128)(2,1)S(1)}, u32[]{:S(2)}, u32[]{:S(2)}) collective-permute-start(bf16[256,1024]{1,0:T(8,128)(2,1)S(1)} %slice.33), channel_id=1, source_target_pairs={{0,2},{1,3},{2,0},{3,1},{4,6},{5,7},{6,4},{7,5},{8,10},{9,11},{10,... | collective-permute-start | bytes 1572872 | tf_op jit(solution)/shard_map/ppermute | solution.py:322
  6.8 16.9 %collective-permute-start.6 = (bf16[128,1024]{1,0:T(8,128)(2,1)}, bf16[128,1024]{1,0:T(8,128)(2,1)S(1)}, u32[]{:S(2)}, u32[]{:S(2)}) collective-permute-start(bf16[128,1024]{1,0:T(8,128)(2,1)} %get-tuple-element.55), channel_id=1, source_target_pairs={{0,2},{1,3},{2,0},{3,1},{4,6},{5,7},{6,4},{7,5},{8,10},{9,11},{10,... | collective-permute-start | bytes 786440 | tf_op jit(solution)/shard_map/ppermute | solution.py:322
  6.9 12.3 %copy-start.3 = (bf16[128,1024]{1,0:T(8,128)(2,1)S(1)}, bf16[128,1024]{1,0:T(8,128)(2,1)}, u32[]{:S(2)}) copy-start(bf16[128,1024]{1,0:T(8,128)(2,1)} %get-tuple-element.54) | copy-start | bytes 786436
  17.7 1.4 %collective-permute-start.2 = (bf16[64,1024]{1,0:T(8,128)(2,1)S(1)}, bf16[64,1024]{1,0:T(8,128)(2,1)S(1)}, u32[]{:S(2)}, u32[]{:S(2)}) collective-permute-start(bf16[64,1024]{1,0:T(8,128)(2,1)S(1)} %get-tuple-element.59), channel_id=1, source_target_pairs={{0,1},{1,0},{2,3},{3,2},{4,5},{5,4},{6,7},{7,6},{8,9},{9,8},{10,11... | collective-permute-start | bytes 393224 | tf_op jit(solution)/shard_map/ppermute | solution.py:348
  17.8 3.3 %collective-permute-start.3 = (bf16[64,1024]{1,0:T(8,128)(2,1)S(1)}, bf16[64,1024]{1,0:T(8,128)(2,1)S(1)}, u32[]{:S(2)}, u32[]{:S(2)}) collective-permute-start(bf16[64,1024]{1,0:T(8,128)(2,1)S(1)} %get-tuple-element.58), channel_id=1, source_target_pairs={{0,1},{1,0},{2,3},{3,2},{4,5},{5,4},{6,7},{7,6},{8,9},{9,8},{10,11... | collective-permute-start | bytes 393224 | tf_op jit(solution)/shard_map/ppermute | solution.py:348
  18.3 2.8 %collective-permute-start.4 = (bf16[64,1024]{1,0:T(8,128)(2,1)S(1)}, bf16[64,1024]{1,0:T(8,128)(2,1)S(1)}, u32[]{:S(2)}, u32[]{:S(2)}) collective-permute-start(bf16[64,1024]{1,0:T(8,128)(2,1)S(1)} %get-tuple-element.57), channel_id=1, source_target_pairs={{0,1},{1,0},{2,3},{3,2},{4,5},{5,4},{6,7},{7,6},{8,9},{9,8},{10,11... | collective-permute-start | bytes 393224 | tf_op jit(solution)/shard_map/ppermute | solution.py:348
  18.4 2.7 %collective-permute-start.5 = (bf16[64,1024]{1,0:T(8,128)(2,1)S(1)}, bf16[64,1024]{1,0:T(8,128)(2,1)S(1)}, u32[]{:S(2)}, u32[]{:S(2)}) collective-permute-start(bf16[64,1024]{1,0:T(8,128)(2,1)S(1)} %get-tuple-element.56), channel_id=1, source_target_pairs={{0,1},{1,0},{2,3},{3,2},{4,5},{5,4},{6,7},{7,6},{8,9},{9,8},{10,11... | collective-permute-start | bytes 393224 | tf_op jit(solution)/shard_map/ppermute | solution.py:348
  19.1 9.5 %collective-permute-start.9 = (bf16[128,1024]{1,0:T(8,128)(2,1)S(1)}, bf16[128,1024]{1,0:T(8,128)(2,1)S(1)}, u32[]{:S(2)}, u32[]{:S(2)}) collective-permute-start(bf16[128,1024]{1,0:T(8,128)(2,1)S(1)} %copy-done.3), channel_id=1, source_target_pairs={{0,2},{1,3},{2,0},{3,1},{4,6},{5,7},{6,4},{7,5},{8,10},{9,11},{10,... | collective-permute-start | bytes 786440 | tf_op jit(solution)/shard_map/ppermute | solution.py:322
  23.7 2.2 %collective-permute-start.7 = (bf16[64,1024]{1,0:T(8,128)(2,1)S(1)}, bf16[64,1024]{1,0:T(8,128)(2,1)S(1)}, u32[]{:S(2)}, u32[]{:S(2)}) collective-permute-start(bf16[64,1024]{1,0:T(8,128)(2,1)S(1)} %get-tuple-element.63), channel_id=1, source_target_pairs={{0,1},{1,0},{2,3},{3,2},{4,5},{5,4},{6,7},{7,6},{8,9},{9,8},{10,11... | collective-permute-start | bytes 393224 | tf_op jit(solution)/shard_map/ppermute | solution.py:348
  23.8 2.1 %collective-permute-start.8 = (bf16[64,1024]{1,0:T(8,128)(2,1)S(1)}, bf16[64,1024]{1,0:T(8,128)(2,1)S(1)}, u32[]{:S(2)}, u32[]{:S(2)}) collective-permute-start(bf16[64,1024]{1,0:T(8,128)(2,1)S(1)} %get-tuple-element.62), channel_id=1, source_target_pairs={{0,1},{1,0},{2,3},{3,2},{4,5},{5,4},{6,7},{7,6},{8,9},{9,8},{10,11... | collective-permute-start | bytes 393224 | tf_op jit(solution)/shard_map/ppermute | solution.py:348
  24.3 11.6 %collective-permute-start.12 = (bf16[256,512]{1,0:T(8,128)(2,1)S(1)}, bf16[256,512]{1,0:T(8,128)(2,1)S(1)}, u32[]{:S(2)}, u32[]{:S(2)}) collective-permute-start(bf16[256,512]{1,0:T(8,128)(2,1)S(1)} %get-tuple-element.44.refs_3_), channel_id=1, source_target_pairs={{0,4},{4,8},{8,12},{12,16},{16,20},{20,24},{24,28},{28,0},{1,5},{5... | collective-permute-start | bytes 786440 | tf_op jit(solution)/shard_map/ppermute | solution.py:351
  28.7 2.4 %collective-permute-start.10 = (bf16[64,1024]{1,0:T(8,128)(2,1)S(1)}, bf16[64,1024]{1,0:T(8,128)(2,1)S(1)}, u32[]{:S(2)}, u32[]{:S(2)}) collective-permute-start(bf16[64,1024]{1,0:T(8,128)(2,1)S(1)} %get-tuple-element.61), channel_id=1, source_target_pairs={{0,1},{1,0},{2,3},{3,2},{4,5},{5,4},{6,7},{7,6},{8,9},{9,8},{10,11... | collective-permute-start | bytes 393224 | tf_op jit(solution)/shard_map/ppermute | solution.py:348
  28.7 2.3 %collective-permute-start.11 = (bf16[64,1024]{1,0:T(8,128)(2,1)S(1)}, bf16[64,1024]{1,0:T(8,128)(2,1)S(1)}, u32[]{:S(2)}, u32[]{:S(2)}) collective-permute-start(bf16[64,1024]{1,0:T(8,128)(2,1)S(1)} %get-tuple-element.60), channel_id=1, source_target_pairs={{0,1},{1,0},{2,3},{3,2},{4,5},{5,4},{6,7},{7,6},{8,9},{9,8},{10,11... | collective-permute-start | bytes 393224 | tf_op jit(solution)/shard_map/ppermute | solution.py:348
  29.2 9.1 %collective-permute-start.13 = (bf16[128,512]{1,0:T(8,128)(2,1)S(1)}, bf16[128,512]{1,0:T(8,128)(2,1)S(1)}, u32[]{:S(2)}, u32[]{:S(2)}) collective-permute-start(bf16[128,512]{1,0:T(8,128)(2,1)S(1)} %get-tuple-element.45.refs_4_), channel_id=1, source_target_pairs={{0,4},{4,8},{8,12},{12,16},{16,20},{20,24},{24,28},{28,0},{1,5},{5... | collective-permute-start | bytes 393224 | tf_op jit(solution)/shard_map/ppermute | solution.py:351
  32.7 8.4 %copy-start.2 = (s32[4]{0:T(128)S(1)}, s32[4]{0:T(128)}, u32[]{:S(2)}) copy-start(s32[4]{0:T(128)} %server_ref.1) | copy-start | bytes 52
  32.7 8.4 %collective-permute-start.14 = (bf16[128,512]{1,0:T(8,128)(2,1)S(1)}, bf16[128,512]{1,0:T(8,128)(2,1)S(1)}, u32[]{:S(2)}, u32[]{:S(2)}) collective-permute-start(bf16[128,512]{1,0:T(8,128)(2,1)S(1)} %get-tuple-element.46.refs_5_), channel_id=1, source_target_pairs={{0,4},{4,8},{8,12},{12,16},{16,20},{20,24},{24,28},{28,0},{1,5},{5... | collective-permute-start | bytes 393224 | tf_op jit(solution)/shard_map/ppermute | solution.py:351

commit v4 on v3

v4 whole, which is shorter than its diff:
```python
import functools
import math

import jax
import jax.numpy as jnp
from jax import lax
from jax.experimental import pallas as pl
from jax.experimental.pallas import tpu as pltpu
from jax.sharding import PartitionSpec as P

HEAD_SIZE = 128
QUERY_BLOCK_ROWS = 128
CORES = 2

masked_value = -1e30
norm_eps = 1e-05
score_scale = 1.0 / HEAD_SIZE**0.5
log2_scale = score_scale * math.log2(math.e)

VMEM = pl.BlockSpec(memory_space=pltpu.VMEM)
SMEM = pl.BlockSpec(memory_space=pltpu.SMEM)
HBM = pl.BlockSpec(memory_space=pltpu.HBM)


def params(limit=16 << 20):
    return pltpu.CompilerParams(vmem_limit_bytes=limit)


def part_terms(x, gain):
    values = x.astype(jnp.float32)
    scaled = (values * gain).astype(jnp.bfloat16)
    return scaled, jnp.sum(values * values, axis=1, keepdims=True)


def cost():
    return pl.CostEstimate(flops=1 << 10, bytes_accessed=1 << 10, transcendentals=0)


def local_kernel(order_ref, docs_ref, server_ref, x_ref, other_ref, gain_ref, wk, wv, wq, *refs):
    q_ref, kv_ref, sq_ref, bound_ref, route_ref, gain_rest, kv_rest, q_rest, kv_own, q_own, sems = refs
    features, width = x_ref.shape[1], wk.shape[1]

    def fetch(slot, kv_to, q_to, place):
        rows = pl.ds(pl.multiple_of(order_ref[slot] * features, features), features)
        here = pl.ds(place * features, features)
        copies = (
            pltpu.make_async_copy(wk.at[rows, :], kv_to.at[here, pl.ds(0, width)], sems.at[slot, 0]),
            pltpu.make_async_copy(wv.at[rows, :], kv_to.at[here, pl.ds(width, width)], sems.at[slot, 1]),
            pltpu.make_async_copy(wq.at[rows, :], q_to.at[here, :], sems.at[slot, 2]),
        )
        for copy in copies:
            copy.start()
        return copies

    mine = [fetch(slot, kv_own, q_own, slot) for slot in range(CORES)]
    rest = [fetch(CORES + i, kv_rest, q_rest, i) for i in range(q_rest.shape[0] // features)]

    shape = bound_ref.shape
    base = order_ref[order_ref.shape[0] - 1]
    position = lax.broadcasted_iota(jnp.int32, shape, 0) * shape[1] + lax.broadcasted_iota(jnp.int32, shape, 1)
    start = -base
    bounds = jnp.full(shape, start, jnp.int32)
    for d in range(docs_ref.shape[0]):
        bounds = jnp.where(position >= start, start, bounds)
        start = start + docs_ref[d]
    bound_ref[...] = bounds
    for block in range(route_ref.shape[0]):
        route_ref[block] = jnp.full(route_ref.shape[1:], server_ref[block], jnp.int32)
    for i in range(gain_rest.shape[0]):
        gain_rest[i : i + 1, :] = gain_ref[pl.ds(order_ref[CORES + i], 1), :]

    parts = [
        part_terms(ref[...], gain_ref[pl.ds(order_ref[slot], 1), :]) for slot, ref in enumerate((x_ref, other_ref))
    ]
    sq_ref[...] = parts[0][1] + parts[1][1]
    scaled = jnp.concatenate([part[0] for part in parts], axis=1)
    for k, v, _ in mine:
        k.wait()
        v.wait()
    kv_ref[...] = jnp.dot(scaled, kv_own[...], preferred_element_type=jnp.float32)
    for _, _, q in mine:
        q.wait()
    q_ref[...] = jnp.dot(scaled, q_own[...], preferred_element_type=jnp.float32)
    for copies in rest:
        for copy in copies:
            copy.wait()


def local_part(order, docs, block_server, x, other, gains, wk, wv, wq):
    rows, features = x.shape
    q_width, kv_width = wq.shape[1], 2 * wk.shape[1]
    rest = wq.shape[0] - CORES * features
    return pl.pallas_call(
        local_kernel,
        out_shape=(
            pltpu.VMEM((rows, q_width), jnp.float32),
            pltpu.VMEM((rows, kv_width), jnp.float32),
            pltpu.VMEM((rows, 1), jnp.float32),
            pltpu.VMEM((rows // QUERY_BLOCK_ROWS, QUERY_BLOCK_ROWS), jnp.int32),
            pltpu.VMEM((rows // QUERY_BLOCK_ROWS, q_width // HEAD_SIZE, QUERY_BLOCK_ROWS), jnp.int32),
            pltpu.VMEM((rest // features, features), jnp.float32),
            pltpu.VMEM((rest, kv_width), jnp.bfloat16),
            pltpu.VMEM((rest, q_width), jnp.bfloat16),
        ),
        in_specs=[SMEM, SMEM, SMEM, VMEM, VMEM, VMEM, HBM, HBM, HBM],
        out_specs=(VMEM,) * 8,
        scratch_shapes=[
            pltpu.VMEM((CORES * features, kv_width), jnp.bfloat16),
            pltpu.VMEM((CORES * features, q_width), jnp.bfloat16),
            pltpu.SemaphoreType.DMA((wq.shape[0] // features, 3)),
        ],
        compiler_params=params(32 << 20),
        cost_estimate=cost(),
    )(order, docs, block_server, x, other, gains, wk, wv, wq)


def remote_rows(sizes, refs, gain_ref):
    terms = []
    for i, size in enumerate(sizes):
        x = jnp.concatenate([ref[...] for ref in refs[:size]], axis=0)
        refs = refs[size:]
        terms.append(part_terms(x, gain_ref[i : i + 1, :]))
    return jnp.concatenate([x for x, _ in terms], axis=1), sum(square for _, square in terms)


def chunk_kernel(sizes, row, kinds, *refs):
    pieces, (gain_ref, sq_ref, *refs) = refs[: sum(sizes)], refs[sum(sizes) :]
    scaled, squares = remote_rows(sizes, pieces, gain_ref)
    here = slice(row, row + scaled.shape[0])
    features = scaled.shape[1] // len(sizes)
    inverse = lax.rsqrt((sq_ref[here, :] + squares) / (features * (len(sizes) + CORES)) + norm_eps)
    for i, kind in enumerate(kinds):
        w_ref, acc_ref = refs[2 * i : 2 * i + 2]
        total = acc_ref[here, :] + jnp.dot(scaled, w_ref[...], preferred_element_type=jnp.float32)
        factor = inverse * log2_scale if kind == "q" else inverse
        refs[2 * len(kinds) + i][...] = (total * factor).astype(jnp.bfloat16)


def project(rows, row, groups, gains, squares, **sides):
    operands = [piece for group in groups for piece in group] + [gains, squares]
    for side in sides.values():
        operands += side
    return pl.pallas_call(
        functools.partial(chunk_kernel, [len(group) for group in groups], row, tuple(sides)),
        out_shape=tuple(jax.ShapeDtypeStruct((rows, w.shape[1]), jnp.bfloat16) for w, _ in sides.values()),
        in_specs=[VMEM] * len(operands),
        out_specs=(VMEM,) * len(sides),
        compiler_params=params(),
        cost_estimate=cost(),
    )(*operands)


def block_parts(refs, chunks):
    found = {}
    block = QUERY_BLOCK_ROWS
    for i in range(chunks[0][1] // block):
        parts = []
        for ref, (low, high) in zip(refs, chunks):
            first, last = max(low, i * block), min(high, (i + 1) * block)
            if first < last:
                parts.insert(0, (ref, first - low, last - low))
        if sum(last - first for _, first, last in parts) == block:
            found[i] = parts
    return found


def key_bias(bounds, key_starts, row_start):
    rows = QUERY_BLOCK_ROWS
    query_pos = row_start + lax.broadcasted_iota(jnp.int32, (rows, rows), 1)
    bias = []
    for start in key_starts:
        key_pos = start + lax.broadcasted_iota(jnp.int32, (rows, rows), 0)
        ok = key_pos >= bounds
        if start == row_start:
            ok = ok & (key_pos <= query_pos)
        bias.append(jnp.where(ok, 0.0, masked_value))
    return jnp.concatenate(bias, axis=0)


def attend_blocks(wanted, blocks, queries, owns, priors, bounds_ref, outs, lse_refs):
    rows = QUERY_BLOCK_ROWS
    width = owns[wanted[0]][0][0].shape[1] // 2
    kv_heads, group = width // HEAD_SIZE, outs[wanted[0]][0].shape[1] // width
    keys = {
        b: [part for i in range(b, blocks) for part in priors[i]] + [part for i in range(b + 1) for part in owns[i]]
        for b in wanted
    }
    bias = {}
    for b in wanted:
        starts = [(i - blocks) * rows for i in range(b, blocks)] + [i * rows for i in range(b + 1)]
        block_bias = key_bias(bounds_ref[b : b + 1, :], starts, b * rows)
        bias[b] = jnp.concatenate([block_bias] * group, axis=1)
    steps = [(b, n) for b in wanted for n in range(kv_heads)]

    def columns(parts, first):
        return jnp.concatenate([ref[i:j, first : first + HEAD_SIZE] for ref, i, j in parts], axis=0)

    def score(b, n):
        heads = range(n * group, (n + 1) * group)
        stacked = jnp.concatenate([columns(queries[b], h * HEAD_SIZE) for h in heads], axis=0)
        return lax.dot_general(
            columns(keys[b], n * HEAD_SIZE), stacked, (((1,), (1,)), ((), ())), preferred_element_type=jnp.float32
        )

    def weigh(b, scores):
        scores = scores + bias[b]
        highest = jnp.max(scores, axis=0, keepdims=True)
        return highest, jnp.exp2(scores - highest)

    def finish(b, n, highest, weights):
        total = jnp.sum(weights, axis=0, keepdims=True)
        summed = lax.dot_general(
            columns(keys[b], width + n * HEAD_SIZE),
            weights.astype(jnp.bfloat16),
            (((0,), (0,)), ((), ())),
            preferred_element_type=jnp.float32,
        )
        result = (summed / total).astype(jnp.bfloat16)
        lse = (highest + jnp.log2(total)) * math.log(2.0)
        ref, at = outs[b]
        for g in range(group):
            h, part = n * group + g, slice(g * rows, (g + 1) * rows)
            ref[at : at + rows, h * HEAD_SIZE : (h + 1) * HEAD_SIZE] = jnp.transpose(result[:, part])
            lse_refs[b][h : h + 1, :] = lse[:, part]

    scores, pending = score(*steps[0]), None
    for i, (b, n) in enumerate(steps):
        ahead = score(*steps[i + 1]) if i + 1 < len(steps) else None
        highest, weights = weigh(b, scores)
        if pending is not None:
            finish(*pending)
        pending, scores = (b, n, highest, weights), ahead
    finish(*pending)


def attention_refs(chunks, refs):
    count = len(chunks)
    queries = block_parts(refs[:count], chunks)
    owns = block_parts(refs[count : 2 * count], chunks)
    return queries, owns, refs[2 * count :]


def high_attention_kernel(chunks, wanted, *refs):
    queries, owns, (*priors, bounds_ref, out_ref, lse_ref) = attention_refs(chunks, refs)
    priors = block_parts(priors, chunks)
    outs = {b: (out_ref, (b - wanted[0]) * QUERY_BLOCK_ROWS) for b in wanted}
    lses = {b: lse_ref.at[b - wanted[0]] for b in wanted}
    attend_blocks(wanted, chunks[0][1] // QUERY_BLOCK_ROWS, queries, owns, priors, bounds_ref, outs, lses)


def low_attention_kernel(chunks, wanted, *refs):
    queries, owns, (*priors, bounds_ref, above_ref, out_ref, lse_ref, out_hbm, sem) = attention_refs(chunks, refs)
    priors = block_parts(priors, chunks)
    rows = pl.ds((wanted[-1] + 1) * QUERY_BLOCK_ROWS, above_ref.shape[0])
    copy = pltpu.make_async_copy(above_ref, out_hbm.at[rows, :], sem)
    copy.start()
    outs = {b: (out_ref, (b - wanted[0]) * QUERY_BLOCK_ROWS) for b in wanted}
    lses = {b: lse_ref.at[b - wanted[0]] for b in wanted}
    attend_blocks(wanted, chunks[0][1] // QUERY_BLOCK_ROWS, queries, owns, priors, bounds_ref, outs, lses)
    copy.wait()


def last_attention_kernel(chunks, servers, *refs):
    queries, owns, refs = attention_refs(chunks, refs)
    *priors, bounds_ref, route_ref, below_ref, below_lse, above_lse, _, out_hbm, here, send_ref, lse, sem = refs
    priors = block_parts(priors, chunks)
    rows = pl.ds(QUERY_BLOCK_ROWS, below_ref.shape[0])
    copy = pltpu.make_async_copy(below_ref, out_hbm.at[rows, :], sem)
    copy.start()
    attend_blocks([0], chunks[0][1] // QUERY_BLOCK_ROWS, queries, owns, priors, bounds_ref, {0: (here, 0)}, {0: lse})
    lses = [lse[...]] + [ref[i] for ref in (below_lse, above_lse) for i in range(ref.shape[0])]
    for s in range(servers):
        value = jnp.full(lses[0].shape, jnp.inf, jnp.float32)
        for block, rows in enumerate(lses):
            value = jnp.where(route_ref[block] == s, rows, value)
        send_ref[s] = value.astype(jnp.bfloat16)
    copy.wait()


def pick_kernel(blocks, recv_ref, here_ref, _, served_hbm, out_hbm, served, sems):
    here = pltpu.make_async_copy(here_ref, out_hbm.at[pl.ds(0, here_ref.shape[0]), :], sems.at[0])
    here.start()
    shape = recv_ref.shape[1:]
    rank = jnp.zeros(shape, jnp.int32)
    picked = [jnp.zeros(shape, jnp.float32) for _ in range(blocks)]
    for i in range(recv_ref.shape[0]):
        value = recv_ref[i].astype(jnp.float32)
        valid = value < jnp.inf
        for k in range(blocks):
            picked[k] = jnp.where(valid & (rank == k), value, picked[k])
        rank = rank + valid.astype(jnp.int32)
    for k in range(blocks):
        served[k] = picked[k]
    copy = pltpu.make_async_copy(served, served_hbm, sems.at[1])
    copy.start()
    copy.wait()
    here.wait()


def shards(tokens, norm_gain, w_query, w_key, value_matrix, doc_lengths, block_server):
    rows, features = tokens.shape
    width = w_key.shape[1]
    heads = w_query.shape[1] // HEAD_SIZE
    block = QUERY_BLOCK_ROWS
    blocks = rows // block
    servers = lax.axis_size("attn")
    sharers = lax.axis_size("proj")
    chips = sharers // CORES
    me_attn = lax.axis_index("attn")
    me_proj = lax.axis_index("proj")
    sibling = [(i, i ^ 1) for i in range(sharers)]

    def across(distance):
        return [(i, (i + distance * CORES) % sharers) for i in range(sharers)]

    middle = blocks // 2
    chunks = [(middle * block, rows)] + [(i * block, (i + 1) * block) for i in reversed(range(middle))]
    arrived = []
    rest = tokens
    for low, high in chunks:
        piece = rest[low:high]
        if not arrived:
            piece, rest = lax.optimization_barrier((piece, rest))
        arrived.append([lax.ppermute(piece, "proj", across(d)) for d in range(1, chips)])
    other = lax.ppermute(tokens, "proj", sibling)

    order = [me_proj, me_proj ^ 1]
    for d in range(1, chips):
        source = (me_proj + sharers - d * CORES) % sharers
        order += [source, source ^ 1]
    order = jnp.stack([*order, me_attn * rows]).astype(jnp.int32)
    gains = norm_gain.reshape(sharers, features)

    w_key, value_matrix, w_query = [
        pltpu.with_memory_space_constraint(w, pltpu.HBM) for w in (w_key, value_matrix, w_query)
    ]
    q_acc, kv_acc, squares, bounds, routes, gain_rest, wkv_rest, wq_rest = local_part(
        order, doc_lengths, block_server, tokens, other, gains, w_key, value_matrix, w_query
    )

    onward = [(i, (i + 1) % servers) for i in range(servers)]
    own, prior, queries = [], [], []
    tie = kv_acc
    for (low, high), sources in zip(chunks, arrived):
        sources, tie = lax.optimization_barrier((sources, tie))
        cuts = range(0, high - low, 64)
        groups = []
        for piece in sources:
            pieces = [piece[i:j] for i, j in zip(cuts, [*cuts[1:], piece.shape[0]])]
            groups += [[piece], [lax.ppermute(part, "proj", sibling) for part in pieces]]
        rest = (high - low, low, groups, gain_rest, squares)
        if low:
            kv, q = project(*rest, k=(wkv_rest, kv_acc), q=(wq_rest, q_acc))
        else:
            (kv,) = project(*rest, k=(wkv_rest, kv_acc))
            (q,) = project(*rest, q=(wq_rest, q_acc))
        tie = q
        prior.append(lax.ppermute(kv, "attn", onward))
        own.append(kv)
        queries.append(q)

    queries = list(lax.optimization_barrier(tuple(queries)))

    operands = (*queries, *own)
    width = heads * HEAD_SIZE

    def results(count):
        return (
            jax.ShapeDtypeStruct((count * block, width), jnp.bfloat16),
            jax.ShapeDtypeStruct((count, heads, block), jnp.float32),
        )

    whole = jax.ShapeDtypeStruct((rows, width), jnp.bfloat16)
    above, above_lse = pl.pallas_call(
        functools.partial(high_attention_kernel, chunks, list(range(middle, blocks))),
        out_shape=results(blocks - middle),
        in_specs=[VMEM] * (len(operands) + 2),
        out_specs=(VMEM, VMEM),
        compiler_params=params(24 << 20),
        cost_estimate=cost(),
    )(*operands, prior[0], bounds)
    below, below_lse, out = pl.pallas_call(
        functools.partial(low_attention_kernel, chunks, list(range(1, middle))),
        out_shape=(*results(middle - 1), whole),
        in_specs=[VMEM] * (len(operands) + len(prior) + 1),
        out_specs=(VMEM, VMEM, HBM),
        scratch_shapes=[pltpu.SemaphoreType.DMA],
        compiler_params=params(24 << 20),
        cost_estimate=cost(),
    )(*operands, *prior[:-1], bounds, above)
    out, here, send = pl.pallas_call(
        functools.partial(last_attention_kernel, chunks, servers),
        out_shape=(
            whole,
            results(1)[0],
            jax.ShapeDtypeStruct((servers, heads, block), jnp.bfloat16),
        ),
        in_specs=[VMEM] * (len(operands) + len(prior) + 5) + [HBM],
        out_specs=(HBM, VMEM, VMEM),
        scratch_shapes=[pltpu.VMEM((heads, block), jnp.float32), pltpu.SemaphoreType.DMA],
        input_output_aliases={len(operands) + len(prior) + 5: 0},
        compiler_params=params(24 << 20),
        cost_estimate=cost(),
    )(*operands, *prior, bounds, routes, below, below_lse, above_lse, out)
    recv = lax.all_to_all(send, "attn", split_axis=0, concat_axis=0, tiled=True)
    served, out = pl.pallas_call(
        functools.partial(pick_kernel, blocks),
        out_shape=(
            jax.ShapeDtypeStruct((blocks, heads, block), jnp.float32),
            jax.ShapeDtypeStruct((rows, heads * HEAD_SIZE), jnp.bfloat16),
        ),
        in_specs=[VMEM, VMEM, HBM],
        out_specs=(HBM, HBM),
        scratch_shapes=[pltpu.VMEM((blocks, heads, block), jnp.float32), pltpu.SemaphoreType.DMA((2,))],
        input_output_aliases={2: 1},
        compiler_params=params(),
    )(recv, here, out)
    return (out, served)


def solution(mesh):
    return jax.shard_map(
        shards,
        mesh=mesh,
        in_specs=(
            P("attn", "proj"),
            P(),
            P(None, "proj"),
            P(None, "proj"),
            P(None, "proj"),
            P(),
            P("attn"),
        ),
        out_specs=(P("attn", "proj"), P("attn", "proj", None)),
        check_vma=False,
    )
```

time: 53.8 us -> 52.6 us (0.978)
  Pallas kernels: 19.5 us -> 16.5 us
  waiting for transfers between devices: 8.35 us -> 9.94 us
    pallas_call x3 -> x4, Pallas kernels: 5.85 us -> 4.33 us  [project(): pl.pallas_call(functools.partial(chunk_kernel, [len(group) for group in g...]
    pallas_call x1, Pallas kernels: 2.54 us -> 1.19 us  [shards(): pl.pallas_call(functools.partial(last_attention_kernel, chunks, servers),...]
    ppermute x3, waiting for transfers between devices: 3.11 us -> 3.93 us  [shards(): prior.append(lax.ppermute(kv, 'attn', onward))]
    ppermute x3, waiting for transfers between devices: 4.89 us -> 5.66 us  [shards(): lax.ppermute(piece, 'proj', across(d))]
  transfers between devices with their start and end apart: 15 -> 15, of which waited for: 6 -> 7; matrix products, arithmetic and copies ran while one was open for 6% -> 6% of each run, Pallas kernels for 30% -> 28%
where the time goes in v4:
time: 52.6 us; the launch traced here: 52.4 us
  Pallas kernels  16.5 us (31%)
  starting transfers between devices  12.7 us (24%)
  waiting for transfers between devices  9.94 us (19%)
  blocking collectives  9.4 us (18%)
  local copies, waits for them, and re-layouts  3.12 us (6%)
  between operations  0.8 us (2%)
    all_to_all x1, blocking collectives, shards(): recv = lax.all_to_all(send, 'attn', split_axis=0, concat_axis=0, tiled=True)  9.4 us
    pallas_call x1, Pallas kernels, local_part(): pl.pallas_call(local_kernel, out_shape=(pltpu.VMEM((rows, q_width), jnp.f...  7 us
    ppermute x3, waiting for transfers between devices, shards(): lax.ppermute(piece, 'proj', across(d))  5.66 us
    ppermute x3, starting transfers between devices, shards(): prior.append(lax.ppermute(kv, 'attn', onward))  5.34 us
    ppermute x3, starting transfers between devices, shards(): lax.ppermute(piece, 'proj', across(d))  4.61 us
    pallas_call x4, Pallas kernels, project(): pl.pallas_call(functools.partial(chunk_kernel, [len(group) for group in g...  4.33 us
    ppermute x3, waiting for transfers between devices, shards(): prior.append(lax.ppermute(kv, 'attn', onward))  3.93 us
    slice x2, local copies, waits for them, and re-layouts, shards(): piece = rest[low:high]  2.93 us
  transfers between devices with their start and end apart: 15, of which 7 were waited for; matrix products, arithmetic and copies ran while one was open for 6% of the time, Pallas kernels for 28%

profile of v4, /device:TPU:0, one launch (start us, length us, event | category | flops | bytes accessed | tf_op | source)
XLA Modules:
  0.0 52.4 jit_solution(6647959690442202401)
XLA Ops:
  0.7 0.5 collective-permute-start.1
  1.2 1.1 %slice.33 = bf16[256,1024]{1,0:T(8,128)(2,1)S(1)} slice(bf16[512,1024]{1,0:T(8,128)(2,1)} %x_ref.1), slice={[256:512], [0:1024]} | slice | bytes 1048576 | tf_op jit(solution)/shard_map/slice | solution.py:321
  2.3 2.6 %collective-permute-start = (bf16[256,1024]{1,0:T(8,128)(2,1)S(1)}, bf16[256,1024]{1,0:T(8,128)(2,1)S(1)}, u32[]{:S(2)}, u32[]{:S(2)}) collective-permute-start(bf16[256,1024]{1,0:T(8,128)(2,1)S(1)} %slice.33), channel_id=1, source_target_pairs={{0,2},{1,3},{2,0},{3,1},{4,6},{5,7},{6,4},{7,5},{8,10},{9,11},{10,... | collective-permute-start | bytes 1572872 | tf_op jit(solution)/shard_map/ppermute | solution.py:324
  4.9 1.9 %fusion = (bf16[128,1024]{1,0:T(8,128)(2,1)}, bf16[128,1024]{1,0:T(8,128)(2,1)}) fusion(bf16[512,1024]{1,0:T(8,128)(2,1)} %x_ref.1), kind=kLoop, calls=%fused_computation | loop fusion | bytes 1048576 | tf_op jit(solution)/shard_map/slice | solution.py:321
  6.8 0.1 stack.23.order_ref
  6.9 7.0 %shard_map.86 = (f32[512,1024]{1,0:T(8,128)S(1)}, f32[512,512]{1,0:T(8,128)S(1)}, f32[512,1]{1,0:T(8,128)S(1)}, s32[4,128]{1,0:T(4,128)S(1)}, s32[4,8,128]{2,1,0...) custom-call(s32[5]{0:T(128)S(1)} %stack.23.order_ref, ...), custom_call_target="tpu_custom_call" | custom-call | flops 1024 | bytes 1024 | tf_op jit(solution)/shard_map/pallas_call | solution.py:93
  13.9 3.8 %collective-permute-done.refs_0_ = bf16[256,1024]{1,0:T(8,128)(2,1)S(1)} collective-permute-done((bf16[256,1024]{1,0:T(8,128)(2,1)S(1)}, bf16[256,1024]{1,0:T(8,128)(2,1)S(1)}, u32[]{:S(2)}, u32[]{:S(2)}) %collective-permute-start) | collective-permute-done | bytes 524320 | tf_op jit(solution)/shard_map/ppermute | solution.py:324
  17.7 0.1 collective-permute-start.2
  17.8 0.5 collective-permute-start.3
  18.3 0.1 collective-permute-start.4
  18.4 0.4 collective-permute-start.5
  18.8 0.3 collective-permute-done.2.refs_1_
  19.1 2.0 %collective-permute-start.9 = (bf16[128,1024]{1,0:T(8,128)(2,1)S(1)}, bf16[128,1024]{1,0:T(8,128)(2,1)S(1)}, u32[]{:S(2)}, u32[]{:S(2)}) collective-permute-start(bf16[128,1024]{1,0:T(8,128)(2,1)S(1)} %copy-done.3), channel_id=1, source_target_pairs={{0,2},{1,3},{2,0},{3,1},{4,6},{5,7},{6,4},{7,5},{8,10},{9,11},{10,... | collective-permute-start | bytes 786440 | tf_op jit(solution)/shard_map/ppermute | solution.py:324
  21.1 2.0 %shard_map.87 = (bf16[256,512]{1,0:T(8,128)(2,1)S(1)}, bf16[256,1024]{1,0:T(8,128)(2,1)S(1)}) custom-call(bf16[256,1024]{1,0:T(8,128)(2,1)S(1)} %collective-permute-done.refs_0_, bf16[64,1024]{1,0:T(8,128)(2,1)S(1)} %collective-permute-done.2.refs_1_, bf16[64,1024]{1,0:T(8,128)(2,1)S(1)} %collective-permute-done.3.refs_2_, ...), custom_call_target="tpu_custom_call" | custom-call | flops 1024 | bytes 1024 | tf_op jit(solution)/shard_map/pallas_call | solution.py:143
  23.1 0.2 collective-permute-done.6.refs_0_
  23.4 0.5 collective-permute-start.8
  23.9 2.0 %collective-permute-start.12 = (bf16[256,512]{1,0:T(8,128)(2,1)S(1)}, bf16[256,512]{1,0:T(8,128)(2,1)S(1)}, u32[]{:S(2)}, u32[]{:S(2)}) collective-permute-start(bf16[256,512]{1,0:T(8,128)(2,1)S(1)} %get-tuple-element.48.refs_3_), channel_id=1, source_target_pairs={{0,4},{4,8},{8,12},{12,16},{16,20},{20,24},{24,28},{28,0},{1,5},{5... | collective-permute-start | bytes 786440 | tf_op jit(solution)/shard_map/ppermute | solution.py:358
  25.9 1.1 %shard_map.88 = (bf16[128,512]{1,0:T(8,128)(2,1)S(1)}, bf16[128,1024]{1,0:T(8,128)(2,1)S(1)}) custom-call(bf16[128,1024]{1,0:T(8,128)(2,1)S(1)} %collective-permute-done.6.refs_0_, bf16[64,1024]{1,0:T(8,128)(2,1)S(1)} %collective-permute-done.7.refs_1_, bf16[64,1024]{1,0:T(8,128)(2,1)S(1)} %collective-permute-done.8.refs_2_, ...), custom_call_target="tpu_custom_call" | custom-call | flops 1024 | bytes 1024 | tf_op jit(solution)/shard_map/pallas_call | solution.py:143
  27.0 1.7 %collective-permute-done.9.refs_0_ = bf16[128,1024]{1,0:T(8,128)(2,1)S(1)} collective-permute-done((bf16[128,1024]{1,0:T(8,128)(2,1)S(1)}, bf16[128,1024]{1,0:T(8,128)(2,1)S(1)}, u32[]{:S(2)}, u32[]{:S(2)}) %collective-permute-start.9) | collective-permute-done | bytes 262176 | tf_op jit(solution)/shard_map/ppermute | solution.py:324
  28.8 0.5 collective-permute-start.11
  29.3 1.8 %collective-permute-start.13 = (bf16[128,512]{1,0:T(8,128)(2,1)S(1)}, bf16[128,512]{1,0:T(8,128)(2,1)S(1)}, u32[]{:S(2)}, u32[]{:S(2)}) collective-permute-start(bf16[128,512]{1,0:T(8,128)(2,1)S(1)} %get-tuple-element.49.refs_4_), channel_id=1, source_target_pairs={{0,4},{4,8},{8,12},{12,16},{16,20},{20,24},{24,28},{28,0},{1,5},{5... | collective-permute-start | bytes 393224 | tf_op jit(solution)/shard_map/ppermute | solution.py:358
  31.0 0.5 shard_map.90.refs_5_
  31.5 1.6 %collective-permute-start.14 = (bf16[128,512]{1,0:T(8,128)(2,1)S(1)}, bf16[128,512]{1,0:T(8,128)(2,1)S(1)}, u32[]{:S(2)}, u32[]{:S(2)}) collective-permute-start(bf16[128,512]{1,0:T(8,128)(2,1)S(1)} %shard_map.90.refs_5_), channel_id=1, source_target_pairs={{0,4},{4,8},{8,12},{12,16},{16,20},{20,24},{24,28},{28,0},{1,5},{5... | collective-permute-start | bytes 393224 | tf_op jit(solution)/shard_map/ppermute | solution.py:358
  33.1 0.8 %shard_map.89.refs_2_ = bf16[128,1024]{1,0:T(8,128)(2,1)S(1)} custom-call(bf16[128,1024]{1,0:T(8,128)(2,1)S(1)} %collective-permute-done.9.refs_0_, bf16[64,1024]{1,0:T(8,128)(2,1)S(1)} %collective-permute-done.10.refs_1_, bf16[64,1024]{1,0:T(8,128)(2,1)S(1)} %collective-permute-done.11.refs_2_, f32[2,1024]{1,0:T(2,128)S(1)} %get-tuple-element.35.refs_5_.refs_3_, ...), custom_call_target="tpu_custom_call" | custom-call | flops 1024 | bytes 1024 | tf_op jit(solution)/shard_map/pallas_call | solution.py:143
  33.9 1.9 %collective-permute-done.12.refs_6_ = bf16[256,512]{1,0:T(8,128)(2,1)S(1)} collective-permute-done((bf16[256,512]{1,0:T(8,128)(2,1)S(1)}, bf16[256,512]{1,0:T(8,128)(2,1)S(1)}, u32[]{:S(2)}, u32[]{:S(2)}) %collective-permute-start.12) | collective-permute-done | bytes 262176 | tf_op jit(solution)/shard_map/ppermute | solution.py:358
  35.9 2.0 %shard_map.91 = (bf16[256,1024]{1,0:T(8,128)(2,1)S(1)}, f32[2,8,128]{2,1,0:T(8,128)S(1)}) custom-call(bf16[256,1024]{1,0:T(8,128)(2,1)S(1)} %get-tuple-element.45.refs_0_, bf16[128,1024]{1,0:T(8,128)(2,1)S(1)} %get-tuple-element.46.refs_1_, bf16[128,1024]{1,0:T(8,128)(2,1)S(1)} %shard_map.89.refs_2_, bf16[256,512]{1,0:T(8,128)(2,1)S(1)} %get-tuple-element.48.refs_3_, ...), custom_call_target="tpu_custom_call" | custom-call | flops 1024 | bytes 1024 | tf_op jit(solution)/shard_map/pallas_call | solution.py:374
  37.9 0.8 %collective-permute-done.13.refs_7_ = bf16[128,512]{1,0:T(8,128)(2,1)S(1)} collective-permute-done((bf16[128,512]{1,0:T(8,128)(2,1)S(1)}, bf16[128,512]{1,0:T(8,128)(2,1)S(1)}, u32[]{:S(2)}, u32[]{:S(2)}) %collective-permute-start.13) | collective-permute-done | bytes 131104 | tf_op jit(solution)/shard_map/ppermute | solution.py:358
  38.7 1.2 %shard_map.92 = (bf16[128,1024]{1,0:T(8,128)(2,1)S(1)}, f32[1,8,128]{2,1,0:T(8,128)S(1)}, bf16[512,1024]{1,0:T(8,128)(2,1)}) custom-call(bf16[256,1024]{1,0:T(8,128)(2,1)S(1)} %get-tuple-element.45.refs_0_, bf16[128,1024]{1,0:T(8,128)(2,1)S(1)} %get-tuple-element.46.refs_1_, bf16[128,1024]{1,0:T(8,128)(2,1)S(1)} %shard_map.89.refs_2_, ...), custom_call_target="tpu_custom_call" | custom-call | flops 1024 | bytes 1024 | tf_op jit(solution)/shard_map/pallas_call | solution.py:382
  39.9 1.2 %collective-permute-done.14.refs_8_ = bf16[128,512]{1,0:T(8,128)(2,1)S(1)} collective-permute-done((bf16[128,512]{1,0:T(8,128)(2,1)S(1)}, bf16[128,512]{1,0:T(8,128)(2,1)S(1)}, u32[]{:S(2)}, u32[]{:S(2)}) %collective-permute-start.14) | collective-permute-done | bytes 131104 | tf_op jit(solution)/shard_map/ppermute | solution.py:358
  41.1 1.2 %shard_map.93 = (bf16[512,1024]{1,0:T(8,128)(2,1)}, bf16[128,1024]{1,0:T(8,128)(2,1)S(1)}, bf16[8,8,128]{2,1,0:T(8,128)(2,1)S(1)}) custom-call(bf16[256,1024]{1,0:T(8,128)(2,1)S(1)} %get-tuple-element.45.refs_0_, bf16[128,1024]{1,0:T(8,128)(2,1)S(1)} %get-tuple-element.46.refs_1_, ...), custom_call_target="tpu_custom_call", output_to_operand_aliasing={{0}: (14, {})} | custom-call | flops 1024 | bytes 1024 | tf_op jit(solution)/shard_map/pallas_call | solution.py:391
  42.3 9.4 %all_to_all.5.recv_ref = bf16[8,8,128]{2,1,0:T(8,128)(2,1)S(1)} all-to-all(bf16[8,8,128]{2,1,0:T(8,128)(2,1)S(1)} %get-tuple-element.57), channel_id=1, replica_groups=mesh['attn'=8,'proj'=4] {'attn'}, dimensions={0} | all-to-all | bytes 32768 | tf_op jit(solution)/shard_map/all_to_all | solution.py:405
  51.7 0.7 %shard_map.94 = (f32[4,8,128]{2,1,0:T(8,128)}, bf16[512,1024]{1,0:T(8,128)(2,1)}) custom-call(bf16[8,8,128]{2,1,0:T(8,128)(2,1)S(1)} %all_to_all.5.recv_ref, bf16[128,1024]{1,0:T(8,128)(2,1)S(1)} %get-tuple-element.58.here_ref, bf16[512,1024]{1,0:T(8,128)(2,1)} %get-tuple-element.59._), custom_call_target="tpu_custom_call", output_to_operand_aliasing={{1}: (2, {})} | custom-call | tf_op jit(solution)/shard_map/pallas_call | solution.py:406
  (25 shorter events, 0.3 us)
Async XLA Ops:
  0.6 6.3 %copy-start = (bf16[512,1024]{1,0:T(8,128)(2,1)S(1)}, bf16[512,1024]{1,0:T(8,128)(2,1)}, u32[]{:S(2)}) copy-start(bf16[512,1024]{1,0:T(8,128)(2,1)} %x_ref.1) | copy-start | bytes 3145732
  0.6 6.1 %copy-start.4 = (f32[4096]{0:T(1024)S(1)}, f32[4096]{0:T(1024)}, u32[]{:S(2)}) copy-start(f32[4096]{0:T(1024)} %param.8) | copy-start | bytes 49156
  0.7 6.2 %copy-start.1 = (s32[32]{0:T(128)S(1)}, s32[32]{0:T(128)}, u32[]{:S(2)}) copy-start(s32[32]{0:T(128)} %docs_ref.1) | copy-start | bytes 388
  0.7 6.2 %copy-start.2 = (s32[4]{0:T(128)S(1)}, s32[4]{0:T(128)}, u32[]{:S(2)}) copy-start(s32[4]{0:T(128)} %server_ref.1) | copy-start | bytes 52
  0.7 6.2 %collective-permute-start.1 = (bf16[512,1024]{1,0:T(8,128)(2,1)}, bf16[512,1024]{1,0:T(8,128)(2,1)S(1)}, u32[]{:S(2)}, u32[]{:S(2)}) collective-permute-start(bf16[512,1024]{1,0:T(8,128)(2,1)} %x_ref.1), channel_id=1, source_target_pairs={{0,1},{1,0},{2,3},{3,2},{4,5},{5,4},{6,7},{7,6},{8,9},{9,8},{10,11... | collective-permute-start | bytes 3145736 | tf_op jit(solution)/shard_map/ppermute | solution.py:325
  2.3 15.4 %collective-permute-start = (bf16[256,1024]{1,0:T(8,128)(2,1)S(1)}, bf16[256,1024]{1,0:T(8,128)(2,1)S(1)}, u32[]{:S(2)}, u32[]{:S(2)}) collective-permute-start(bf16[256,1024]{1,0:T(8,128)(2,1)S(1)} %slice.33), channel_id=1, source_target_pairs={{0,2},{1,3},{2,0},{3,1},{4,6},{5,7},{6,4},{7,5},{8,10},{9,11},{10,... | collective-permute-start | bytes 1572872 | tf_op jit(solution)/shard_map/ppermute | solution.py:324
  6.8 16.5 %collective-permute-start.6 = (bf16[128,1024]{1,0:T(8,128)(2,1)}, bf16[128,1024]{1,0:T(8,128)(2,1)S(1)}, u32[]{:S(2)}, u32[]{:S(2)}) collective-permute-start(bf16[128,1024]{1,0:T(8,128)(2,1)} %get-tuple-element.63), channel_id=1, source_target_pairs={{0,2},{1,3},{2,0},{3,1},{4,6},{5,7},{6,4},{7,5},{8,10},{9,11},{10,... | collective-permute-start | bytes 786440 | tf_op jit(solution)/shard_map/ppermute | solution.py:324
  6.9 12.3 %copy-start.3 = (bf16[128,1024]{1,0:T(8,128)(2,1)S(1)}, bf16[128,1024]{1,0:T(8,128)(2,1)}, u32[]{:S(2)}) copy-start(bf16[128,1024]{1,0:T(8,128)(2,1)} %get-tuple-element.62) | copy-start | bytes 786436
  17.7 1.4 %collective-permute-start.2 = (bf16[64,1024]{1,0:T(8,128)(2,1)S(1)}, bf16[64,1024]{1,0:T(8,128)(2,1)S(1)}, u32[]{:S(2)}, u32[]{:S(2)}) collective-permute-start(bf16[64,1024]{1,0:T(8,128)(2,1)S(1)} %get-tuple-element.67), channel_id=1, source_target_pairs={{0,1},{1,0},{2,3},{3,2},{4,5},{5,4},{6,7},{7,6},{8,9},{9,8},{10,11... | collective-permute-start | bytes 393224 | tf_op jit(solution)/shard_map/ppermute | solution.py:350
  17.8 3.3 %collective-permute-start.3 = (bf16[64,1024]{1,0:T(8,128)(2,1)S(1)}, bf16[64,1024]{1,0:T(8,128)(2,1)S(1)}, u32[]{:S(2)}, u32[]{:S(2)}) collective-permute-start(bf16[64,1024]{1,0:T(8,128)(2,1)S(1)} %get-tuple-element.66), channel_id=1, source_target_pairs={{0,1},{1,0},{2,3},{3,2},{4,5},{5,4},{6,7},{7,6},{8,9},{9,8},{10,11... | collective-permute-start | bytes 393224 | tf_op jit(solution)/shard_map/ppermute | solution.py:350
  18.3 2.8 %collective-permute-start.4 = (bf16[64,1024]{1,0:T(8,128)(2,1)S(1)}, bf16[64,1024]{1,0:T(8,128)(2,1)S(1)}, u32[]{:S(2)}, u32[]{:S(2)}) collective-permute-start(bf16[64,1024]{1,0:T(8,128)(2,1)S(1)} %get-tuple-element.65), channel_id=1, source_target_pairs={{0,1},{1,0},{2,3},{3,2},{4,5},{5,4},{6,7},{7,6},{8,9},{9,8},{10,11... | collective-permute-start | bytes 393224 | tf_op jit(solution)/shard_map/ppermute | solution.py:350
  18.4 2.7 %collective-permute-start.5 = (bf16[64,1024]{1,0:T(8,128)(2,1)S(1)}, bf16[64,1024]{1,0:T(8,128)(2,1)S(1)}, u32[]{:S(2)}, u32[]{:S(2)}) collective-permute-start(bf16[64,1024]{1,0:T(8,128)(2,1)S(1)} %get-tuple-element.64), channel_id=1, source_target_pairs={{0,1},{1,0},{2,3},{3,2},{4,5},{5,4},{6,7},{7,6},{8,9},{9,8},{10,11... | collective-permute-start | bytes 393224 | tf_op jit(solution)/shard_map/ppermute | solution.py:350
  19.1 9.5 %collective-permute-start.9 = (bf16[128,1024]{1,0:T(8,128)(2,1)S(1)}, bf16[128,1024]{1,0:T(8,128)(2,1)S(1)}, u32[]{:S(2)}, u32[]{:S(2)}) collective-permute-start(bf16[128,1024]{1,0:T(8,128)(2,1)S(1)} %copy-done.3), channel_id=1, source_target_pairs={{0,2},{1,3},{2,0},{3,1},{4,6},{5,7},{6,4},{7,5},{8,10},{9,11},{10,... | collective-permute-start | bytes 786440 | tf_op jit(solution)/shard_map/ppermute | solution.py:324
  23.3 2.6 %collective-permute-start.7 = (bf16[64,1024]{1,0:T(8,128)(2,1)S(1)}, bf16[64,1024]{1,0:T(8,128)(2,1)S(1)}, u32[]{:S(2)}, u32[]{:S(2)}) collective-permute-start(bf16[64,1024]{1,0:T(8,128)(2,1)S(1)} %get-tuple-element.71), channel_id=1, source_target_pairs={{0,1},{1,0},{2,3},{3,2},{4,5},{5,4},{6,7},{7,6},{8,9},{9,8},{10,11... | collective-permute-start | bytes 393224 | tf_op jit(solution)/shard_map/ppermute | solution.py:350
  23.4 2.5 %collective-permute-start.8 = (bf16[64,1024]{1,0:T(8,128)(2,1)S(1)}, bf16[64,1024]{1,0:T(8,128)(2,1)S(1)}, u32[]{:S(2)}, u32[]{:S(2)}) collective-permute-start(bf16[64,1024]{1,0:T(8,128)(2,1)S(1)} %get-tuple-element.70), channel_id=1, source_target_pairs={{0,1},{1,0},{2,3},{3,2},{4,5},{5,4},{6,7},{7,6},{8,9},{9,8},{10,11... | collective-permute-start | bytes 393224 | tf_op jit(solution)/shard_map/ppermute | solution.py:350
  23.9 12.0 %collective-permute-start.12 = (bf16[256,512]{1,0:T(8,128)(2,1)S(1)}, bf16[256,512]{1,0:T(8,128)(2,1)S(1)}, u32[]{:S(2)}, u32[]{:S(2)}) collective-permute-start(bf16[256,512]{1,0:T(8,128)(2,1)S(1)} %get-tuple-element.48.refs_3_), channel_id=1, source_target_pairs={{0,4},{4,8},{8,12},{12,16},{16,20},{20,24},{24,28},{28,0},{1,5},{5... | collective-permute-start | bytes 786440 | tf_op jit(solution)/shard_map/ppermute | solution.py:358
  28.7 2.4 %collective-permute-start.10 = (bf16[64,1024]{1,0:T(8,128)(2,1)S(1)}, bf16[64,1024]{1,0:T(8,128)(2,1)S(1)}, u32[]{:S(2)}, u32[]{:S(2)}) collective-permute-start(bf16[64,1024]{1,0:T(8,128)(2,1)S(1)} %get-tuple-element.69), channel_id=1, source_target_pairs={{0,1},{1,0},{2,3},{3,2},{4,5},{5,4},{6,7},{7,6},{8,9},{9,8},{10,11... | collective-permute-start | bytes 393224 | tf_op jit(solution)/shard_map/ppermute | solution.py:350
  28.8 2.3 %collective-permute-start.11 = (bf16[64,1024]{1,0:T(8,128)(2,1)S(1)}, bf16[64,1024]{1,0:T(8,128)(2,1)S(1)}, u32[]{:S(2)}, u32[]{:S(2)}) collective-permute-start(bf16[64,1024]{1,0:T(8,128)(2,1)S(1)} %get-tuple-element.68), channel_id=1, source_target_pairs={{0,1},{1,0},{2,3},{3,2},{4,5},{5,4},{6,7},{7,6},{8,9},{9,8},{10,11... | collective-permute-start | bytes 393224 | tf_op jit(solution)/shard_map/ppermute | solution.py:350
  29.3 9.4 %collective-permute-start.13 = (bf16[128,512]{1,0:T(8,128)(2,1)S(1)}, bf16[128,512]{1,0:T(8,128)(2,1)S(1)}, u32[]{:S(2)}, u32[]{:S(2)}) collective-permute-start(bf16[128,512]{1,0:T(8,128)(2,1)S(1)} %get-tuple-element.49.refs_4_), channel_id=1, source_target_pairs={{0,4},{4,8},{8,12},{12,16},{16,20},{20,24},{24,28},{28,0},{1,5},{5... | collective-permute-start | bytes 393224 | tf_op jit(solution)/shard_map/ppermute | solution.py:358
  31.5 9.5 %collective-permute-start.14 = (bf16[128,512]{1,0:T(8,128)(2,1)S(1)}, bf16[128,512]{1,0:T(8,128)(2,1)S(1)}, u32[]{:S(2)}, u32[]{:S(2)}) collective-permute-start(bf16[128,512]{1,0:T(8,128)(2,1)S(1)} %shard_map.90.refs_5_), channel_id=1, source_target_pairs={{0,4},{4,8},{8,12},{12,16},{16,20},{20,24},{24,28},{28,0},{1,5},{5... | collective-permute-start | bytes 393224 | tf_op jit(solution)/shard_map/ppermute | solution.py:358

commit v5 on v4

--- a/solution.py
+++ b/solution.py
@@ -177,17 +177,15 @@
     return jnp.concatenate(bias, axis=0)
 
 
-def attend_blocks(wanted, blocks, queries, owns, priors, bounds_ref, outs, lse_refs):
+def attend_blocks(wanted, blocks, queries, owns, priors, bounds_ref, outs, lse_refs, states=()):
     rows = QUERY_BLOCK_ROWS
     width = owns[wanted[0]][0][0].shape[1] // 2
     kv_heads, group = width // HEAD_SIZE, outs[wanted[0]][0].shape[1] // width
-    keys = {
-        b: [part for i in range(b, blocks) for part in priors[i]] + [part for i in range(b + 1) for part in owns[i]]
-        for b in wanted
-    }
-    bias = {}
+    keys, bias = {}, {}
     for b in wanted:
-        starts = [(i - blocks) * rows for i in range(b, blocks)] + [i * rows for i in range(b + 1)]
+        before = [i for i in range(b, blocks) if i in priors]
+        keys[b] = [part for i in before for part in priors[i]] + [part for i in range(b + 1) for part in owns[i]]
+        starts = [(i - blocks) * rows for i in before] + [i * rows for i in range(b + 1)]
         block_bias = key_bias(bounds_ref[b : b + 1, :], starts, b * rows)
         bias[b] = jnp.concatenate([block_bias] * group, axis=1)
     steps = [(b, n) for b in wanted for n in range(kv_heads)]
@@ -215,6 +213,10 @@
             (((0,), (0,)), ((), ())),
             preferred_element_type=jnp.float32,
         )
+        if b == 0:
+            for ref, value in zip(states, (highest, total, summed)):
+                ref[n] = value
+            return
         result = (summed / total).astype(jnp.bfloat16)
         lse = (highest + jnp.log2(total)) * math.log(2.0)
         ref, at = outs[b]
@@ -249,30 +251,60 @@
 
 
 def low_attention_kernel(chunks, wanted, *refs):
-    queries, owns, (*priors, bounds_ref, above_ref, out_ref, lse_ref, out_hbm, sem) = attention_refs(chunks, refs)
+    queries, owns, refs = attention_refs(chunks, refs)
+    *priors, bounds_ref, above_ref, out_ref, lse_ref, highest_ref, total_ref, summed_ref, out_hbm, sem = refs
+    states = (highest_ref, total_ref, summed_ref)
     priors = block_parts(priors, chunks)
     rows = pl.ds((wanted[-1] + 1) * QUERY_BLOCK_ROWS, above_ref.shape[0])
     copy = pltpu.make_async_copy(above_ref, out_hbm.at[rows, :], sem)
     copy.start()
     outs = {b: (out_ref, (b - wanted[0]) * QUERY_BLOCK_ROWS) for b in wanted}
     lses = {b: lse_ref.at[b - wanted[0]] for b in wanted}
-    attend_blocks(wanted, chunks[0][1] // QUERY_BLOCK_ROWS, queries, owns, priors, bounds_ref, outs, lses)
+    blocks = chunks[0][1] // QUERY_BLOCK_ROWS
+    attend_blocks([*wanted, 0], blocks, queries, owns, priors, bounds_ref, outs, lses, states)
     copy.wait()
 
 
-def last_attention_kernel(chunks, servers, *refs):
-    queries, owns, refs = attention_refs(chunks, refs)
-    *priors, bounds_ref, route_ref, below_ref, below_lse, above_lse, _, out_hbm, here, send_ref, lse, sem = refs
-    priors = block_parts(priors, chunks)
-    rows = pl.ds(QUERY_BLOCK_ROWS, below_ref.shape[0])
-    copy = pltpu.make_async_copy(below_ref, out_hbm.at[rows, :], sem)
+def last_attention_kernel(blocks, servers, q_ref, prior_ref, bounds_ref, *refs):
+    *states, route_ref, below_ref, below_lse, above_lse, _, out_hbm, here, send_ref, lse_ref, sem = refs
+    block = QUERY_BLOCK_ROWS
+    copy = pltpu.make_async_copy(below_ref, out_hbm.at[pl.ds(block, below_ref.shape[0]), :], sem)
     copy.start()
-    attend_blocks([0], chunks[0][1] // QUERY_BLOCK_ROWS, queries, owns, priors, bounds_ref, {0: (here, 0)}, {0: lse})
-    lses = [lse[...]] + [ref[i] for ref in (below_lse, above_lse) for i in range(ref.shape[0])]
+    width = prior_ref.shape[1] // 2
+    group = q_ref.shape[1] // width
+    bias = jnp.concatenate([key_bias(bounds_ref[:1, :], [-blocks * block], 0)] * group, axis=1)
+    for n in range(width // HEAD_SIZE):
+        heads = range(n * group, (n + 1) * group)
+        stacked = jnp.concatenate([q_ref[:, h * HEAD_SIZE : (h + 1) * HEAD_SIZE] for h in heads], axis=0)
+        scores = lax.dot_general(
+            prior_ref[:, n * HEAD_SIZE : (n + 1) * HEAD_SIZE],
+            stacked,
+            (((1,), (1,)), ((), ())),
+            preferred_element_type=jnp.float32,
+        )
+        scores = scores + bias
+        highest, total, summed = (ref[n] for ref in states)
+        top = jnp.maximum(highest, jnp.max(scores, axis=0, keepdims=True))
+        weights = jnp.exp2(scores - top)
+        scale = jnp.exp2(highest - top)
+        total = total * scale + jnp.sum(weights, axis=0, keepdims=True)
+        summed = summed * scale + lax.dot_general(
+            prior_ref[:, width + n * HEAD_SIZE : width + (n + 1) * HEAD_SIZE],
+            weights.astype(jnp.bfloat16),
+            (((0,), (0,)), ((), ())),
+            preferred_element_type=jnp.float32,
+        )
+        result = (summed / total).astype(jnp.bfloat16)
+        lse = (top + jnp.log2(total)) * math.log(2.0)
+        for g, h in enumerate(heads):
+            part = slice(g * block, (g + 1) * block)
+            here[:, h * HEAD_SIZE : (h + 1) * HEAD_SIZE] = jnp.transpose(result[:, part])
+            lse_ref[h : h + 1, :] = lse[:, part]
+    lses = [lse_ref[...]] + [ref[i] for ref in (below_lse, above_lse) for i in range(ref.shape[0])]
     for s in range(servers):
         value = jnp.full(lses[0].shape, jnp.inf, jnp.float32)
-        for block, rows in enumerate(lses):
-            value = jnp.where(route_ref[block] == s, rows, value)
+        for i, rows in enumerate(lses):
+            value = jnp.where(route_ref[i] == s, rows, value)
         send_ref[s] = value.astype(jnp.bfloat16)
     copy.wait()
 
@@ -379,29 +411,32 @@
         compiler_params=params(24 << 20),
         cost_estimate=cost(),
     )(*operands, prior[0], bounds)
-    below, below_lse, out = pl.pallas_call(
+    kv_heads = w_key.shape[1] // HEAD_SIZE
+    lanes = heads // kv_heads * block
+    states = tuple(jax.ShapeDtypeStruct((kv_heads, n, lanes), jnp.float32) for n in (1, 1, HEAD_SIZE))
+    below, below_lse, *states, out = pl.pallas_call(
         functools.partial(low_attention_kernel, chunks, list(range(1, middle))),
-        out_shape=(*results(middle - 1), whole),
+        out_shape=(*results(middle - 1), *states, whole),
         in_specs=[VMEM] * (len(operands) + len(prior) + 1),
-        out_specs=(VMEM, VMEM, HBM),
+        out_specs=(VMEM,) * 5 + (HBM,),
         scratch_shapes=[pltpu.SemaphoreType.DMA],
         compiler_params=params(24 << 20),
         cost_estimate=cost(),
     )(*operands, *prior[:-1], bounds, above)
     out, here, send = pl.pallas_call(
-        functools.partial(last_attention_kernel, chunks, servers),
+        functools.partial(last_attention_kernel, blocks, servers),
         out_shape=(
             whole,
             results(1)[0],
             jax.ShapeDtypeStruct((servers, heads, block), jnp.bfloat16),
         ),
-        in_specs=[VMEM] * (len(operands) + len(prior) + 5) + [HBM],
+        in_specs=[VMEM] * 10 + [HBM],
         out_specs=(HBM, VMEM, VMEM),
         scratch_shapes=[pltpu.VMEM((heads, block), jnp.float32), pltpu.SemaphoreType.DMA],
-        input_output_aliases={len(operands) + len(prior) + 5: 0},
+        input_output_aliases={10: 0},
         compiler_params=params(24 << 20),
         cost_estimate=cost(),
-    )(*operands, *prior, bounds, routes, below, below_lse, above_lse, out)
+    )(queries[-1], prior[-1], bounds, *states, routes, below, below_lse, above_lse, out)
     recv = lax.all_to_all(send, "attn", split_axis=0, concat_axis=0, tiled=True)
     served, out = pl.pallas_call(
         functools.partial(pick_kernel, blocks),

time: 52.6 us -> 52.4 us (level)
  waiting for transfers between devices: 9.94 us -> 9.28 us
    pallas_call x1, Pallas kernels: 1.19 us -> 1.87 us  [shards(): pl.pallas_call(functools.partial(low_attention_kernel, chunks, list(range...]
    ppermute x3, waiting for transfers between devices: 3.93 us -> 3.27 us  [shards(): prior.append(lax.ppermute(kv, 'attn', onward))]
  transfers between devices with their start and end apart: 15 -> 15, of which waited for: 7 -> 7; matrix products, arithmetic and copies ran while one was open for 6% -> 6% of each run, Pallas kernels for 28% -> 29%
where the time goes in v5:
time: 52.4 us; the launch traced here: 52.2 us
  Pallas kernels  16.9 us (32%)
  starting transfers between devices  12.7 us (24%)
  blocking collectives  9.39 us (18%)
  waiting for transfers between devices  9.28 us (18%)
  local copies, waits for them, and re-layouts  3.12 us (6%)
  between operations  0.8 us (2%)
    all_to_all x1, blocking collectives, shards(): recv = lax.all_to_all(send, 'attn', split_axis=0, concat_axis=0, tiled=True)  9.39 us
    pallas_call x1, Pallas kernels, local_part(): pl.pallas_call(local_kernel, out_shape=(pltpu.VMEM((rows, q_width), jnp.f...  7 us
    ppermute x3, waiting for transfers between devices, shards(): lax.ppermute(piece, 'proj', across(d))  5.66 us
    ppermute x3, starting transfers between devices, shards(): prior.append(lax.ppermute(kv, 'attn', onward))  5.34 us
    ppermute x3, starting transfers between devices, shards(): lax.ppermute(piece, 'proj', across(d))  4.61 us
    pallas_call x4, Pallas kernels, project(): pl.pallas_call(functools.partial(chunk_kernel, [len(group) for group in g...  4.31 us
    ppermute x3, waiting for transfers between devices, shards(): prior.append(lax.ppermute(kv, 'attn', onward))  3.27 us
    slice x2, local copies, waits for them, and re-layouts, shards(): piece = rest[low:high]  2.93 us
  transfers between devices with their start and end apart: 15, of which 7 were waited for; matrix products, arithmetic and copies ran while one was open for 6% of the time, Pallas kernels for 29%

profile of v5, /device:TPU:0, one launch (start us, length us, event | category | flops | bytes accessed | tf_op | source)
XLA Modules:
  0.0 52.2 jit_solution(1419853348148151289)
XLA Ops:
  0.7 0.5 collective-permute-start.1
  1.2 1.1 %slice.33 = bf16[256,1024]{1,0:T(8,128)(2,1)S(1)} slice(bf16[512,1024]{1,0:T(8,128)(2,1)} %x_ref.1), slice={[256:512], [0:1024]} | slice | bytes 1048576 | tf_op jit(solution)/shard_map/slice | solution.py:353
  2.3 2.6 %collective-permute-start = (bf16[256,1024]{1,0:T(8,128)(2,1)S(1)}, bf16[256,1024]{1,0:T(8,128)(2,1)S(1)}, u32[]{:S(2)}, u32[]{:S(2)}) collective-permute-start(bf16[256,1024]{1,0:T(8,128)(2,1)S(1)} %slice.33), channel_id=1, source_target_pairs={{0,2},{1,3},{2,0},{3,1},{4,6},{5,7},{6,4},{7,5},{8,10},{9,11},{10,... | collective-permute-start | bytes 1572872 | tf_op jit(solution)/shard_map/ppermute | solution.py:356
  4.9 1.9 %fusion = (bf16[128,1024]{1,0:T(8,128)(2,1)}, bf16[128,1024]{1,0:T(8,128)(2,1)}) fusion(bf16[512,1024]{1,0:T(8,128)(2,1)} %x_ref.1), kind=kLoop, calls=%fused_computation | loop fusion | bytes 1048576 | tf_op jit(solution)/shard_map/slice | solution.py:353
  6.8 0.1 stack.23.order_ref
  6.9 7.0 %shard_map.86 = (f32[512,1024]{1,0:T(8,128)S(1)}, f32[512,512]{1,0:T(8,128)S(1)}, f32[512,1]{1,0:T(8,128)S(1)}, s32[4,128]{1,0:T(4,128)S(1)}, s32[4,8,128]{2,1,0...) custom-call(s32[5]{0:T(128)S(1)} %stack.23.order_ref, ...), custom_call_target="tpu_custom_call" | custom-call | flops 1024 | bytes 1024 | tf_op jit(solution)/shard_map/pallas_call | solution.py:93
  13.9 3.8 %collective-permute-done.refs_0_ = bf16[256,1024]{1,0:T(8,128)(2,1)S(1)} collective-permute-done((bf16[256,1024]{1,0:T(8,128)(2,1)S(1)}, bf16[256,1024]{1,0:T(8,128)(2,1)S(1)}, u32[]{:S(2)}, u32[]{:S(2)}) %collective-permute-start) | collective-permute-done | bytes 524320 | tf_op jit(solution)/shard_map/ppermute | solution.py:356
  17.8 0.5 collective-permute-start.3
  18.3 0.1 collective-permute-start.4
  18.4 0.4 collective-permute-start.5
  18.8 0.3 collective-permute-done.2.refs_1_
  19.1 2.0 %collective-permute-start.9 = (bf16[128,1024]{1,0:T(8,128)(2,1)S(1)}, bf16[128,1024]{1,0:T(8,128)(2,1)S(1)}, u32[]{:S(2)}, u32[]{:S(2)}) collective-permute-start(bf16[128,1024]{1,0:T(8,128)(2,1)S(1)} %copy-done.3), channel_id=1, source_target_pairs={{0,2},{1,3},{2,0},{3,1},{4,6},{5,7},{6,4},{7,5},{8,10},{9,11},{10,... | collective-permute-start | bytes 786440 | tf_op jit(solution)/shard_map/ppermute | solution.py:356
  21.1 2.0 %shard_map.87 = (bf16[256,512]{1,0:T(8,128)(2,1)S(1)}, bf16[256,1024]{1,0:T(8,128)(2,1)S(1)}) custom-call(bf16[256,1024]{1,0:T(8,128)(2,1)S(1)} %collective-permute-done.refs_0_, bf16[64,1024]{1,0:T(8,128)(2,1)S(1)} %collective-permute-done.2.refs_1_, bf16[64,1024]{1,0:T(8,128)(2,1)S(1)} %collective-permute-done.3.refs_2_, ...), custom_call_target="tpu_custom_call" | custom-call | flops 1024 | bytes 1024 | tf_op jit(solution)/shard_map/pallas_call | solution.py:143
  23.1 0.2 collective-permute-done.6.refs_0_
  23.3 0.1 collective-permute-start.7
  23.4 0.5 collective-permute-start.8
  23.9 2.0 %collective-permute-start.13 = (bf16[256,512]{1,0:T(8,128)(2,1)S(1)}, bf16[256,512]{1,0:T(8,128)(2,1)S(1)}, u32[]{:S(2)}, u32[]{:S(2)}) collective-permute-start(bf16[256,512]{1,0:T(8,128)(2,1)S(1)} %get-tuple-element.52.refs_3_), channel_id=1, source_target_pairs={{0,4},{4,8},{8,12},{12,16},{16,20},{20,24},{24,28},{28,0},{1,5},{5... | collective-permute-start | bytes 786440 | tf_op jit(solution)/shard_map/ppermute | solution.py:390
  25.9 1.1 %shard_map.88 = (bf16[128,512]{1,0:T(8,128)(2,1)S(1)}, bf16[128,1024]{1,0:T(8,128)(2,1)S(1)}) custom-call(bf16[128,1024]{1,0:T(8,128)(2,1)S(1)} %collective-permute-done.6.refs_0_, bf16[64,1024]{1,0:T(8,128)(2,1)S(1)} %collective-permute-done.7.refs_1_, bf16[64,1024]{1,0:T(8,128)(2,1)S(1)} %collective-permute-done.8.refs_2_, ...), custom_call_target="tpu_custom_call" | custom-call | flops 1024 | bytes 1024 | tf_op jit(solution)/shard_map/pallas_call | solution.py:143
  27.0 1.7 %collective-permute-done.9.refs_0_ = bf16[128,1024]{1,0:T(8,128)(2,1)S(1)} collective-permute-done((bf16[128,1024]{1,0:T(8,128)(2,1)S(1)}, bf16[128,1024]{1,0:T(8,128)(2,1)S(1)}, u32[]{:S(2)}, u32[]{:S(2)}) %collective-permute-start.9) | collective-permute-done | bytes 262176 | tf_op jit(solution)/shard_map/ppermute | solution.py:356
  28.8 0.5 collective-permute-start.11
  29.3 1.8 %collective-permute-start.14 = (bf16[128,512]{1,0:T(8,128)(2,1)S(1)}, bf16[128,512]{1,0:T(8,128)(2,1)S(1)}, u32[]{:S(2)}, u32[]{:S(2)}) collective-permute-start(bf16[128,512]{1,0:T(8,128)(2,1)S(1)} %get-tuple-element.53.refs_4_), channel_id=1, source_target_pairs={{0,4},{4,8},{8,12},{12,16},{16,20},{20,24},{24,28},{28,0},{1,5},{5... | collective-permute-start | bytes 393224 | tf_op jit(solution)/shard_map/ppermute | solution.py:390
  31.0 0.5 shard_map.90.refs_5_
  31.5 1.6 %collective-permute-start.12 = (bf16[128,512]{1,0:T(8,128)(2,1)S(1)}, bf16[128,512]{1,0:T(8,128)(2,1)S(1)}, u32[]{:S(2)}, u32[]{:S(2)}) collective-permute-start(bf16[128,512]{1,0:T(8,128)(2,1)S(1)} %shard_map.90.refs_5_), channel_id=1, source_target_pairs={{0,4},{4,8},{8,12},{12,16},{16,20},{20,24},{24,28},{28,0},{1,5},{5... | collective-permute-start | bytes 393224 | tf_op jit(solution)/shard_map/ppermute | solution.py:390
  33.1 0.8 %shard_map.89.refs_2_.q_ref = bf16[128,1024]{1,0:T(8,128)(2,1)S(1)} custom-call(bf16[128,1024]{1,0:T(8,128)(2,1)S(1)} %collective-permute-done.9.refs_0_, bf16[64,1024]{1,0:T(8,128)(2,1)S(1)} %collective-permute-done.10.refs_1_, bf16[64,1024]{1,0:T(8,128)(2,1)S(1)} %collective-permute-done.11.refs_2_, f32[2,1024]{1,0:T(2,128)S(1)} %get-tuple-element.38.refs_5_.refs_3_, ...), custom_call_target="tpu_custom_call" | custom-call | flops 1024 | bytes 1024 | tf_op jit(solution)/shard_map/pallas_call | solution.py:143
  33.9 2.0 %collective-permute-done.13.refs_6_ = bf16[256,512]{1,0:T(8,128)(2,1)S(1)} collective-permute-done((bf16[256,512]{1,0:T(8,128)(2,1)S(1)}, bf16[256,512]{1,0:T(8,128)(2,1)S(1)}, u32[]{:S(2)}, u32[]{:S(2)}) %collective-permute-start.13) | collective-permute-done | bytes 262176 | tf_op jit(solution)/shard_map/ppermute | solution.py:390
  35.9 2.0 %shard_map.91 = (bf16[256,1024]{1,0:T(8,128)(2,1)S(1)}, f32[2,8,128]{2,1,0:T(8,128)S(1)}) custom-call(bf16[256,1024]{1,0:T(8,128)(2,1)S(1)} %get-tuple-element.50.refs_0_, bf16[128,1024]{1,0:T(8,128)(2,1)S(1)} %get-tuple-element.51.refs_1_, bf16[128,1024]{1,0:T(8,128)(2,1)S(1)} %shard_map.89.refs_2_.q_ref, bf16[256,512]{1,0:T(8,128)(2,1)S(1)} %get-tuple-element.52.refs_3_, ...), custom_call_target="tpu_custom_call" | custom-call | flops 1024 | bytes 1024 | tf_op jit(solution)/shard_map/pallas_call | solution.py:406
  37.9 0.8 %collective-permute-done.14.refs_7_ = bf16[128,512]{1,0:T(8,128)(2,1)S(1)} collective-permute-done((bf16[128,512]{1,0:T(8,128)(2,1)S(1)}, bf16[128,512]{1,0:T(8,128)(2,1)S(1)}, u32[]{:S(2)}, u32[]{:S(2)}) %collective-permute-start.14) | collective-permute-done | bytes 131104 | tf_op jit(solution)/shard_map/ppermute | solution.py:390
  38.7 1.9 %shard_map.92 = (bf16[128,1024]{1,0:T(8,128)(2,1)S(1)}, f32[1,8,128]{2,1,0:T(8,128)S(1)}, f32[2,1,512]{2,1,0:T(1,128)S(1)}, f32[2,1,512]{2,1,0:T(1,128)S(1)}, f3...) custom-call(bf16[256,1024]{1,0:T(8,128)(2,1)S(1)} %get-tuple-element.50.refs_0_, ...), custom_call_target="tpu_custom_call" | custom-call | flops 1024 | bytes 1024 | tf_op jit(solution)/shard_map/pallas_call | solution.py:417
  40.6 0.5 %collective-permute-done.12.prior_ref = bf16[128,512]{1,0:T(8,128)(2,1)S(1)} collective-permute-done((bf16[128,512]{1,0:T(8,128)(2,1)S(1)}, bf16[128,512]{1,0:T(8,128)(2,1)S(1)}, u32[]{:S(2)}, u32[]{:S(2)}) %collective-permute-start.12) | collective-permute-done | bytes 131104 | tf_op jit(solution)/shard_map/ppermute | solution.py:390
  41.1 1.0 %shard_map.93 = (bf16[512,1024]{1,0:T(8,128)(2,1)}, bf16[128,1024]{1,0:T(8,128)(2,1)S(1)}, bf16[8,8,128]{2,1,0:T(8,128)(2,1)S(1)}) custom-call(bf16[128,1024]{1,0:T(8,128)(2,1)S(1)} %shard_map.89.refs_2_.q_ref, bf16[128,512]{1,0:T(8,128)(2,1)S(1)} %collective-permute-done.12.prior_ref, ...), custom_call_target="tpu_custom_call", output_to_operand_aliasing={{0}: (10, {})} | custom-call | flops 1024 | bytes 1024 | tf_op jit(solution)/shard_map/pallas_call | solution.py:426
  42.1 9.4 %all_to_all.5.recv_ref = bf16[8,8,128]{2,1,0:T(8,128)(2,1)S(1)} all-to-all(bf16[8,8,128]{2,1,0:T(8,128)(2,1)S(1)} %get-tuple-element.63), channel_id=1, replica_groups=mesh['attn'=8,'proj'=4] {'attn'}, dimensions={0} | all-to-all | bytes 32768 | tf_op jit(solution)/shard_map/all_to_all | solution.py:440
  51.5 0.7 %shard_map.94 = (f32[4,8,128]{2,1,0:T(8,128)}, bf16[512,1024]{1,0:T(8,128)(2,1)}) custom-call(bf16[8,8,128]{2,1,0:T(8,128)(2,1)S(1)} %all_to_all.5.recv_ref, bf16[128,1024]{1,0:T(8,128)(2,1)S(1)} %get-tuple-element.64.here_ref, bf16[512,1024]{1,0:T(8,128)(2,1)} %get-tuple-element.65._), custom_call_target="tpu_custom_call", output_to_operand_aliasing={{1}: (2, {})} | custom-call | tf_op jit(solution)/shard_map/pallas_call | solution.py:441
  (25 shorter events, 0.3 us)
Async XLA Ops:
  0.6 6.3 %copy-start = (bf16[512,1024]{1,0:T(8,128)(2,1)S(1)}, bf16[512,1024]{1,0:T(8,128)(2,1)}, u32[]{:S(2)}) copy-start(bf16[512,1024]{1,0:T(8,128)(2,1)} %x_ref.1) | copy-start | bytes 3145732
  0.6 6.1 %copy-start.4 = (f32[4096]{0:T(1024)S(1)}, f32[4096]{0:T(1024)}, u32[]{:S(2)}) copy-start(f32[4096]{0:T(1024)} %param.8) | copy-start | bytes 49156
  0.7 6.2 %copy-start.1 = (s32[32]{0:T(128)S(1)}, s32[32]{0:T(128)}, u32[]{:S(2)}) copy-start(s32[32]{0:T(128)} %docs_ref.1) | copy-start | bytes 388
  0.7 6.2 %copy-start.2 = (s32[4]{0:T(128)S(1)}, s32[4]{0:T(128)}, u32[]{:S(2)}) copy-start(s32[4]{0:T(128)} %server_ref.1) | copy-start | bytes 52
  0.7 6.2 %collective-permute-start.1 = (bf16[512,1024]{1,0:T(8,128)(2,1)}, bf16[512,1024]{1,0:T(8,128)(2,1)S(1)}, u32[]{:S(2)}, u32[]{:S(2)}) collective-permute-start(bf16[512,1024]{1,0:T(8,128)(2,1)} %x_ref.1), channel_id=1, source_target_pairs={{0,1},{1,0},{2,3},{3,2},{4,5},{5,4},{6,7},{7,6},{8,9},{9,8},{10,11... | collective-permute-start | bytes 3145736 | tf_op jit(solution)/shard_map/ppermute | solution.py:357
  2.3 15.4 %collective-permute-start = (bf16[256,1024]{1,0:T(8,128)(2,1)S(1)}, bf16[256,1024]{1,0:T(8,128)(2,1)S(1)}, u32[]{:S(2)}, u32[]{:S(2)}) collective-permute-start(bf16[256,1024]{1,0:T(8,128)(2,1)S(1)} %slice.33), channel_id=1, source_target_pairs={{0,2},{1,3},{2,0},{3,1},{4,6},{5,7},{6,4},{7,5},{8,10},{9,11},{10,... | collective-permute-start | bytes 1572872 | tf_op jit(solution)/shard_map/ppermute | solution.py:356
  6.8 16.5 %collective-permute-start.6 = (bf16[128,1024]{1,0:T(8,128)(2,1)}, bf16[128,1024]{1,0:T(8,128)(2,1)S(1)}, u32[]{:S(2)}, u32[]{:S(2)}) collective-permute-start(bf16[128,1024]{1,0:T(8,128)(2,1)} %get-tuple-element.69), channel_id=1, source_target_pairs={{0,2},{1,3},{2,0},{3,1},{4,6},{5,7},{6,4},{7,5},{8,10},{9,11},{10,... | collective-permute-start | bytes 786440 | tf_op jit(solution)/shard_map/ppermute | solution.py:356
  6.9 12.3 %copy-start.3 = (bf16[128,1024]{1,0:T(8,128)(2,1)S(1)}, bf16[128,1024]{1,0:T(8,128)(2,1)}, u32[]{:S(2)}) copy-start(bf16[128,1024]{1,0:T(8,128)(2,1)} %get-tuple-element.68) | copy-start | bytes 786436
  17.7 1.4 %collective-permute-start.2 = (bf16[64,1024]{1,0:T(8,128)(2,1)S(1)}, bf16[64,1024]{1,0:T(8,128)(2,1)S(1)}, u32[]{:S(2)}, u32[]{:S(2)}) collective-permute-start(bf16[64,1024]{1,0:T(8,128)(2,1)S(1)} %get-tuple-element.73), channel_id=1, source_target_pairs={{0,1},{1,0},{2,3},{3,2},{4,5},{5,4},{6,7},{7,6},{8,9},{9,8},{10,11... | collective-permute-start | bytes 393224 | tf_op jit(solution)/shard_map/ppermute | solution.py:382
  17.8 3.3 %collective-permute-start.3 = (bf16[64,1024]{1,0:T(8,128)(2,1)S(1)}, bf16[64,1024]{1,0:T(8,128)(2,1)S(1)}, u32[]{:S(2)}, u32[]{:S(2)}) collective-permute-start(bf16[64,1024]{1,0:T(8,128)(2,1)S(1)} %get-tuple-element.72), channel_id=1, source_target_pairs={{0,1},{1,0},{2,3},{3,2},{4,5},{5,4},{6,7},{7,6},{8,9},{9,8},{10,11... | collective-permute-start | bytes 393224 | tf_op jit(solution)/shard_map/ppermute | solution.py:382
  18.3 2.8 %collective-permute-start.4 = (bf16[64,1024]{1,0:T(8,128)(2,1)S(1)}, bf16[64,1024]{1,0:T(8,128)(2,1)S(1)}, u32[]{:S(2)}, u32[]{:S(2)}) collective-permute-start(bf16[64,1024]{1,0:T(8,128)(2,1)S(1)} %get-tuple-element.71), channel_id=1, source_target_pairs={{0,1},{1,0},{2,3},{3,2},{4,5},{5,4},{6,7},{7,6},{8,9},{9,8},{10,11... | collective-permute-start | bytes 393224 | tf_op jit(solution)/shard_map/ppermute | solution.py:382
  18.4 2.7 %collective-permute-start.5 = (bf16[64,1024]{1,0:T(8,128)(2,1)S(1)}, bf16[64,1024]{1,0:T(8,128)(2,1)S(1)}, u32[]{:S(2)}, u32[]{:S(2)}) collective-permute-start(bf16[64,1024]{1,0:T(8,128)(2,1)S(1)} %get-tuple-element.70), channel_id=1, source_target_pairs={{0,1},{1,0},{2,3},{3,2},{4,5},{5,4},{6,7},{7,6},{8,9},{9,8},{10,11... | collective-permute-start | bytes 393224 | tf_op jit(solution)/shard_map/ppermute | solution.py:382
  19.1 9.5 %collective-permute-start.9 = (bf16[128,1024]{1,0:T(8,128)(2,1)S(1)}, bf16[128,1024]{1,0:T(8,128)(2,1)S(1)}, u32[]{:S(2)}, u32[]{:S(2)}) collective-permute-start(bf16[128,1024]{1,0:T(8,128)(2,1)S(1)} %copy-done.3), channel_id=1, source_target_pairs={{0,2},{1,3},{2,0},{3,1},{4,6},{5,7},{6,4},{7,5},{8,10},{9,11},{10,... | collective-permute-start | bytes 786440 | tf_op jit(solution)/shard_map/ppermute | solution.py:356
  23.3 2.6 %collective-permute-start.7 = (bf16[64,1024]{1,0:T(8,128)(2,1)S(1)}, bf16[64,1024]{1,0:T(8,128)(2,1)S(1)}, u32[]{:S(2)}, u32[]{:S(2)}) collective-permute-start(bf16[64,1024]{1,0:T(8,128)(2,1)S(1)} %get-tuple-element.77), channel_id=1, source_target_pairs={{0,1},{1,0},{2,3},{3,2},{4,5},{5,4},{6,7},{7,6},{8,9},{9,8},{10,11... | collective-permute-start | bytes 393224 | tf_op jit(solution)/shard_map/ppermute | solution.py:382
  23.4 2.5 %collective-permute-start.8 = (bf16[64,1024]{1,0:T(8,128)(2,1)S(1)}, bf16[64,1024]{1,0:T(8,128)(2,1)S(1)}, u32[]{:S(2)}, u32[]{:S(2)}) collective-permute-start(bf16[64,1024]{1,0:T(8,128)(2,1)S(1)} %get-tuple-element.76), channel_id=1, source_target_pairs={{0,1},{1,0},{2,3},{3,2},{4,5},{5,4},{6,7},{7,6},{8,9},{9,8},{10,11... | collective-permute-start | bytes 393224 | tf_op jit(solution)/shard_map/ppermute | solution.py:382
  23.9 12.0 %collective-permute-start.13 = (bf16[256,512]{1,0:T(8,128)(2,1)S(1)}, bf16[256,512]{1,0:T(8,128)(2,1)S(1)}, u32[]{:S(2)}, u32[]{:S(2)}) collective-permute-start(bf16[256,512]{1,0:T(8,128)(2,1)S(1)} %get-tuple-element.52.refs_3_), channel_id=1, source_target_pairs={{0,4},{4,8},{8,12},{12,16},{16,20},{20,24},{24,28},{28,0},{1,5},{5... | collective-permute-start | bytes 786440 | tf_op jit(solution)/shard_map/ppermute | solution.py:390
  28.7 2.4 %collective-permute-start.10 = (bf16[64,1024]{1,0:T(8,128)(2,1)S(1)}, bf16[64,1024]{1,0:T(8,128)(2,1)S(1)}, u32[]{:S(2)}, u32[]{:S(2)}) collective-permute-start(bf16[64,1024]{1,0:T(8,128)(2,1)S(1)} %get-tuple-element.75), channel_id=1, source_target_pairs={{0,1},{1,0},{2,3},{3,2},{4,5},{5,4},{6,7},{7,6},{8,9},{9,8},{10,11... | collective-permute-start | bytes 393224 | tf_op jit(solution)/shard_map/ppermute | solution.py:382
  28.8 2.3 %collective-permute-start.11 = (bf16[64,1024]{1,0:T(8,128)(2,1)S(1)}, bf16[64,1024]{1,0:T(8,128)(2,1)S(1)}, u32[]{:S(2)}, u32[]{:S(2)}) collective-permute-start(bf16[64,1024]{1,0:T(8,128)(2,1)S(1)} %get-tuple-element.74), channel_id=1, source_target_pairs={{0,1},{1,0},{2,3},{3,2},{4,5},{5,4},{6,7},{7,6},{8,9},{9,8},{10,11... | collective-permute-start | bytes 393224 | tf_op jit(solution)/shard_map/ppermute | solution.py:382
  29.3 9.4 %collective-permute-start.14 = (bf16[128,512]{1,0:T(8,128)(2,1)S(1)}, bf16[128,512]{1,0:T(8,128)(2,1)S(1)}, u32[]{:S(2)}, u32[]{:S(2)}) collective-permute-start(bf16[128,512]{1,0:T(8,128)(2,1)S(1)} %get-tuple-element.53.refs_4_), channel_id=1, source_target_pairs={{0,4},{4,8},{8,12},{12,16},{16,20},{20,24},{24,28},{28,0},{1,5},{5... | collective-permute-start | bytes 393224 | tf_op jit(solution)/shard_map/ppermute | solution.py:390
  31.5 9.6 %collective-permute-start.12 = (bf16[128,512]{1,0:T(8,128)(2,1)S(1)}, bf16[128,512]{1,0:T(8,128)(2,1)S(1)}, u32[]{:S(2)}, u32[]{:S(2)}) collective-permute-start(bf16[128,512]{1,0:T(8,128)(2,1)S(1)} %shard_map.90.refs_5_), channel_id=1, source_target_pairs={{0,4},{4,8},{8,12},{12,16},{16,20},{20,24},{24,28},{28,0},{1,5},{5... | collective-permute-start | bytes 393224 | tf_op jit(solution)/shard_map/ppermute | solution.py:390

commit v6 on v5

--- a/solution.py
+++ b/solution.py
@@ -129,20 +129,19 @@
     here = slice(row, row + scaled.shape[0])
     features = scaled.shape[1] // len(sizes)
     inverse = lax.rsqrt((sq_ref[here, :] + squares) / (features * (len(sizes) + CORES)) + norm_eps)
-    for i, kind in enumerate(kinds):
+    for i in range(kinds):
         w_ref, acc_ref = refs[2 * i : 2 * i + 2]
         total = acc_ref[here, :] + jnp.dot(scaled, w_ref[...], preferred_element_type=jnp.float32)
-        factor = inverse * log2_scale if kind == "q" else inverse
-        refs[2 * len(kinds) + i][...] = (total * factor).astype(jnp.bfloat16)
-
-
-def project(rows, row, groups, gains, squares, **sides):
+        refs[2 * kinds + i][...] = (total * inverse).astype(jnp.bfloat16)
+
+
+def project(rows, row, groups, gains, squares, *sides):
     operands = [piece for group in groups for piece in group] + [gains, squares]
-    for side in sides.values():
+    for side in sides:
         operands += side
     return pl.pallas_call(
-        functools.partial(chunk_kernel, [len(group) for group in groups], row, tuple(sides)),
-        out_shape=tuple(jax.ShapeDtypeStruct((rows, w.shape[1]), jnp.bfloat16) for w, _ in sides.values()),
+        functools.partial(chunk_kernel, [len(group) for group in groups], row, len(sides)),
+        out_shape=tuple(jax.ShapeDtypeStruct((rows, w.shape[1]), jnp.bfloat16) for w, _ in sides),
         in_specs=[VMEM] * len(operands),
         out_specs=(VMEM,) * len(sides),
         compiler_params=params(),
@@ -164,30 +163,29 @@
     return found
 
 
-def key_bias(bounds, key_starts, row_start):
+def score_caps(bounds, key_starts, row_start):
     rows = QUERY_BLOCK_ROWS
     query_pos = row_start + lax.broadcasted_iota(jnp.int32, (rows, rows), 1)
-    bias = []
+    caps = []
     for start in key_starts:
         key_pos = start + lax.broadcasted_iota(jnp.int32, (rows, rows), 0)
         ok = key_pos >= bounds
         if start == row_start:
             ok = ok & (key_pos <= query_pos)
-        bias.append(jnp.where(ok, 0.0, masked_value))
-    return jnp.concatenate(bias, axis=0)
+        caps.append(jnp.where(ok, jnp.inf, masked_value))
+    return jnp.concatenate(caps, axis=0)
 
 
 def attend_blocks(wanted, blocks, queries, owns, priors, bounds_ref, outs, lse_refs, states=()):
     rows = QUERY_BLOCK_ROWS
     width = owns[wanted[0]][0][0].shape[1] // 2
     kv_heads, group = width // HEAD_SIZE, outs[wanted[0]][0].shape[1] // width
-    keys, bias = {}, {}
+    keys, caps = {}, {}
     for b in wanted:
         before = [i for i in range(b, blocks) if i in priors]
         keys[b] = [part for i in before for part in priors[i]] + [part for i in range(b + 1) for part in owns[i]]
         starts = [(i - blocks) * rows for i in before] + [i * rows for i in range(b + 1)]
-        block_bias = key_bias(bounds_ref[b : b + 1, :], starts, b * rows)
-        bias[b] = jnp.concatenate([block_bias] * group, axis=1)
+        caps[b] = jnp.concatenate([score_caps(bounds_ref[b : b + 1, :], starts, b * rows)] * group, axis=1)
     steps = [(b, n) for b in wanted for n in range(kv_heads)]
 
     def columns(parts, first):
@@ -201,9 +199,9 @@
         )
 
     def weigh(b, scores):
-        scores = scores + bias[b]
+        scores = jnp.minimum(scores, caps[b])
         highest = jnp.max(scores, axis=0, keepdims=True)
-        return highest, jnp.exp2(scores - highest)
+        return highest, jnp.exp2((scores - highest) * log2_scale)
 
     def finish(b, n, highest, weights):
         total = jnp.sum(weights, axis=0, keepdims=True)
@@ -218,7 +216,7 @@
                 ref[n] = value
             return
         result = (summed / total).astype(jnp.bfloat16)
-        lse = (highest + jnp.log2(total)) * math.log(2.0)
+        lse = highest * score_scale + jnp.log(total)
         ref, at = outs[b]
         for g in range(group):
             h, part = n * group + g, slice(g * rows, (g + 1) * rows)
@@ -242,18 +240,53 @@
     return queries, owns, refs[2 * count :]
 
 
+def merge_keys(n, prior_parts, query_parts, caps, states):
+    width = prior_parts[0][0].shape[1] // 2
+    group = query_parts[0][0].shape[1] // width
+
+    def columns(parts, first):
+        return jnp.concatenate([ref[i:j, first : first + HEAD_SIZE] for ref, i, j in parts], axis=0)
+
+    heads = range(n * group, (n + 1) * group)
+    stacked = jnp.concatenate([columns(query_parts, h * HEAD_SIZE) for h in heads], axis=0)
+    scores = lax.dot_general(
+        columns(prior_parts, n * HEAD_SIZE), stacked, (((1,), (1,)), ((), ())), preferred_element_type=jnp.float32
+    )
+    scores = jnp.minimum(scores, caps)
+    highest, total, summed = (ref[n] for ref in states)
+    top = jnp.maximum(highest, jnp.max(scores, axis=0, keepdims=True))
+    weights = jnp.exp2((scores - top) * log2_scale)
+    scale = jnp.exp2((highest - top) * log2_scale)
+    total = total * scale + jnp.sum(weights, axis=0, keepdims=True)
+    summed = summed * scale + lax.dot_general(
+        columns(prior_parts, width + n * HEAD_SIZE),
+        weights.astype(jnp.bfloat16),
+        (((0,), (0,)), ((), ())),
+        preferred_element_type=jnp.float32,
+    )
+    return top, total, summed
+
+
+def prior_caps(bounds_ref, block, blocks, group):
+    starts = [(block - blocks) * QUERY_BLOCK_ROWS]
+    return jnp.concatenate([score_caps(bounds_ref[:1, :], starts, 0)] * group, axis=1)
+
+
 def high_attention_kernel(chunks, wanted, *refs):
-    queries, owns, (*priors, bounds_ref, out_ref, lse_ref) = attention_refs(chunks, refs)
-    priors = block_parts(priors, chunks)
-    outs = {b: (out_ref, (b - wanted[0]) * QUERY_BLOCK_ROWS) for b in wanted}
-    lses = {b: lse_ref.at[b - wanted[0]] for b in wanted}
-    attend_blocks(wanted, chunks[0][1] // QUERY_BLOCK_ROWS, queries, owns, priors, bounds_ref, outs, lses)
+    queries, owns, refs = attention_refs(chunks, refs)
+    prior_ref, bounds_ref, out_ref, lse_ref, *states = refs
+    priors = block_parts([prior_ref], chunks)
+    low, blocks = wanted[0], chunks[0][1] // QUERY_BLOCK_ROWS
+    outs = {b: (out_ref, (b - low) * QUERY_BLOCK_ROWS) for b in wanted}
+    lses = {b: lse_ref.at[b - low] for b in wanted}
+    attend_blocks([*wanted, 0], blocks, queries, owns, priors, bounds_ref, outs, lses, states)
 
 
 def low_attention_kernel(chunks, wanted, *refs):
     queries, owns, refs = attention_refs(chunks, refs)
-    *priors, bounds_ref, above_ref, out_ref, lse_ref, highest_ref, total_ref, summed_ref, out_hbm, sem = refs
-    states = (highest_ref, total_ref, summed_ref)
+    *refs, out_hbm, sem = refs
+    *refs, out_ref, lse_ref, highest_ref, total_ref, summed_ref = refs
+    *priors, bounds_ref, above_ref, highest, total, summed = refs
     priors = block_parts(priors, chunks)
     rows = pl.ds((wanted[-1] + 1) * QUERY_BLOCK_ROWS, above_ref.shape[0])
     copy = pltpu.make_async_copy(above_ref, out_hbm.at[rows, :], sem)
@@ -261,7 +294,17 @@
     outs = {b: (out_ref, (b - wanted[0]) * QUERY_BLOCK_ROWS) for b in wanted}
     lses = {b: lse_ref.at[b - wanted[0]] for b in wanted}
     blocks = chunks[0][1] // QUERY_BLOCK_ROWS
-    attend_blocks([*wanted, 0], blocks, queries, owns, priors, bounds_ref, outs, lses, states)
+    attend_blocks(wanted, blocks, queries, owns, priors, bounds_ref, outs, lses)
+    kv_heads = highest.shape[0]
+    group = highest.shape[2] // QUERY_BLOCK_ROWS
+    for n in range(kv_heads):
+        states = (highest, total, summed)
+        for b in wanted:
+            caps = prior_caps(bounds_ref, b, blocks, group)
+            values = merge_keys(n, priors[b], queries[0], caps, states)
+            states = (highest_ref, total_ref, summed_ref)
+            for ref, value in zip(states, values):
+                ref[n] = value
     copy.wait()
 
 
@@ -270,34 +313,15 @@
     block = QUERY_BLOCK_ROWS
     copy = pltpu.make_async_copy(below_ref, out_hbm.at[pl.ds(block, below_ref.shape[0]), :], sem)
     copy.start()
-    width = prior_ref.shape[1] // 2
-    group = q_ref.shape[1] // width
-    bias = jnp.concatenate([key_bias(bounds_ref[:1, :], [-blocks * block], 0)] * group, axis=1)
-    for n in range(width // HEAD_SIZE):
-        heads = range(n * group, (n + 1) * group)
-        stacked = jnp.concatenate([q_ref[:, h * HEAD_SIZE : (h + 1) * HEAD_SIZE] for h in heads], axis=0)
-        scores = lax.dot_general(
-            prior_ref[:, n * HEAD_SIZE : (n + 1) * HEAD_SIZE],
-            stacked,
-            (((1,), (1,)), ((), ())),
-            preferred_element_type=jnp.float32,
-        )
-        scores = scores + bias
-        highest, total, summed = (ref[n] for ref in states)
-        top = jnp.maximum(highest, jnp.max(scores, axis=0, keepdims=True))
-        weights = jnp.exp2(scores - top)
-        scale = jnp.exp2(highest - top)
-        total = total * scale + jnp.sum(weights, axis=0, keepdims=True)
-        summed = summed * scale + lax.dot_general(
-            prior_ref[:, width + n * HEAD_SIZE : width + (n + 1) * HEAD_SIZE],
-            weights.astype(jnp.bfloat16),
-            (((0,), (0,)), ((), ())),
-            preferred_element_type=jnp.float32,
-        )
+    kv_heads = states[0].shape[0]
+    group = states[0].shape[2] // block
+    caps = prior_caps(bounds_ref, 0, blocks, group)
+    for n in range(kv_heads):
+        highest, total, summed = merge_keys(n, [(prior_ref, 0, block)], [(q_ref, 0, block)], caps, states)
         result = (summed / total).astype(jnp.bfloat16)
-        lse = (top + jnp.log2(total)) * math.log(2.0)
-        for g, h in enumerate(heads):
-            part = slice(g * block, (g + 1) * block)
+        lse = highest * score_scale + jnp.log(total)
+        for g in range(group):
+            h, part = n * group + g, slice(g * block, (g + 1) * block)
             here[:, h * HEAD_SIZE : (h + 1) * HEAD_SIZE] = jnp.transpose(result[:, part])
             lse_ref[h : h + 1, :] = lse[:, part]
     lses = [lse_ref[...]] + [ref[i] for ref in (below_lse, above_lse) for i in range(ref.shape[0])]
@@ -382,10 +406,10 @@
             groups += [[piece], [lax.ppermute(part, "proj", sibling) for part in pieces]]
         rest = (high - low, low, groups, gain_rest, squares)
         if low:
-            kv, q = project(*rest, k=(wkv_rest, kv_acc), q=(wq_rest, q_acc))
+            kv, q = project(*rest, (wkv_rest, kv_acc), (wq_rest, q_acc))
         else:
-            (kv,) = project(*rest, k=(wkv_rest, kv_acc))
-            (q,) = project(*rest, q=(wq_rest, q_acc))
+            (kv,) = project(*rest, (wkv_rest, kv_acc))
+            (q,) = project(*rest, (wq_rest, q_acc))
         tie = q
         prior.append(lax.ppermute(kv, "attn", onward))
         own.append(kv)
@@ -403,26 +427,26 @@
         )
 
     whole = jax.ShapeDtypeStruct((rows, width), jnp.bfloat16)
-    above, above_lse = pl.pallas_call(
+    kv_heads = w_key.shape[1] // HEAD_SIZE
+    lanes = heads // kv_heads * block
+    state_shapes = tuple(jax.ShapeDtypeStruct((kv_heads, n, lanes), jnp.float32) for n in (1, 1, HEAD_SIZE))
+    above, above_lse, *states = pl.pallas_call(
         functools.partial(high_attention_kernel, chunks, list(range(middle, blocks))),
-        out_shape=results(blocks - middle),
+        out_shape=(*results(blocks - middle), *state_shapes),
         in_specs=[VMEM] * (len(operands) + 2),
-        out_specs=(VMEM, VMEM),
+        out_specs=(VMEM,) * 5,
         compiler_params=params(24 << 20),
         cost_estimate=cost(),
     )(*operands, prior[0], bounds)
-    kv_heads = w_key.shape[1] // HEAD_SIZE
-    lanes = heads // kv_heads * block
-    states = tuple(jax.ShapeDtypeStruct((kv_heads, n, lanes), jnp.float32) for n in (1, 1, HEAD_SIZE))
     below, below_lse, *states, out = pl.pallas_call(
         functools.partial(low_attention_kernel, chunks, list(range(1, middle))),
-        out_shape=(*results(middle - 1), *states, whole),
-        in_specs=[VMEM] * (len(operands) + len(prior) + 1),
+        out_shape=(*results(middle - 1), *state_shapes, whole),
+        in_specs=[VMEM] * (len(operands) + len(prior) + 4),
         out_specs=(VMEM,) * 5 + (HBM,),
         scratch_shapes=[pltpu.SemaphoreType.DMA],
         compiler_params=params(24 << 20),
         cost_estimate=cost(),
-    )(*operands, *prior[:-1], bounds, above)
+    )(*operands, *prior[:-1], bounds, above, *states)
     out, here, send = pl.pallas_call(
         functools.partial(last_attention_kernel, blocks, servers),
         out_shape=(

time: 52.4 us -> 52.4 us (level)
  Pallas kernels: 16.9 us -> 18 us
  waiting for transfers between devices: 9.28 us -> 8.24 us
    ppermute x3, waiting for transfers between devices: 3.27 us -> 2.24 us  [shards(): prior.append(lax.ppermute(kv, 'attn', onward))]
    pallas_call x1, Pallas kernels: 2.03 us -> 2.77 us  [shards(): pl.pallas_call(functools.partial(high_attention_kernel, chunks, list(rang...]
  transfers between devices with their start and end apart: 15 -> 15, of which waited for: 7 -> 6; matrix products, arithmetic and copies ran while one was open for 6% -> 6% of each run, Pallas kernels for 29% -> 31%
where the time goes in v6:
time: 52.4 us; the launch traced here: 52.2 us
  Pallas kernels  18 us (34%)
  starting transfers between devices  12.7 us (24%)
  blocking collectives  9.39 us (18%)
  waiting for transfers between devices  8.24 us (16%)
  local copies, waits for them, and re-layouts  3.12 us (6%)
  between operations  0.8 us (2%)
    all_to_all x1, blocking collectives, shards(): recv = lax.all_to_all(send, 'attn', split_axis=0, concat_axis=0, tiled=True)  9.39 us
    pallas_call x1, Pallas kernels, local_part(): pl.pallas_call(local_kernel, out_shape=(pltpu.VMEM((rows, q_width), jnp.f...  7 us
    ppermute x3, waiting for transfers between devices, shards(): lax.ppermute(piece, 'proj', across(d))  5.65 us
    ppermute x3, starting transfers between devices, shards(): prior.append(lax.ppermute(kv, 'attn', onward))  5.34 us
    ppermute x3, starting transfers between devices, shards(): lax.ppermute(piece, 'proj', across(d))  4.61 us
    pallas_call x4, Pallas kernels, project(): pl.pallas_call(functools.partial(chunk_kernel, [len(group) for group in g...  4.33 us
    slice x2, local copies, waits for them, and re-layouts, shards(): piece = rest[low:high]  2.93 us
    pallas_call x1, Pallas kernels, shards(): pl.pallas_call(functools.partial(high_attention_kernel, chunks, list(rang...  2.77 us
  transfers between devices with their start and end apart: 15, of which 6 were waited for; matrix products, arithmetic and copies ran while one was open for 6% of the time, Pallas kernels for 31%

profile of v6, /device:TPU:0, one launch (start us, length us, event | category | flops | bytes accessed | tf_op | source)
XLA Modules:
  0.0 52.2 jit_solution(2465520652622718053)
XLA Ops:
  0.7 0.5 collective-permute-start.1
  1.2 1.1 %slice.33 = bf16[256,1024]{1,0:T(8,128)(2,1)S(1)} slice(bf16[512,1024]{1,0:T(8,128)(2,1)} %x_ref.1), slice={[256:512], [0:1024]} | slice | bytes 1048576 | tf_op jit(solution)/shard_map/slice | solution.py:377
  2.3 2.6 %collective-permute-start = (bf16[256,1024]{1,0:T(8,128)(2,1)S(1)}, bf16[256,1024]{1,0:T(8,128)(2,1)S(1)}, u32[]{:S(2)}, u32[]{:S(2)}) collective-permute-start(bf16[256,1024]{1,0:T(8,128)(2,1)S(1)} %slice.33), channel_id=1, source_target_pairs={{0,2},{1,3},{2,0},{3,1},{4,6},{5,7},{6,4},{7,5},{8,10},{9,11},{10,... | collective-permute-start | bytes 1572872 | tf_op jit(solution)/shard_map/ppermute | solution.py:380
  4.9 1.9 %fusion = (bf16[128,1024]{1,0:T(8,128)(2,1)}, bf16[128,1024]{1,0:T(8,128)(2,1)}) fusion(bf16[512,1024]{1,0:T(8,128)(2,1)} %x_ref.1), kind=kLoop, calls=%fused_computation | loop fusion | bytes 1048576 | tf_op jit(solution)/shard_map/slice | solution.py:377
  6.8 0.1 stack.23.order_ref
  6.9 7.0 %shard_map.86 = (f32[512,1024]{1,0:T(8,128)S(1)}, f32[512,512]{1,0:T(8,128)S(1)}, f32[512,1]{1,0:T(8,128)S(1)}, s32[4,128]{1,0:T(4,128)S(1)}, s32[4,8,128]{2,1,0...) custom-call(s32[5]{0:T(128)S(1)} %stack.23.order_ref, ...), custom_call_target="tpu_custom_call" | custom-call | flops 1024 | bytes 1024 | tf_op jit(solution)/shard_map/pallas_call | solution.py:93
  13.9 3.8 %collective-permute-done.refs_0_ = bf16[256,1024]{1,0:T(8,128)(2,1)S(1)} collective-permute-done((bf16[256,1024]{1,0:T(8,128)(2,1)S(1)}, bf16[256,1024]{1,0:T(8,128)(2,1)S(1)}, u32[]{:S(2)}, u32[]{:S(2)}) %collective-permute-start) | collective-permute-done | bytes 524320 | tf_op jit(solution)/shard_map/ppermute | solution.py:380
  17.7 0.1 collective-permute-start.2
  17.8 0.5 collective-permute-start.3
  18.3 0.1 collective-permute-start.4
  18.4 0.4 collective-permute-start.5
  18.8 0.3 collective-permute-done.2.refs_1_
  19.1 2.0 %collective-permute-start.9 = (bf16[128,1024]{1,0:T(8,128)(2,1)S(1)}, bf16[128,1024]{1,0:T(8,128)(2,1)S(1)}, u32[]{:S(2)}, u32[]{:S(2)}) collective-permute-start(bf16[128,1024]{1,0:T(8,128)(2,1)S(1)} %copy-done.3), channel_id=1, source_target_pairs={{0,2},{1,3},{2,0},{3,1},{4,6},{5,7},{6,4},{7,5},{8,10},{9,11},{10,... | collective-permute-start | bytes 786440 | tf_op jit(solution)/shard_map/ppermute | solution.py:380
  21.1 1.9 %shard_map.87 = (bf16[256,512]{1,0:T(8,128)(2,1)S(1)}, bf16[256,1024]{1,0:T(8,128)(2,1)S(1)}) custom-call(bf16[256,1024]{1,0:T(8,128)(2,1)S(1)} %collective-permute-done.refs_0_, bf16[64,1024]{1,0:T(8,128)(2,1)S(1)} %collective-permute-done.2.refs_1_, bf16[64,1024]{1,0:T(8,128)(2,1)S(1)} %collective-permute-done.3.refs_2_, ...), custom_call_target="tpu_custom_call" | custom-call | flops 1024 | bytes 1024 | tf_op jit(solution)/shard_map/pallas_call | solution.py:142
  23.1 0.2 collective-permute-done.6.refs_0_
  23.3 0.1 collective-permute-start.7
  23.4 0.5 collective-permute-start.8
  23.9 2.0 %collective-permute-start.13 = (bf16[256,512]{1,0:T(8,128)(2,1)S(1)}, bf16[256,512]{1,0:T(8,128)(2,1)S(1)}, u32[]{:S(2)}, u32[]{:S(2)}) collective-permute-start(bf16[256,512]{1,0:T(8,128)(2,1)S(1)} %get-tuple-element.55.refs_3_), channel_id=1, source_target_pairs={{0,4},{4,8},{8,12},{12,16},{16,20},{20,24},{24,28},{28,0},{1,5},{5... | collective-permute-start | bytes 786440 | tf_op jit(solution)/shard_map/ppermute | solution.py:414
  25.9 1.1 %shard_map.88 = (bf16[128,512]{1,0:T(8,128)(2,1)S(1)}, bf16[128,1024]{1,0:T(8,128)(2,1)S(1)}) custom-call(bf16[128,1024]{1,0:T(8,128)(2,1)S(1)} %collective-permute-done.6.refs_0_, bf16[64,1024]{1,0:T(8,128)(2,1)S(1)} %collective-permute-done.7.refs_1_, bf16[64,1024]{1,0:T(8,128)(2,1)S(1)} %collective-permute-done.8.refs_2_, ...), custom_call_target="tpu_custom_call" | custom-call | flops 1024 | bytes 1024 | tf_op jit(solution)/shard_map/pallas_call | solution.py:142
  27.0 1.6 %collective-permute-done.9.refs_0_ = bf16[128,1024]{1,0:T(8,128)(2,1)S(1)} collective-permute-done((bf16[128,1024]{1,0:T(8,128)(2,1)S(1)}, bf16[128,1024]{1,0:T(8,128)(2,1)S(1)}, u32[]{:S(2)}, u32[]{:S(2)}) %collective-permute-start.9) | collective-permute-done | bytes 262176 | tf_op jit(solution)/shard_map/ppermute | solution.py:380
  28.8 0.5 collective-permute-start.11
  29.3 1.8 %collective-permute-start.14 = (bf16[128,512]{1,0:T(8,128)(2,1)S(1)}, bf16[128,512]{1,0:T(8,128)(2,1)S(1)}, u32[]{:S(2)}, u32[]{:S(2)}) collective-permute-start(bf16[128,512]{1,0:T(8,128)(2,1)S(1)} %get-tuple-element.56.refs_4_), channel_id=1, source_target_pairs={{0,4},{4,8},{8,12},{12,16},{16,20},{20,24},{24,28},{28,0},{1,5},{5... | collective-permute-start | bytes 393224 | tf_op jit(solution)/shard_map/ppermute | solution.py:414
  31.0 0.5 shard_map.90.refs_5_
  31.5 1.6 %collective-permute-start.12 = (bf16[128,512]{1,0:T(8,128)(2,1)S(1)}, bf16[128,512]{1,0:T(8,128)(2,1)S(1)}, u32[]{:S(2)}, u32[]{:S(2)}) collective-permute-start(bf16[128,512]{1,0:T(8,128)(2,1)S(1)} %shard_map.90.refs_5_), channel_id=1, source_target_pairs={{0,4},{4,8},{8,12},{12,16},{16,20},{20,24},{24,28},{28,0},{1,5},{5... | collective-permute-start | bytes 393224 | tf_op jit(solution)/shard_map/ppermute | solution.py:414
  33.1 0.8 %shard_map.89.refs_2_.q_ref = bf16[128,1024]{1,0:T(8,128)(2,1)S(1)} custom-call(bf16[128,1024]{1,0:T(8,128)(2,1)S(1)} %collective-permute-done.9.refs_0_, bf16[64,1024]{1,0:T(8,128)(2,1)S(1)} %collective-permute-done.10.refs_1_, bf16[64,1024]{1,0:T(8,128)(2,1)S(1)} %collective-permute-done.11.refs_2_, f32[2,1024]{1,0:T(2,128)S(1)} %get-tuple-element.41.refs_5_.refs_3_, ...), custom_call_target="tpu_custom_call" | custom-call | flops 1024 | bytes 1024 | tf_op jit(solution)/shard_map/pallas_call | solution.py:142
  33.9 2.0 %collective-permute-done.13.refs_6_ = bf16[256,512]{1,0:T(8,128)(2,1)S(1)} collective-permute-done((bf16[256,512]{1,0:T(8,128)(2,1)S(1)}, bf16[256,512]{1,0:T(8,128)(2,1)S(1)}, u32[]{:S(2)}, u32[]{:S(2)}) %collective-permute-start.13) | collective-permute-done | bytes 262176 | tf_op jit(solution)/shard_map/ppermute | solution.py:414
  35.9 2.8 %shard_map.91 = (bf16[256,1024]{1,0:T(8,128)(2,1)S(1)}, f32[2,8,128]{2,1,0:T(8,128)S(1)}, f32[2,1,512]{2,1,0:T(1,128)S(1)}, f32[2,1,512]{2,1,0:T(1,128)S(1)}, f32[2,128,512]{2,1,0:T(8,128)S(1)}) custom-call(bf16[256,1024]{1,0:T(8,128)(2,1)S(1)} %get-tuple-element.53.refs_0_, bf16[128,1024]{1,0:T(8,128)(2,1)S(1)} %get-tuple-element.54.refs_1_, ...), custom_call_target="tpu_custom_call" | custom-call | flops 1024 | bytes 1024 | tf_op jit(solution)/shard_map/pallas_call | solution.py:433
  38.7 2.2 %shard_map.92 = (bf16[128,1024]{1,0:T(8,128)(2,1)S(1)}, f32[1,8,128]{2,1,0:T(8,128)S(1)}, f32[2,1,512]{2,1,0:T(1,128)S(1)}, f32[2,1,512]{2,1,0:T(1,128)S(1)}, f3...) custom-call(bf16[256,1024]{1,0:T(8,128)(2,1)S(1)} %get-tuple-element.53.refs_0_, ...), custom_call_target="tpu_custom_call" | custom-call | flops 1024 | bytes 1024 | tf_op jit(solution)/shard_map/pallas_call | solution.py:441
  40.8 0.2 collective-permute-done.12.prior_ref
  41.1 1.0 %shard_map.93 = (bf16[512,1024]{1,0:T(8,128)(2,1)}, bf16[128,1024]{1,0:T(8,128)(2,1)S(1)}, bf16[8,8,128]{2,1,0:T(8,128)(2,1)S(1)}) custom-call(bf16[128,1024]{1,0:T(8,128)(2,1)S(1)} %shard_map.89.refs_2_.q_ref, bf16[128,512]{1,0:T(8,128)(2,1)S(1)} %collective-permute-done.12.prior_ref, ...), custom_call_target="tpu_custom_call", output_to_operand_aliasing={{0}: (10, {})} | custom-call | flops 1024 | bytes 1024 | tf_op jit(solution)/shard_map/pallas_call | solution.py:450
  42.1 9.4 %all_to_all.5.recv_ref = bf16[8,8,128]{2,1,0:T(8,128)(2,1)S(1)} all-to-all(bf16[8,8,128]{2,1,0:T(8,128)(2,1)S(1)} %get-tuple-element.69), channel_id=1, replica_groups=mesh['attn'=8,'proj'=4] {'attn'}, dimensions={0} | all-to-all | bytes 32768 | tf_op jit(solution)/shard_map/all_to_all | solution.py:464
  51.5 0.7 %shard_map.94 = (f32[4,8,128]{2,1,0:T(8,128)}, bf16[512,1024]{1,0:T(8,128)(2,1)}) custom-call(bf16[8,8,128]{2,1,0:T(8,128)(2,1)S(1)} %all_to_all.5.recv_ref, bf16[128,1024]{1,0:T(8,128)(2,1)S(1)} %get-tuple-element.70.here_ref, bf16[512,1024]{1,0:T(8,128)(2,1)} %get-tuple-element.71._), custom_call_target="tpu_custom_call", output_to_operand_aliasing={{1}: (2, {})} | custom-call | tf_op jit(solution)/shard_map/pallas_call | solution.py:465
  (25 shorter events, 0.2 us)
Async XLA Ops:
  0.6 6.3 %copy-start = (bf16[512,1024]{1,0:T(8,128)(2,1)S(1)}, bf16[512,1024]{1,0:T(8,128)(2,1)}, u32[]{:S(2)}) copy-start(bf16[512,1024]{1,0:T(8,128)(2,1)} %x_ref.1) | copy-start | bytes 3145732
  0.6 6.1 %copy-start.4 = (f32[4096]{0:T(1024)S(1)}, f32[4096]{0:T(1024)}, u32[]{:S(2)}) copy-start(f32[4096]{0:T(1024)} %param.8) | copy-start | bytes 49156
  0.7 6.2 %copy-start.1 = (s32[32]{0:T(128)S(1)}, s32[32]{0:T(128)}, u32[]{:S(2)}) copy-start(s32[32]{0:T(128)} %docs_ref.1) | copy-start | bytes 388
  0.7 6.2 %copy-start.2 = (s32[4]{0:T(128)S(1)}, s32[4]{0:T(128)}, u32[]{:S(2)}) copy-start(s32[4]{0:T(128)} %server_ref.1) | copy-start | bytes 52
  0.7 6.2 %collective-permute-start.1 = (bf16[512,1024]{1,0:T(8,128)(2,1)}, bf16[512,1024]{1,0:T(8,128)(2,1)S(1)}, u32[]{:S(2)}, u32[]{:S(2)}) collective-permute-start(bf16[512,1024]{1,0:T(8,128)(2,1)} %x_ref.1), channel_id=1, source_target_pairs={{0,1},{1,0},{2,3},{3,2},{4,5},{5,4},{6,7},{7,6},{8,9},{9,8},{10,11... | collective-permute-start | bytes 3145736 | tf_op jit(solution)/shard_map/ppermute | solution.py:381
  2.3 15.4 %collective-permute-start = (bf16[256,1024]{1,0:T(8,128)(2,1)S(1)}, bf16[256,1024]{1,0:T(8,128)(2,1)S(1)}, u32[]{:S(2)}, u32[]{:S(2)}) collective-permute-start(bf16[256,1024]{1,0:T(8,128)(2,1)S(1)} %slice.33), channel_id=1, source_target_pairs={{0,2},{1,3},{2,0},{3,1},{4,6},{5,7},{6,4},{7,5},{8,10},{9,11},{10,... | collective-permute-start | bytes 1572872 | tf_op jit(solution)/shard_map/ppermute | solution.py:380
  6.8 16.5 %collective-permute-start.6 = (bf16[128,1024]{1,0:T(8,128)(2,1)}, bf16[128,1024]{1,0:T(8,128)(2,1)S(1)}, u32[]{:S(2)}, u32[]{:S(2)}) collective-permute-start(bf16[128,1024]{1,0:T(8,128)(2,1)} %get-tuple-element.75), channel_id=1, source_target_pairs={{0,2},{1,3},{2,0},{3,1},{4,6},{5,7},{6,4},{7,5},{8,10},{9,11},{10,... | collective-permute-start | bytes 786440 | tf_op jit(solution)/shard_map/ppermute | solution.py:380
  6.9 12.3 %copy-start.3 = (bf16[128,1024]{1,0:T(8,128)(2,1)S(1)}, bf16[128,1024]{1,0:T(8,128)(2,1)}, u32[]{:S(2)}) copy-start(bf16[128,1024]{1,0:T(8,128)(2,1)} %get-tuple-element.74) | copy-start | bytes 786436
  17.7 1.4 %collective-permute-start.2 = (bf16[64,1024]{1,0:T(8,128)(2,1)S(1)}, bf16[64,1024]{1,0:T(8,128)(2,1)S(1)}, u32[]{:S(2)}, u32[]{:S(2)}) collective-permute-start(bf16[64,1024]{1,0:T(8,128)(2,1)S(1)} %get-tuple-element.79), channel_id=1, source_target_pairs={{0,1},{1,0},{2,3},{3,2},{4,5},{5,4},{6,7},{7,6},{8,9},{9,8},{10,11... | collective-permute-start | bytes 393224 | tf_op jit(solution)/shard_map/ppermute | solution.py:406
  17.8 3.3 %collective-permute-start.3 = (bf16[64,1024]{1,0:T(8,128)(2,1)S(1)}, bf16[64,1024]{1,0:T(8,128)(2,1)S(1)}, u32[]{:S(2)}, u32[]{:S(2)}) collective-permute-start(bf16[64,1024]{1,0:T(8,128)(2,1)S(1)} %get-tuple-element.78), channel_id=1, source_target_pairs={{0,1},{1,0},{2,3},{3,2},{4,5},{5,4},{6,7},{7,6},{8,9},{9,8},{10,11... | collective-permute-start | bytes 393224 | tf_op jit(solution)/shard_map/ppermute | solution.py:406
  18.3 2.8 %collective-permute-start.4 = (bf16[64,1024]{1,0:T(8,128)(2,1)S(1)}, bf16[64,1024]{1,0:T(8,128)(2,1)S(1)}, u32[]{:S(2)}, u32[]{:S(2)}) collective-permute-start(bf16[64,1024]{1,0:T(8,128)(2,1)S(1)} %get-tuple-element.77), channel_id=1, source_target_pairs={{0,1},{1,0},{2,3},{3,2},{4,5},{5,4},{6,7},{7,6},{8,9},{9,8},{10,11... | collective-permute-start | bytes 393224 | tf_op jit(solution)/shard_map/ppermute | solution.py:406
  18.4 2.7 %collective-permute-start.5 = (bf16[64,1024]{1,0:T(8,128)(2,1)S(1)}, bf16[64,1024]{1,0:T(8,128)(2,1)S(1)}, u32[]{:S(2)}, u32[]{:S(2)}) collective-permute-start(bf16[64,1024]{1,0:T(8,128)(2,1)S(1)} %get-tuple-element.76), channel_id=1, source_target_pairs={{0,1},{1,0},{2,3},{3,2},{4,5},{5,4},{6,7},{7,6},{8,9},{9,8},{10,11... | collective-permute-start | bytes 393224 | tf_op jit(solution)/shard_map/ppermute | solution.py:406
  19.1 9.5 %collective-permute-start.9 = (bf16[128,1024]{1,0:T(8,128)(2,1)S(1)}, bf16[128,1024]{1,0:T(8,128)(2,1)S(1)}, u32[]{:S(2)}, u32[]{:S(2)}) collective-permute-start(bf16[128,1024]{1,0:T(8,128)(2,1)S(1)} %copy-done.3), channel_id=1, source_target_pairs={{0,2},{1,3},{2,0},{3,1},{4,6},{5,7},{6,4},{7,5},{8,10},{9,11},{10,... | collective-permute-start | bytes 786440 | tf_op jit(solution)/shard_map/ppermute | solution.py:380
  23.3 2.6 %collective-permute-start.7 = (bf16[64,1024]{1,0:T(8,128)(2,1)S(1)}, bf16[64,1024]{1,0:T(8,128)(2,1)S(1)}, u32[]{:S(2)}, u32[]{:S(2)}) collective-permute-start(bf16[64,1024]{1,0:T(8,128)(2,1)S(1)} %get-tuple-element.83), channel_id=1, source_target_pairs={{0,1},{1,0},{2,3},{3,2},{4,5},{5,4},{6,7},{7,6},{8,9},{9,8},{10,11... | collective-permute-start | bytes 393224 | tf_op jit(solution)/shard_map/ppermute | solution.py:406
  23.4 2.5 %collective-permute-start.8 = (bf16[64,1024]{1,0:T(8,128)(2,1)S(1)}, bf16[64,1024]{1,0:T(8,128)(2,1)S(1)}, u32[]{:S(2)}, u32[]{:S(2)}) collective-permute-start(bf16[64,1024]{1,0:T(8,128)(2,1)S(1)} %get-tuple-element.82), channel_id=1, source_target_pairs={{0,1},{1,0},{2,3},{3,2},{4,5},{5,4},{6,7},{7,6},{8,9},{9,8},{10,11... | collective-permute-start | bytes 393224 | tf_op jit(solution)/shard_map/ppermute | solution.py:406
  23.9 12.0 %collective-permute-start.13 = (bf16[256,512]{1,0:T(8,128)(2,1)S(1)}, bf16[256,512]{1,0:T(8,128)(2,1)S(1)}, u32[]{:S(2)}, u32[]{:S(2)}) collective-permute-start(bf16[256,512]{1,0:T(8,128)(2,1)S(1)} %get-tuple-element.55.refs_3_), channel_id=1, source_target_pairs={{0,4},{4,8},{8,12},{12,16},{16,20},{20,24},{24,28},{28,0},{1,5},{5... | collective-permute-start | bytes 786440 | tf_op jit(solution)/shard_map/ppermute | solution.py:414
  28.7 2.4 %collective-permute-start.10 = (bf16[64,1024]{1,0:T(8,128)(2,1)S(1)}, bf16[64,1024]{1,0:T(8,128)(2,1)S(1)}, u32[]{:S(2)}, u32[]{:S(2)}) collective-permute-start(bf16[64,1024]{1,0:T(8,128)(2,1)S(1)} %get-tuple-element.81), channel_id=1, source_target_pairs={{0,1},{1,0},{2,3},{3,2},{4,5},{5,4},{6,7},{7,6},{8,9},{9,8},{10,11... | collective-permute-start | bytes 393224 | tf_op jit(solution)/shard_map/ppermute | solution.py:406
  28.8 2.3 %collective-permute-start.11 = (bf16[64,1024]{1,0:T(8,128)(2,1)S(1)}, bf16[64,1024]{1,0:T(8,128)(2,1)S(1)}, u32[]{:S(2)}, u32[]{:S(2)}) collective-permute-start(bf16[64,1024]{1,0:T(8,128)(2,1)S(1)} %get-tuple-element.80), channel_id=1, source_target_pairs={{0,1},{1,0},{2,3},{3,2},{4,5},{5,4},{6,7},{7,6},{8,9},{9,8},{10,11... | collective-permute-start | bytes 393224 | tf_op jit(solution)/shard_map/ppermute | solution.py:406
  29.3 9.4 %collective-permute-start.14 = (bf16[128,512]{1,0:T(8,128)(2,1)S(1)}, bf16[128,512]{1,0:T(8,128)(2,1)S(1)}, u32[]{:S(2)}, u32[]{:S(2)}) collective-permute-start(bf16[128,512]{1,0:T(8,128)(2,1)S(1)} %get-tuple-element.56.refs_4_), channel_id=1, source_target_pairs={{0,4},{4,8},{8,12},{12,16},{16,20},{20,24},{24,28},{28,0},{1,5},{5... | collective-permute-start | bytes 393224 | tf_op jit(solution)/shard_map/ppermute | solution.py:414
  31.5 9.6 %collective-permute-start.12 = (bf16[128,512]{1,0:T(8,128)(2,1)S(1)}, bf16[128,512]{1,0:T(8,128)(2,1)S(1)}, u32[]{:S(2)}, u32[]{:S(2)}) collective-permute-start(bf16[128,512]{1,0:T(8,128)(2,1)S(1)} %shard_map.90.refs_5_), channel_id=1, source_target_pairs={{0,4},{4,8},{8,12},{12,16},{16,20},{20,24},{24,28},{28,0},{1,5},{5... | collective-permute-start | bytes 393224 | tf_op jit(solution)/shard_map/ppermute | solution.py:414

commit v7 on v6

--- a/solution.py
+++ b/solution.py
@@ -309,10 +309,8 @@
 
 
 def last_attention_kernel(blocks, servers, q_ref, prior_ref, bounds_ref, *refs):
-    *states, route_ref, below_ref, below_lse, above_lse, _, out_hbm, here, send_ref, lse_ref, sem = refs
+    *states, route_ref, below_lse, above_lse, here, send_ref, lse_ref = refs
     block = QUERY_BLOCK_ROWS
-    copy = pltpu.make_async_copy(below_ref, out_hbm.at[pl.ds(block, below_ref.shape[0]), :], sem)
-    copy.start()
     kv_heads = states[0].shape[0]
     group = states[0].shape[2] // block
     caps = prior_caps(bounds_ref, 0, blocks, group)
@@ -330,12 +328,14 @@
         for i, rows in enumerate(lses):
             value = jnp.where(route_ref[i] == s, rows, value)
         send_ref[s] = value.astype(jnp.bfloat16)
-    copy.wait()
-
-
-def pick_kernel(blocks, recv_ref, here_ref, _, served_hbm, out_hbm, served, sems):
+
+
+def pick_kernel(blocks, recv_ref, here_ref, below_ref, _, served_hbm, out_hbm, served, sems):
     here = pltpu.make_async_copy(here_ref, out_hbm.at[pl.ds(0, here_ref.shape[0]), :], sems.at[0])
     here.start()
+    rows = pl.ds(here_ref.shape[0], below_ref.shape[0])
+    below = pltpu.make_async_copy(below_ref, out_hbm.at[rows, :], sems.at[2])
+    below.start()
     shape = recv_ref.shape[1:]
     rank = jnp.zeros(shape, jnp.int32)
     picked = [jnp.zeros(shape, jnp.float32) for _ in range(blocks)]
@@ -351,6 +351,7 @@
     copy.start()
     copy.wait()
     here.wait()
+    below.wait()
 
 
 def shards(tokens, norm_gain, w_query, w_key, value_matrix, doc_lengths, block_server):
@@ -447,20 +448,15 @@
         compiler_params=params(24 << 20),
         cost_estimate=cost(),
     )(*operands, *prior[:-1], bounds, above, *states)
-    out, here, send = pl.pallas_call(
+    here, send = pl.pallas_call(
         functools.partial(last_attention_kernel, blocks, servers),
-        out_shape=(
-            whole,
-            results(1)[0],
-            jax.ShapeDtypeStruct((servers, heads, block), jnp.bfloat16),
-        ),
-        in_specs=[VMEM] * 10 + [HBM],
-        out_specs=(HBM, VMEM, VMEM),
-        scratch_shapes=[pltpu.VMEM((heads, block), jnp.float32), pltpu.SemaphoreType.DMA],
-        input_output_aliases={10: 0},
+        out_shape=(results(1)[0], jax.ShapeDtypeStruct((servers, heads, block), jnp.bfloat16)),
+        in_specs=[VMEM] * 9,
+        out_specs=(VMEM, VMEM),
+        scratch_shapes=[pltpu.VMEM((heads, block), jnp.float32)],
         compiler_params=params(24 << 20),
         cost_estimate=cost(),
-    )(queries[-1], prior[-1], bounds, *states, routes, below, below_lse, above_lse, out)
+    )(queries[-1], prior[-1], bounds, *states, routes, below_lse, above_lse)
     recv = lax.all_to_all(send, "attn", split_axis=0, concat_axis=0, tiled=True)
     served, out = pl.pallas_call(
         functools.partial(pick_kernel, blocks),
@@ -468,12 +464,12 @@
             jax.ShapeDtypeStruct((blocks, heads, block), jnp.float32),
             jax.ShapeDtypeStruct((rows, heads * HEAD_SIZE), jnp.bfloat16),
         ),
-        in_specs=[VMEM, VMEM, HBM],
+        in_specs=[VMEM, VMEM, VMEM, HBM],
         out_specs=(HBM, HBM),
-        scratch_shapes=[pltpu.VMEM((blocks, heads, block), jnp.float32), pltpu.SemaphoreType.DMA((2,))],
-        input_output_aliases={2: 1},
+        scratch_shapes=[pltpu.VMEM((blocks, heads, block), jnp.float32), pltpu.SemaphoreType.DMA((3,))],
+        input_output_aliases={3: 1},
         compiler_params=params(),
-    )(recv, here, out)
+    )(recv, here, below, out)
     return (out, served)
 
 

time: 52.4 us -> 52.3 us (level)
  no operation moved by 1% of the time
where the time goes in v7:
time: 52.3 us; the launch traced here: 52.1 us
  Pallas kernels  17.8 us (34%)
  starting transfers between devices  12.7 us (24%)
  blocking collectives  9.4 us (18%)
  waiting for transfers between devices  8.24 us (16%)
  local copies, waits for them, and re-layouts  3.12 us (6%)
  between operations  0.8 us (2%)
    all_to_all x1, blocking collectives, shards(): recv = lax.all_to_all(send, 'attn', split_axis=0, concat_axis=0, tiled=True)  9.4 us
    pallas_call x1, Pallas kernels, local_part(): pl.pallas_call(local_kernel, out_shape=(pltpu.VMEM((rows, q_width), jnp.f...  7 us
    ppermute x3, waiting for transfers between devices, shards(): lax.ppermute(piece, 'proj', across(d))  5.65 us
    ppermute x3, starting transfers between devices, shards(): prior.append(lax.ppermute(kv, 'attn', onward))  5.34 us
    ppermute x3, starting transfers between devices, shards(): lax.ppermute(piece, 'proj', across(d))  4.61 us
    pallas_call x4, Pallas kernels, project(): pl.pallas_call(functools.partial(chunk_kernel, [len(group) for group in g...  4.33 us
    slice x2, local copies, waits for them, and re-layouts, shards(): piece = rest[low:high]  2.93 us
    pallas_call x1, Pallas kernels, shards(): pl.pallas_call(functools.partial(high_attention_kernel, chunks, list(rang...  2.77 us
  transfers between devices with their start and end apart: 15, of which 6 were waited for; matrix products, arithmetic and copies ran while one was open for 6% of the time, Pallas kernels for 31%

profile of v7, /device:TPU:0, one launch (start us, length us, event | category | flops | bytes accessed | tf_op | source)
XLA Modules:
  0.0 52.1 jit_solution(2032186788788611144)
XLA Ops:
  0.7 0.5 collective-permute-start.1
  1.2 1.1 %slice.33 = bf16[256,1024]{1,0:T(8,128)(2,1)S(1)} slice(bf16[512,1024]{1,0:T(8,128)(2,1)} %x_ref.1), slice={[256:512], [0:1024]} | slice | bytes 1048576 | tf_op jit(solution)/shard_map/slice | solution.py:378
  2.3 2.6 %collective-permute-start = (bf16[256,1024]{1,0:T(8,128)(2,1)S(1)}, bf16[256,1024]{1,0:T(8,128)(2,1)S(1)}, u32[]{:S(2)}, u32[]{:S(2)}) collective-permute-start(bf16[256,1024]{1,0:T(8,128)(2,1)S(1)} %slice.33), channel_id=1, source_target_pairs={{0,2},{1,3},{2,0},{3,1},{4,6},{5,7},{6,4},{7,5},{8,10},{9,11},{10,... | collective-permute-start | bytes 1572872 | tf_op jit(solution)/shard_map/ppermute | solution.py:381
  4.9 1.9 %fusion = (bf16[128,1024]{1,0:T(8,128)(2,1)}, bf16[128,1024]{1,0:T(8,128)(2,1)}) fusion(bf16[512,1024]{1,0:T(8,128)(2,1)} %x_ref.1), kind=kLoop, calls=%fused_computation | loop fusion | bytes 1048576 | tf_op jit(solution)/shard_map/slice | solution.py:378
  6.8 0.1 stack.23.order_ref
  6.9 7.0 %shard_map.86 = (f32[512,1024]{1,0:T(8,128)S(1)}, f32[512,512]{1,0:T(8,128)S(1)}, f32[512,1]{1,0:T(8,128)S(1)}, s32[4,128]{1,0:T(4,128)S(1)}, s32[4,8,128]{2,1,0...) custom-call(s32[5]{0:T(128)S(1)} %stack.23.order_ref, ...), custom_call_target="tpu_custom_call" | custom-call | flops 1024 | bytes 1024 | tf_op jit(solution)/shard_map/pallas_call | solution.py:93
  13.9 3.8 %collective-permute-done.refs_0_ = bf16[256,1024]{1,0:T(8,128)(2,1)S(1)} collective-permute-done((bf16[256,1024]{1,0:T(8,128)(2,1)S(1)}, bf16[256,1024]{1,0:T(8,128)(2,1)S(1)}, u32[]{:S(2)}, u32[]{:S(2)}) %collective-permute-start) | collective-permute-done | bytes 524320 | tf_op jit(solution)/shard_map/ppermute | solution.py:381
  17.7 0.1 collective-permute-start.2
  17.8 0.5 collective-permute-start.3
  18.3 0.1 collective-permute-start.4
  18.4 0.4 collective-permute-start.5
  18.8 0.3 collective-permute-done.2.refs_1_
  19.1 2.0 %collective-permute-start.9 = (bf16[128,1024]{1,0:T(8,128)(2,1)S(1)}, bf16[128,1024]{1,0:T(8,128)(2,1)S(1)}, u32[]{:S(2)}, u32[]{:S(2)}) collective-permute-start(bf16[128,1024]{1,0:T(8,128)(2,1)S(1)} %copy-done.3), channel_id=1, source_target_pairs={{0,2},{1,3},{2,0},{3,1},{4,6},{5,7},{6,4},{7,5},{8,10},{9,11},{10,... | collective-permute-start | bytes 786440 | tf_op jit(solution)/shard_map/ppermute | solution.py:381
  21.1 1.9 %shard_map.87 = (bf16[256,512]{1,0:T(8,128)(2,1)S(1)}, bf16[256,1024]{1,0:T(8,128)(2,1)S(1)}) custom-call(bf16[256,1024]{1,0:T(8,128)(2,1)S(1)} %collective-permute-done.refs_0_, bf16[64,1024]{1,0:T(8,128)(2,1)S(1)} %collective-permute-done.2.refs_1_, bf16[64,1024]{1,0:T(8,128)(2,1)S(1)} %collective-permute-done.3.refs_2_, ...), custom_call_target="tpu_custom_call" | custom-call | flops 1024 | bytes 1024 | tf_op jit(solution)/shard_map/pallas_call | solution.py:142
  23.1 0.2 collective-permute-done.6.refs_0_
  23.3 0.1 collective-permute-start.7
  23.4 0.5 collective-permute-start.8
  23.9 2.0 %collective-permute-start.13 = (bf16[256,512]{1,0:T(8,128)(2,1)S(1)}, bf16[256,512]{1,0:T(8,128)(2,1)S(1)}, u32[]{:S(2)}, u32[]{:S(2)}) collective-permute-start(bf16[256,512]{1,0:T(8,128)(2,1)S(1)} %get-tuple-element.54.refs_3_), channel_id=1, source_target_pairs={{0,4},{4,8},{8,12},{12,16},{16,20},{20,24},{24,28},{28,0},{1,5},{5... | collective-permute-start | bytes 786440 | tf_op jit(solution)/shard_map/ppermute | solution.py:415
  25.9 1.1 %shard_map.88 = (bf16[128,512]{1,0:T(8,128)(2,1)S(1)}, bf16[128,1024]{1,0:T(8,128)(2,1)S(1)}) custom-call(bf16[128,1024]{1,0:T(8,128)(2,1)S(1)} %collective-permute-done.6.refs_0_, bf16[64,1024]{1,0:T(8,128)(2,1)S(1)} %collective-permute-done.7.refs_1_, bf16[64,1024]{1,0:T(8,128)(2,1)S(1)} %collective-permute-done.8.refs_2_, ...), custom_call_target="tpu_custom_call" | custom-call | flops 1024 | bytes 1024 | tf_op jit(solution)/shard_map/pallas_call | solution.py:142
  27.0 1.6 %collective-permute-done.9.refs_0_ = bf16[128,1024]{1,0:T(8,128)(2,1)S(1)} collective-permute-done((bf16[128,1024]{1,0:T(8,128)(2,1)S(1)}, bf16[128,1024]{1,0:T(8,128)(2,1)S(1)}, u32[]{:S(2)}, u32[]{:S(2)}) %collective-permute-start.9) | collective-permute-done | bytes 262176 | tf_op jit(solution)/shard_map/ppermute | solution.py:381
  28.8 0.5 collective-permute-start.11
  29.3 1.8 %collective-permute-start.14 = (bf16[128,512]{1,0:T(8,128)(2,1)S(1)}, bf16[128,512]{1,0:T(8,128)(2,1)S(1)}, u32[]{:S(2)}, u32[]{:S(2)}) collective-permute-start(bf16[128,512]{1,0:T(8,128)(2,1)S(1)} %get-tuple-element.55.refs_4_), channel_id=1, source_target_pairs={{0,4},{4,8},{8,12},{12,16},{16,20},{20,24},{24,28},{28,0},{1,5},{5... | collective-permute-start | bytes 393224 | tf_op jit(solution)/shard_map/ppermute | solution.py:415
  31.0 0.5 shard_map.90.refs_5_
  31.5 1.6 %collective-permute-start.12 = (bf16[128,512]{1,0:T(8,128)(2,1)S(1)}, bf16[128,512]{1,0:T(8,128)(2,1)S(1)}, u32[]{:S(2)}, u32[]{:S(2)}) collective-permute-start(bf16[128,512]{1,0:T(8,128)(2,1)S(1)} %shard_map.90.refs_5_), channel_id=1, source_target_pairs={{0,4},{4,8},{8,12},{12,16},{16,20},{20,24},{24,28},{28,0},{1,5},{5... | collective-permute-start | bytes 393224 | tf_op jit(solution)/shard_map/ppermute | solution.py:415
  33.1 0.8 %shard_map.89.refs_2_.q_ref = bf16[128,1024]{1,0:T(8,128)(2,1)S(1)} custom-call(bf16[128,1024]{1,0:T(8,128)(2,1)S(1)} %collective-permute-done.9.refs_0_, bf16[64,1024]{1,0:T(8,128)(2,1)S(1)} %collective-permute-done.10.refs_1_, bf16[64,1024]{1,0:T(8,128)(2,1)S(1)} %collective-permute-done.11.refs_2_, f32[2,1024]{1,0:T(2,128)S(1)} %get-tuple-element.40.refs_5_.refs_3_, ...), custom_call_target="tpu_custom_call" | custom-call | flops 1024 | bytes 1024 | tf_op jit(solution)/shard_map/pallas_call | solution.py:142
  33.9 2.0 %collective-permute-done.13.refs_6_ = bf16[256,512]{1,0:T(8,128)(2,1)S(1)} collective-permute-done((bf16[256,512]{1,0:T(8,128)(2,1)S(1)}, bf16[256,512]{1,0:T(8,128)(2,1)S(1)}, u32[]{:S(2)}, u32[]{:S(2)}) %collective-permute-start.13) | collective-permute-done | bytes 262176 | tf_op jit(solution)/shard_map/ppermute | solution.py:415
  35.9 2.8 %shard_map.91 = (bf16[256,1024]{1,0:T(8,128)(2,1)S(1)}, f32[2,8,128]{2,1,0:T(8,128)S(1)}, f32[2,1,512]{2,1,0:T(1,128)S(1)}, f32[2,1,512]{2,1,0:T(1,128)S(1)}, f32[2,128,512]{2,1,0:T(8,128)S(1)}) custom-call(bf16[256,1024]{1,0:T(8,128)(2,1)S(1)} %get-tuple-element.52.refs_0_, bf16[128,1024]{1,0:T(8,128)(2,1)S(1)} %get-tuple-element.53.refs_1_, ...), custom_call_target="tpu_custom_call" | custom-call | flops 1024 | bytes 1024 | tf_op jit(solution)/shard_map/pallas_call | solution.py:434
  38.7 2.2 %shard_map.92 = (bf16[128,1024]{1,0:T(8,128)(2,1)S(1)}, f32[1,8,128]{2,1,0:T(8,128)S(1)}, f32[2,1,512]{2,1,0:T(1,128)S(1)}, f32[2,1,512]{2,1,0:T(1,128)S(1)}, f3...) custom-call(bf16[256,1024]{1,0:T(8,128)(2,1)S(1)} %get-tuple-element.52.refs_0_, ...), custom_call_target="tpu_custom_call" | custom-call | flops 1024 | bytes 1024 | tf_op jit(solution)/shard_map/pallas_call | solution.py:442
  40.8 0.2 collective-permute-done.12.prior_ref
  41.1 0.8 %shard_map.93 = (bf16[128,1024]{1,0:T(8,128)(2,1)S(1)}, bf16[8,8,128]{2,1,0:T(8,128)(2,1)S(1)}) custom-call(bf16[128,1024]{1,0:T(8,128)(2,1)S(1)} %shard_map.89.refs_2_.q_ref, bf16[128,512]{1,0:T(8,128)(2,1)S(1)} %collective-permute-done.12.prior_ref, s32[4,128]{1,0:T(4,128)S(1)} %get-tuple-element.51.refs_7_.refs_8_.bounds_ref, ...), custom_call_target="tpu_custom_call" | custom-call | flops 1024 | bytes 1024 | tf_op jit(solution)/shard_map/pallas_call | solution.py:451
  41.8 9.4 %all_to_all.5.recv_ref = bf16[8,8,128]{2,1,0:T(8,128)(2,1)S(1)} all-to-all(bf16[8,8,128]{2,1,0:T(8,128)(2,1)S(1)} %get-tuple-element.66), channel_id=1, replica_groups=mesh['attn'=8,'proj'=4] {'attn'}, dimensions={0} | all-to-all | bytes 32768 | tf_op jit(solution)/shard_map/all_to_all | solution.py:460
  51.2 0.8 %shard_map.94 = (f32[4,8,128]{2,1,0:T(8,128)}, bf16[512,1024]{1,0:T(8,128)(2,1)}) custom-call(bf16[8,8,128]{2,1,0:T(8,128)(2,1)S(1)} %all_to_all.5.recv_ref, bf16[128,1024]{1,0:T(8,128)(2,1)S(1)} %get-tuple-element.67.here_ref, bf16[128,1024]{1,0:T(8,128)(2,1)S(1)} %get-tuple-element.68.below_ref, ...), custom_call_target="tpu_custom_call", output_to_operand_aliasing={{1}: (3, {})} | custom-call | tf_op jit(solution)/shard_map/pallas_call | solution.py:461
  (25 shorter events, 0.2 us)
Async XLA Ops:
  0.6 6.3 %copy-start = (bf16[512,1024]{1,0:T(8,128)(2,1)S(1)}, bf16[512,1024]{1,0:T(8,128)(2,1)}, u32[]{:S(2)}) copy-start(bf16[512,1024]{1,0:T(8,128)(2,1)} %x_ref.1) | copy-start | bytes 3145732
  0.6 6.1 %copy-start.4 = (f32[4096]{0:T(1024)S(1)}, f32[4096]{0:T(1024)}, u32[]{:S(2)}) copy-start(f32[4096]{0:T(1024)} %param.8) | copy-start | bytes 49156
  0.7 6.2 %copy-start.1 = (s32[32]{0:T(128)S(1)}, s32[32]{0:T(128)}, u32[]{:S(2)}) copy-start(s32[32]{0:T(128)} %docs_ref.1) | copy-start | bytes 388
  0.7 6.2 %copy-start.2 = (s32[4]{0:T(128)S(1)}, s32[4]{0:T(128)}, u32[]{:S(2)}) copy-start(s32[4]{0:T(128)} %server_ref.1) | copy-start | bytes 52
  0.7 6.2 %collective-permute-start.1 = (bf16[512,1024]{1,0:T(8,128)(2,1)}, bf16[512,1024]{1,0:T(8,128)(2,1)S(1)}, u32[]{:S(2)}, u32[]{:S(2)}) collective-permute-start(bf16[512,1024]{1,0:T(8,128)(2,1)} %x_ref.1), channel_id=1, source_target_pairs={{0,1},{1,0},{2,3},{3,2},{4,5},{5,4},{6,7},{7,6},{8,9},{9,8},{10,11... | collective-permute-start | bytes 3145736 | tf_op jit(solution)/shard_map/ppermute | solution.py:382
  2.3 15.4 %collective-permute-start = (bf16[256,1024]{1,0:T(8,128)(2,1)S(1)}, bf16[256,1024]{1,0:T(8,128)(2,1)S(1)}, u32[]{:S(2)}, u32[]{:S(2)}) collective-permute-start(bf16[256,1024]{1,0:T(8,128)(2,1)S(1)} %slice.33), channel_id=1, source_target_pairs={{0,2},{1,3},{2,0},{3,1},{4,6},{5,7},{6,4},{7,5},{8,10},{9,11},{10,... | collective-permute-start | bytes 1572872 | tf_op jit(solution)/shard_map/ppermute | solution.py:381
  6.8 16.5 %collective-permute-start.6 = (bf16[128,1024]{1,0:T(8,128)(2,1)}, bf16[128,1024]{1,0:T(8,128)(2,1)S(1)}, u32[]{:S(2)}, u32[]{:S(2)}) collective-permute-start(bf16[128,1024]{1,0:T(8,128)(2,1)} %get-tuple-element.73), channel_id=1, source_target_pairs={{0,2},{1,3},{2,0},{3,1},{4,6},{5,7},{6,4},{7,5},{8,10},{9,11},{10,... | collective-permute-start | bytes 786440 | tf_op jit(solution)/shard_map/ppermute | solution.py:381
  6.9 12.3 %copy-start.3 = (bf16[128,1024]{1,0:T(8,128)(2,1)S(1)}, bf16[128,1024]{1,0:T(8,128)(2,1)}, u32[]{:S(2)}) copy-start(bf16[128,1024]{1,0:T(8,128)(2,1)} %get-tuple-element.72) | copy-start | bytes 786436
  17.7 1.4 %collective-permute-start.2 = (bf16[64,1024]{1,0:T(8,128)(2,1)S(1)}, bf16[64,1024]{1,0:T(8,128)(2,1)S(1)}, u32[]{:S(2)}, u32[]{:S(2)}) collective-permute-start(bf16[64,1024]{1,0:T(8,128)(2,1)S(1)} %get-tuple-element.77), channel_id=1, source_target_pairs={{0,1},{1,0},{2,3},{3,2},{4,5},{5,4},{6,7},{7,6},{8,9},{9,8},{10,11... | collective-permute-start | bytes 393224 | tf_op jit(solution)/shard_map/ppermute | solution.py:407
  17.8 3.3 %collective-permute-start.3 = (bf16[64,1024]{1,0:T(8,128)(2,1)S(1)}, bf16[64,1024]{1,0:T(8,128)(2,1)S(1)}, u32[]{:S(2)}, u32[]{:S(2)}) collective-permute-start(bf16[64,1024]{1,0:T(8,128)(2,1)S(1)} %get-tuple-element.76), channel_id=1, source_target_pairs={{0,1},{1,0},{2,3},{3,2},{4,5},{5,4},{6,7},{7,6},{8,9},{9,8},{10,11... | collective-permute-start | bytes 393224 | tf_op jit(solution)/shard_map/ppermute | solution.py:407
  18.3 2.8 %collective-permute-start.4 = (bf16[64,1024]{1,0:T(8,128)(2,1)S(1)}, bf16[64,1024]{1,0:T(8,128)(2,1)S(1)}, u32[]{:S(2)}, u32[]{:S(2)}) collective-permute-start(bf16[64,1024]{1,0:T(8,128)(2,1)S(1)} %get-tuple-element.75), channel_id=1, source_target_pairs={{0,1},{1,0},{2,3},{3,2},{4,5},{5,4},{6,7},{7,6},{8,9},{9,8},{10,11... | collective-permute-start | bytes 393224 | tf_op jit(solution)/shard_map/ppermute | solution.py:407
  18.4 2.7 %collective-permute-start.5 = (bf16[64,1024]{1,0:T(8,128)(2,1)S(1)}, bf16[64,1024]{1,0:T(8,128)(2,1)S(1)}, u32[]{:S(2)}, u32[]{:S(2)}) collective-permute-start(bf16[64,1024]{1,0:T(8,128)(2,1)S(1)} %get-tuple-element.74), channel_id=1, source_target_pairs={{0,1},{1,0},{2,3},{3,2},{4,5},{5,4},{6,7},{7,6},{8,9},{9,8},{10,11... | collective-permute-start | bytes 393224 | tf_op jit(solution)/shard_map/ppermute | solution.py:407
  19.1 9.5 %collective-permute-start.9 = (bf16[128,1024]{1,0:T(8,128)(2,1)S(1)}, bf16[128,1024]{1,0:T(8,128)(2,1)S(1)}, u32[]{:S(2)}, u32[]{:S(2)}) collective-permute-start(bf16[128,1024]{1,0:T(8,128)(2,1)S(1)} %copy-done.3), channel_id=1, source_target_pairs={{0,2},{1,3},{2,0},{3,1},{4,6},{5,7},{6,4},{7,5},{8,10},{9,11},{10,... | collective-permute-start | bytes 786440 | tf_op jit(solution)/shard_map/ppermute | solution.py:381
  23.3 2.6 %collective-permute-start.7 = (bf16[64,1024]{1,0:T(8,128)(2,1)S(1)}, bf16[64,1024]{1,0:T(8,128)(2,1)S(1)}, u32[]{:S(2)}, u32[]{:S(2)}) collective-permute-start(bf16[64,1024]{1,0:T(8,128)(2,1)S(1)} %get-tuple-element.81), channel_id=1, source_target_pairs={{0,1},{1,0},{2,3},{3,2},{4,5},{5,4},{6,7},{7,6},{8,9},{9,8},{10,11... | collective-permute-start | bytes 393224 | tf_op jit(solution)/shard_map/ppermute | solution.py:407
  23.4 2.5 %collective-permute-start.8 = (bf16[64,1024]{1,0:T(8,128)(2,1)S(1)}, bf16[64,1024]{1,0:T(8,128)(2,1)S(1)}, u32[]{:S(2)}, u32[]{:S(2)}) collective-permute-start(bf16[64,1024]{1,0:T(8,128)(2,1)S(1)} %get-tuple-element.80), channel_id=1, source_target_pairs={{0,1},{1,0},{2,3},{3,2},{4,5},{5,4},{6,7},{7,6},{8,9},{9,8},{10,11... | collective-permute-start | bytes 393224 | tf_op jit(solution)/shard_map/ppermute | solution.py:407
  23.9 12.0 %collective-permute-start.13 = (bf16[256,512]{1,0:T(8,128)(2,1)S(1)}, bf16[256,512]{1,0:T(8,128)(2,1)S(1)}, u32[]{:S(2)}, u32[]{:S(2)}) collective-permute-start(bf16[256,512]{1,0:T(8,128)(2,1)S(1)} %get-tuple-element.54.refs_3_), channel_id=1, source_target_pairs={{0,4},{4,8},{8,12},{12,16},{16,20},{20,24},{24,28},{28,0},{1,5},{5... | collective-permute-start | bytes 786440 | tf_op jit(solution)/shard_map/ppermute | solution.py:415
  28.7 2.4 %collective-permute-start.10 = (bf16[64,1024]{1,0:T(8,128)(2,1)S(1)}, bf16[64,1024]{1,0:T(8,128)(2,1)S(1)}, u32[]{:S(2)}, u32[]{:S(2)}) collective-permute-start(bf16[64,1024]{1,0:T(8,128)(2,1)S(1)} %get-tuple-element.79), channel_id=1, source_target_pairs={{0,1},{1,0},{2,3},{3,2},{4,5},{5,4},{6,7},{7,6},{8,9},{9,8},{10,11... | collective-permute-start | bytes 393224 | tf_op jit(solution)/shard_map/ppermute | solution.py:407
  28.8 2.3 %collective-permute-start.11 = (bf16[64,1024]{1,0:T(8,128)(2,1)S(1)}, bf16[64,1024]{1,0:T(8,128)(2,1)S(1)}, u32[]{:S(2)}, u32[]{:S(2)}) collective-permute-start(bf16[64,1024]{1,0:T(8,128)(2,1)S(1)} %get-tuple-element.78), channel_id=1, source_target_pairs={{0,1},{1,0},{2,3},{3,2},{4,5},{5,4},{6,7},{7,6},{8,9},{9,8},{10,11... | collective-permute-start | bytes 393224 | tf_op jit(solution)/shard_map/ppermute | solution.py:407
  29.3 9.4 %collective-permute-start.14 = (bf16[128,512]{1,0:T(8,128)(2,1)S(1)}, bf16[128,512]{1,0:T(8,128)(2,1)S(1)}, u32[]{:S(2)}, u32[]{:S(2)}) collective-permute-start(bf16[128,512]{1,0:T(8,128)(2,1)S(1)} %get-tuple-element.55.refs_4_), channel_id=1, source_target_pairs={{0,4},{4,8},{8,12},{12,16},{16,20},{20,24},{24,28},{28,0},{1,5},{5... | collective-permute-start | bytes 393224 | tf_op jit(solution)/shard_map/ppermute | solution.py:415
  31.5 9.6 %collective-permute-start.12 = (bf16[128,512]{1,0:T(8,128)(2,1)S(1)}, bf16[128,512]{1,0:T(8,128)(2,1)S(1)}, u32[]{:S(2)}, u32[]{:S(2)}) collective-permute-start(bf16[128,512]{1,0:T(8,128)(2,1)S(1)} %shard_map.90.refs_5_), channel_id=1, source_target_pairs={{0,4},{4,8},{8,12},{12,16},{16,20},{20,24},{24,28},{28,0},{1,5},{5... | collective-permute-start | bytes 393224 | tf_op jit(solution)/shard_map/ppermute | solution.py:415

commit v8 on v7

--- a/solution.py
+++ b/solution.py
@@ -406,11 +406,7 @@
             pieces = [piece[i:j] for i, j in zip(cuts, [*cuts[1:], piece.shape[0]])]
             groups += [[piece], [lax.ppermute(part, "proj", sibling) for part in pieces]]
         rest = (high - low, low, groups, gain_rest, squares)
-        if low:
-            kv, q = project(*rest, (wkv_rest, kv_acc), (wq_rest, q_acc))
-        else:
-            (kv,) = project(*rest, (wkv_rest, kv_acc))
-            (q,) = project(*rest, (wq_rest, q_acc))
+        kv, q = project(*rest, (wkv_rest, kv_acc), (wq_rest, q_acc))
         tie = q
         prior.append(lax.ppermute(kv, "attn", onward))
         own.append(kv)

time: 52.3 us -> 52.3 us (level)
    pallas_call x4 -> x3, Pallas kernels: 4.33 us -> 4.16 us  [project(): pl.pallas_call(functools.partial(chunk_kernel, [len(group) for group in g...]
where the time goes in v8:
time: 52.3 us; the launch traced here: 52.1 us
  Pallas kernels  17.6 us (34%)
  starting transfers between devices  12.7 us (24%)
  blocking collectives  9.4 us (18%)
  waiting for transfers between devices  8.43 us (16%)
  local copies, waits for them, and re-layouts  3.12 us (6%)
  between operations  0.79 us (2%)
    all_to_all x1, blocking collectives, shards(): recv = lax.all_to_all(send, 'attn', split_axis=0, concat_axis=0, tiled=True)  9.4 us
    pallas_call x1, Pallas kernels, local_part(): pl.pallas_call(local_kernel, out_shape=(pltpu.VMEM((rows, q_width), jnp.f...  7 us
    ppermute x3, waiting for transfers between devices, shards(): lax.ppermute(piece, 'proj', across(d))  5.67 us
    ppermute x3, starting transfers between devices, shards(): prior.append(lax.ppermute(kv, 'attn', onward))  5.34 us
    ppermute x3, starting transfers between devices, shards(): lax.ppermute(piece, 'proj', across(d))  4.61 us
    pallas_call x3, Pallas kernels, project(): pl.pallas_call(functools.partial(chunk_kernel, [len(group) for group in g...  4.16 us
    slice x2, local copies, waits for them, and re-layouts, shards(): piece = rest[low:high]  2.93 us
    pallas_call x1, Pallas kernels, shards(): pl.pallas_call(functools.partial(high_attention_kernel, chunks, list(rang...  2.77 us
  transfers between devices with their start and end apart: 15, of which 6 were waited for; matrix products, arithmetic and copies ran while one was open for 6% of the time, Pallas kernels for 31%

profile of v8, /device:TPU:0, one launch (start us, length us, event | category | flops | bytes accessed | tf_op | source)
XLA Modules:
  0.0 52.1 jit_solution(4877786650702790698)
XLA Ops:
  0.7 0.5 collective-permute-start.1
  1.2 1.1 %slice.33 = bf16[256,1024]{1,0:T(8,128)(2,1)S(1)} slice(bf16[512,1024]{1,0:T(8,128)(2,1)} %x_ref.1), slice={[256:512], [0:1024]} | slice | bytes 1048576 | tf_op jit(solution)/shard_map/slice | solution.py:378
  2.3 2.6 %collective-permute-start = (bf16[256,1024]{1,0:T(8,128)(2,1)S(1)}, bf16[256,1024]{1,0:T(8,128)(2,1)S(1)}, u32[]{:S(2)}, u32[]{:S(2)}) collective-permute-start(bf16[256,1024]{1,0:T(8,128)(2,1)S(1)} %slice.33), channel_id=1, source_target_pairs={{0,2},{1,3},{2,0},{3,1},{4,6},{5,7},{6,4},{7,5},{8,10},{9,11},{10,... | collective-permute-start | bytes 1572872 | tf_op jit(solution)/shard_map/ppermute | solution.py:381
  4.9 1.9 %fusion = (bf16[128,1024]{1,0:T(8,128)(2,1)}, bf16[128,1024]{1,0:T(8,128)(2,1)}) fusion(bf16[512,1024]{1,0:T(8,128)(2,1)} %x_ref.1), kind=kLoop, calls=%fused_computation | loop fusion | bytes 1048576 | tf_op jit(solution)/shard_map/slice | solution.py:378
  6.8 0.1 stack.23.order_ref
  6.9 7.0 %shard_map.86 = (f32[512,1024]{1,0:T(8,128)S(1)}, f32[512,512]{1,0:T(8,128)S(1)}, f32[512,1]{1,0:T(8,128)S(1)}, s32[4,128]{1,0:T(4,128)S(1)}, s32[4,8,128]{2,1,0...) custom-call(s32[5]{0:T(128)S(1)} %stack.23.order_ref, ...), custom_call_target="tpu_custom_call" | custom-call | flops 1024 | bytes 1024 | tf_op jit(solution)/shard_map/pallas_call | solution.py:93
  13.9 3.8 %collective-permute-done.refs_0_ = bf16[256,1024]{1,0:T(8,128)(2,1)S(1)} collective-permute-done((bf16[256,1024]{1,0:T(8,128)(2,1)S(1)}, bf16[256,1024]{1,0:T(8,128)(2,1)S(1)}, u32[]{:S(2)}, u32[]{:S(2)}) %collective-permute-start) | collective-permute-done | bytes 524320 | tf_op jit(solution)/shard_map/ppermute | solution.py:381
  17.7 0.1 collective-permute-start.2
  17.8 0.5 collective-permute-start.3
  18.3 0.1 collective-permute-start.4
  18.4 0.4 collective-permute-start.5
  18.8 0.3 collective-permute-done.2.refs_1_
  19.1 2.0 %collective-permute-start.9 = (bf16[128,1024]{1,0:T(8,128)(2,1)S(1)}, bf16[128,1024]{1,0:T(8,128)(2,1)S(1)}, u32[]{:S(2)}, u32[]{:S(2)}) collective-permute-start(bf16[128,1024]{1,0:T(8,128)(2,1)S(1)} %copy-done.3), channel_id=1, source_target_pairs={{0,2},{1,3},{2,0},{3,1},{4,6},{5,7},{6,4},{7,5},{8,10},{9,11},{10,... | collective-permute-start | bytes 786440 | tf_op jit(solution)/shard_map/ppermute | solution.py:381
  21.1 1.9 %shard_map.87 = (bf16[256,512]{1,0:T(8,128)(2,1)S(1)}, bf16[256,1024]{1,0:T(8,128)(2,1)S(1)}) custom-call(bf16[256,1024]{1,0:T(8,128)(2,1)S(1)} %collective-permute-done.refs_0_, bf16[64,1024]{1,0:T(8,128)(2,1)S(1)} %collective-permute-done.2.refs_1_, bf16[64,1024]{1,0:T(8,128)(2,1)S(1)} %collective-permute-done.3.refs_2_, ...), custom_call_target="tpu_custom_call" | custom-call | flops 1024 | bytes 1024 | tf_op jit(solution)/shard_map/pallas_call | solution.py:142
  23.1 0.2 collective-permute-done.6.refs_0_
  23.3 0.1 collective-permute-start.7
  23.4 0.5 collective-permute-start.8
  23.9 2.0 %collective-permute-start.13 = (bf16[256,512]{1,0:T(8,128)(2,1)S(1)}, bf16[256,512]{1,0:T(8,128)(2,1)S(1)}, u32[]{:S(2)}, u32[]{:S(2)}) collective-permute-start(bf16[256,512]{1,0:T(8,128)(2,1)S(1)} %get-tuple-element.58.refs_3_), channel_id=1, source_target_pairs={{0,4},{4,8},{8,12},{12,16},{16,20},{20,24},{24,28},{28,0},{1,5},{5... | collective-permute-start | bytes 786440 | tf_op jit(solution)/shard_map/ppermute | solution.py:411
  25.9 1.1 %shard_map.88 = (bf16[128,512]{1,0:T(8,128)(2,1)S(1)}, bf16[128,1024]{1,0:T(8,128)(2,1)S(1)}) custom-call(bf16[128,1024]{1,0:T(8,128)(2,1)S(1)} %collective-permute-done.6.refs_0_, bf16[64,1024]{1,0:T(8,128)(2,1)S(1)} %collective-permute-done.7.refs_1_, bf16[64,1024]{1,0:T(8,128)(2,1)S(1)} %collective-permute-done.8.refs_2_, ...), custom_call_target="tpu_custom_call" | custom-call | flops 1024 | bytes 1024 | tf_op jit(solution)/shard_map/pallas_call | solution.py:142
  27.0 1.7 %collective-permute-done.9.refs_0_ = bf16[128,1024]{1,0:T(8,128)(2,1)S(1)} collective-permute-done((bf16[128,1024]{1,0:T(8,128)(2,1)S(1)}, bf16[128,1024]{1,0:T(8,128)(2,1)S(1)}, u32[]{:S(2)}, u32[]{:S(2)}) %collective-permute-start.9) | collective-permute-done | bytes 262176 | tf_op jit(solution)/shard_map/ppermute | solution.py:381
  28.7 0.1 collective-permute-start.10
  28.8 0.5 collective-permute-start.11
  29.3 1.8 %collective-permute-start.14 = (bf16[128,512]{1,0:T(8,128)(2,1)S(1)}, bf16[128,512]{1,0:T(8,128)(2,1)S(1)}, u32[]{:S(2)}, u32[]{:S(2)}) collective-permute-start(bf16[128,512]{1,0:T(8,128)(2,1)S(1)} %get-tuple-element.59.refs_4_), channel_id=1, source_target_pairs={{0,4},{4,8},{8,12},{12,16},{16,20},{20,24},{24,28},{28,0},{1,5},{5... | collective-permute-start | bytes 393224 | tf_op jit(solution)/shard_map/ppermute | solution.py:411
  31.0 1.1 %shard_map.89 = (bf16[128,512]{1,0:T(8,128)(2,1)S(1)}, bf16[128,1024]{1,0:T(8,128)(2,1)S(1)}) custom-call(bf16[128,1024]{1,0:T(8,128)(2,1)S(1)} %collective-permute-done.9.refs_0_, bf16[64,1024]{1,0:T(8,128)(2,1)S(1)} %collective-permute-done.10.refs_1_, bf16[64,1024]{1,0:T(8,128)(2,1)S(1)} %collective-permute-done.11.refs_2_, ...), custom_call_target="tpu_custom_call" | custom-call | flops 1024 | bytes 1024 | tf_op jit(solution)/shard_map/pallas_call | solution.py:142
  32.2 1.6 %collective-permute-start.12 = (bf16[128,512]{1,0:T(8,128)(2,1)S(1)}, bf16[128,512]{1,0:T(8,128)(2,1)S(1)}, u32[]{:S(2)}, u32[]{:S(2)}) collective-permute-start(bf16[128,512]{1,0:T(8,128)(2,1)S(1)} %get-tuple-element.54.refs_5_), channel_id=1, source_target_pairs={{0,4},{4,8},{8,12},{12,16},{16,20},{20,24},{24,28},{28,0},{1,5},{5... | collective-permute-start | bytes 393224 | tf_op jit(solution)/shard_map/ppermute | solution.py:411
  33.7 2.1 %collective-permute-done.13.refs_6_ = bf16[256,512]{1,0:T(8,128)(2,1)S(1)} collective-permute-done((bf16[256,512]{1,0:T(8,128)(2,1)S(1)}, bf16[256,512]{1,0:T(8,128)(2,1)S(1)}, u32[]{:S(2)}, u32[]{:S(2)}) %collective-permute-start.13) | collective-permute-done | bytes 262176 | tf_op jit(solution)/shard_map/ppermute | solution.py:411
  35.9 2.8 %shard_map.90 = (bf16[256,1024]{1,0:T(8,128)(2,1)S(1)}, f32[2,8,128]{2,1,0:T(8,128)S(1)}, f32[2,1,512]{2,1,0:T(1,128)S(1)}, f32[2,1,512]{2,1,0:T(1,128)S(1)}, f32[2,128,512]{2,1,0:T(8,128)S(1)}) custom-call(bf16[256,1024]{1,0:T(8,128)(2,1)S(1)} %get-tuple-element.56.refs_0_, bf16[128,1024]{1,0:T(8,128)(2,1)S(1)} %get-tuple-element.57.refs_1_, ...), custom_call_target="tpu_custom_call" | custom-call | flops 1024 | bytes 1024 | tf_op jit(solution)/shard_map/pallas_call | solution.py:430
  38.7 2.2 %shard_map.91 = (bf16[128,1024]{1,0:T(8,128)(2,1)S(1)}, f32[1,8,128]{2,1,0:T(8,128)S(1)}, f32[2,1,512]{2,1,0:T(1,128)S(1)}, f32[2,1,512]{2,1,0:T(1,128)S(1)}, f3...) custom-call(bf16[256,1024]{1,0:T(8,128)(2,1)S(1)} %get-tuple-element.56.refs_0_, ...), custom_call_target="tpu_custom_call" | custom-call | flops 1024 | bytes 1024 | tf_op jit(solution)/shard_map/pallas_call | solution.py:438
  40.8 0.2 collective-permute-done.12.prior_ref
  41.1 0.8 %shard_map.92 = (bf16[128,1024]{1,0:T(8,128)(2,1)S(1)}, bf16[8,8,128]{2,1,0:T(8,128)(2,1)S(1)}) custom-call(bf16[128,1024]{1,0:T(8,128)(2,1)S(1)} %get-tuple-element.53.refs_2_.q_ref, bf16[128,512]{1,0:T(8,128)(2,1)S(1)} %collective-permute-done.12.prior_ref, s32[4,128]{1,0:T(4,128)S(1)} %get-tuple-element.55.refs_7_.refs_8_.bounds_ref, ...), custom_call_target="tpu_custom_call" | custom-call | flops 1024 | bytes 1024 | tf_op jit(solution)/shard_map/pallas_call | solution.py:447
  41.8 9.4 %all_to_all.5.recv_ref = bf16[8,8,128]{2,1,0:T(8,128)(2,1)S(1)} all-to-all(bf16[8,8,128]{2,1,0:T(8,128)(2,1)S(1)} %get-tuple-element.70), channel_id=1, replica_groups=mesh['attn'=8,'proj'=4] {'attn'}, dimensions={0} | all-to-all | bytes 32768 | tf_op jit(solution)/shard_map/all_to_all | solution.py:456
  51.2 0.8 %shard_map.93 = (f32[4,8,128]{2,1,0:T(8,128)}, bf16[512,1024]{1,0:T(8,128)(2,1)}) custom-call(bf16[8,8,128]{2,1,0:T(8,128)(2,1)S(1)} %all_to_all.5.recv_ref, bf16[128,1024]{1,0:T(8,128)(2,1)S(1)} %get-tuple-element.71.here_ref, bf16[128,1024]{1,0:T(8,128)(2,1)S(1)} %get-tuple-element.72.below_ref, ...), custom_call_target="tpu_custom_call", output_to_operand_aliasing={{1}: (3, {})} | custom-call | tf_op jit(solution)/shard_map/pallas_call | solution.py:457
  (24 shorter events, 0.2 us)
Async XLA Ops:
  0.6 6.3 %copy-start = (bf16[512,1024]{1,0:T(8,128)(2,1)S(1)}, bf16[512,1024]{1,0:T(8,128)(2,1)}, u32[]{:S(2)}) copy-start(bf16[512,1024]{1,0:T(8,128)(2,1)} %x_ref.1) | copy-start | bytes 3145732
  0.6 6.1 %copy-start.4 = (f32[4096]{0:T(1024)S(1)}, f32[4096]{0:T(1024)}, u32[]{:S(2)}) copy-start(f32[4096]{0:T(1024)} %param.8) | copy-start | bytes 49156
  0.7 6.2 %copy-start.1 = (s32[32]{0:T(128)S(1)}, s32[32]{0:T(128)}, u32[]{:S(2)}) copy-start(s32[32]{0:T(128)} %docs_ref.1) | copy-start | bytes 388
  0.7 6.2 %copy-start.2 = (s32[4]{0:T(128)S(1)}, s32[4]{0:T(128)}, u32[]{:S(2)}) copy-start(s32[4]{0:T(128)} %server_ref.1) | copy-start | bytes 52
  0.7 6.2 %collective-permute-start.1 = (bf16[512,1024]{1,0:T(8,128)(2,1)}, bf16[512,1024]{1,0:T(8,128)(2,1)S(1)}, u32[]{:S(2)}, u32[]{:S(2)}) collective-permute-start(bf16[512,1024]{1,0:T(8,128)(2,1)} %x_ref.1), channel_id=1, source_target_pairs={{0,1},{1,0},{2,3},{3,2},{4,5},{5,4},{6,7},{7,6},{8,9},{9,8},{10,11... | collective-permute-start | bytes 3145736 | tf_op jit(solution)/shard_map/ppermute | solution.py:382
  2.3 15.4 %collective-permute-start = (bf16[256,1024]{1,0:T(8,128)(2,1)S(1)}, bf16[256,1024]{1,0:T(8,128)(2,1)S(1)}, u32[]{:S(2)}, u32[]{:S(2)}) collective-permute-start(bf16[256,1024]{1,0:T(8,128)(2,1)S(1)} %slice.33), channel_id=1, source_target_pairs={{0,2},{1,3},{2,0},{3,1},{4,6},{5,7},{6,4},{7,5},{8,10},{9,11},{10,... | collective-permute-start | bytes 1572872 | tf_op jit(solution)/shard_map/ppermute | solution.py:381
  6.8 16.5 %collective-permute-start.6 = (bf16[128,1024]{1,0:T(8,128)(2,1)}, bf16[128,1024]{1,0:T(8,128)(2,1)S(1)}, u32[]{:S(2)}, u32[]{:S(2)}) collective-permute-start(bf16[128,1024]{1,0:T(8,128)(2,1)} %get-tuple-element.77), channel_id=1, source_target_pairs={{0,2},{1,3},{2,0},{3,1},{4,6},{5,7},{6,4},{7,5},{8,10},{9,11},{10,... | collective-permute-start | bytes 786440 | tf_op jit(solution)/shard_map/ppermute | solution.py:381
  6.9 12.3 %copy-start.3 = (bf16[128,1024]{1,0:T(8,128)(2,1)S(1)}, bf16[128,1024]{1,0:T(8,128)(2,1)}, u32[]{:S(2)}) copy-start(bf16[128,1024]{1,0:T(8,128)(2,1)} %get-tuple-element.76) | copy-start | bytes 786436
  17.7 1.4 %collective-permute-start.2 = (bf16[64,1024]{1,0:T(8,128)(2,1)S(1)}, bf16[64,1024]{1,0:T(8,128)(2,1)S(1)}, u32[]{:S(2)}, u32[]{:S(2)}) collective-permute-start(bf16[64,1024]{1,0:T(8,128)(2,1)S(1)} %get-tuple-element.81), channel_id=1, source_target_pairs={{0,1},{1,0},{2,3},{3,2},{4,5},{5,4},{6,7},{7,6},{8,9},{9,8},{10,11... | collective-permute-start | bytes 393224 | tf_op jit(solution)/shard_map/ppermute | solution.py:407
  17.8 3.3 %collective-permute-start.3 = (bf16[64,1024]{1,0:T(8,128)(2,1)S(1)}, bf16[64,1024]{1,0:T(8,128)(2,1)S(1)}, u32[]{:S(2)}, u32[]{:S(2)}) collective-permute-start(bf16[64,1024]{1,0:T(8,128)(2,1)S(1)} %get-tuple-element.80), channel_id=1, source_target_pairs={{0,1},{1,0},{2,3},{3,2},{4,5},{5,4},{6,7},{7,6},{8,9},{9,8},{10,11... | collective-permute-start | bytes 393224 | tf_op jit(solution)/shard_map/ppermute | solution.py:407
  18.3 2.8 %collective-permute-start.4 = (bf16[64,1024]{1,0:T(8,128)(2,1)S(1)}, bf16[64,1024]{1,0:T(8,128)(2,1)S(1)}, u32[]{:S(2)}, u32[]{:S(2)}) collective-permute-start(bf16[64,1024]{1,0:T(8,128)(2,1)S(1)} %get-tuple-element.79), channel_id=1, source_target_pairs={{0,1},{1,0},{2,3},{3,2},{4,5},{5,4},{6,7},{7,6},{8,9},{9,8},{10,11... | collective-permute-start | bytes 393224 | tf_op jit(solution)/shard_map/ppermute | solution.py:407
  18.4 2.7 %collective-permute-start.5 = (bf16[64,1024]{1,0:T(8,128)(2,1)S(1)}, bf16[64,1024]{1,0:T(8,128)(2,1)S(1)}, u32[]{:S(2)}, u32[]{:S(2)}) collective-permute-start(bf16[64,1024]{1,0:T(8,128)(2,1)S(1)} %get-tuple-element.78), channel_id=1, source_target_pairs={{0,1},{1,0},{2,3},{3,2},{4,5},{5,4},{6,7},{7,6},{8,9},{9,8},{10,11... | collective-permute-start | bytes 393224 | tf_op jit(solution)/shard_map/ppermute | solution.py:407
  19.1 9.5 %collective-permute-start.9 = (bf16[128,1024]{1,0:T(8,128)(2,1)S(1)}, bf16[128,1024]{1,0:T(8,128)(2,1)S(1)}, u32[]{:S(2)}, u32[]{:S(2)}) collective-permute-start(bf16[128,1024]{1,0:T(8,128)(2,1)S(1)} %copy-done.3), channel_id=1, source_target_pairs={{0,2},{1,3},{2,0},{3,1},{4,6},{5,7},{6,4},{7,5},{8,10},{9,11},{10,... | collective-permute-start | bytes 786440 | tf_op jit(solution)/shard_map/ppermute | solution.py:381
  23.3 2.6 %collective-permute-start.7 = (bf16[64,1024]{1,0:T(8,128)(2,1)S(1)}, bf16[64,1024]{1,0:T(8,128)(2,1)S(1)}, u32[]{:S(2)}, u32[]{:S(2)}) collective-permute-start(bf16[64,1024]{1,0:T(8,128)(2,1)S(1)} %get-tuple-element.85), channel_id=1, source_target_pairs={{0,1},{1,0},{2,3},{3,2},{4,5},{5,4},{6,7},{7,6},{8,9},{9,8},{10,11... | collective-permute-start | bytes 393224 | tf_op jit(solution)/shard_map/ppermute | solution.py:407
  23.4 2.5 %collective-permute-start.8 = (bf16[64,1024]{1,0:T(8,128)(2,1)S(1)}, bf16[64,1024]{1,0:T(8,128)(2,1)S(1)}, u32[]{:S(2)}, u32[]{:S(2)}) collective-permute-start(bf16[64,1024]{1,0:T(8,128)(2,1)S(1)} %get-tuple-element.84), channel_id=1, source_target_pairs={{0,1},{1,0},{2,3},{3,2},{4,5},{5,4},{6,7},{7,6},{8,9},{9,8},{10,11... | collective-permute-start | bytes 393224 | tf_op jit(solution)/shard_map/ppermute | solution.py:407
  23.9 12.0 %collective-permute-start.13 = (bf16[256,512]{1,0:T(8,128)(2,1)S(1)}, bf16[256,512]{1,0:T(8,128)(2,1)S(1)}, u32[]{:S(2)}, u32[]{:S(2)}) collective-permute-start(bf16[256,512]{1,0:T(8,128)(2,1)S(1)} %get-tuple-element.58.refs_3_), channel_id=1, source_target_pairs={{0,4},{4,8},{8,12},{12,16},{16,20},{20,24},{24,28},{28,0},{1,5},{5... | collective-permute-start | bytes 786440 | tf_op jit(solution)/shard_map/ppermute | solution.py:411
  28.7 2.4 %collective-permute-start.10 = (bf16[64,1024]{1,0:T(8,128)(2,1)S(1)}, bf16[64,1024]{1,0:T(8,128)(2,1)S(1)}, u32[]{:S(2)}, u32[]{:S(2)}) collective-permute-start(bf16[64,1024]{1,0:T(8,128)(2,1)S(1)} %get-tuple-element.83), channel_id=1, source_target_pairs={{0,1},{1,0},{2,3},{3,2},{4,5},{5,4},{6,7},{7,6},{8,9},{9,8},{10,11... | collective-permute-start | bytes 393224 | tf_op jit(solution)/shard_map/ppermute | solution.py:407
  28.8 2.3 %collective-permute-start.11 = (bf16[64,1024]{1,0:T(8,128)(2,1)S(1)}, bf16[64,1024]{1,0:T(8,128)(2,1)S(1)}, u32[]{:S(2)}, u32[]{:S(2)}) collective-permute-start(bf16[64,1024]{1,0:T(8,128)(2,1)S(1)} %get-tuple-element.82), channel_id=1, source_target_pairs={{0,1},{1,0},{2,3},{3,2},{4,5},{5,4},{6,7},{7,6},{8,9},{9,8},{10,11... | collective-permute-start | bytes 393224 | tf_op jit(solution)/shard_map/ppermute | solution.py:407
  29.3 9.4 %collective-permute-start.14 = (bf16[128,512]{1,0:T(8,128)(2,1)S(1)}, bf16[128,512]{1,0:T(8,128)(2,1)S(1)}, u32[]{:S(2)}, u32[]{:S(2)}) collective-permute-start(bf16[128,512]{1,0:T(8,128)(2,1)S(1)} %get-tuple-element.59.refs_4_), channel_id=1, source_target_pairs={{0,4},{4,8},{8,12},{12,16},{16,20},{20,24},{24,28},{28,0},{1,5},{5... | collective-permute-start | bytes 393224 | tf_op jit(solution)/shard_map/ppermute | solution.py:411
  32.2 8.9 %collective-permute-start.12 = (bf16[128,512]{1,0:T(8,128)(2,1)S(1)}, bf16[128,512]{1,0:T(8,128)(2,1)S(1)}, u32[]{:S(2)}, u32[]{:S(2)}) collective-permute-start(bf16[128,512]{1,0:T(8,128)(2,1)S(1)} %get-tuple-element.54.refs_5_), channel_id=1, source_target_pairs={{0,4},{4,8},{8,12},{12,16},{16,20},{20,24},{24,28},{28,0},{1,5},{5... | collective-permute-start | bytes 393224 | tf_op jit(solution)/shard_map/ppermute | solution.py:411

commit v9 on v8

--- a/solution.py
+++ b/solution.py
@@ -297,12 +297,12 @@
     attend_blocks(wanted, blocks, queries, owns, priors, bounds_ref, outs, lses)
     kv_heads = highest.shape[0]
     group = highest.shape[2] // QUERY_BLOCK_ROWS
-    for n in range(kv_heads):
-        states = (highest, total, summed)
-        for b in wanted:
-            caps = prior_caps(bounds_ref, b, blocks, group)
-            values = merge_keys(n, priors[b], queries[0], caps, states)
-            states = (highest_ref, total_ref, summed_ref)
+    states = (highest, total, summed)
+    for b in wanted:
+        caps = prior_caps(bounds_ref, b, blocks, group)
+        merged = [merge_keys(n, priors[b], queries[0], caps, states) for n in range(kv_heads)]
+        states = (highest_ref, total_ref, summed_ref)
+        for n, values in enumerate(merged):
             for ref, value in zip(states, values):
                 ref[n] = value
     copy.wait()
@@ -314,8 +314,8 @@
     kv_heads = states[0].shape[0]
     group = states[0].shape[2] // block
     caps = prior_caps(bounds_ref, 0, blocks, group)
-    for n in range(kv_heads):
-        highest, total, summed = merge_keys(n, [(prior_ref, 0, block)], [(q_ref, 0, block)], caps, states)
+    merged = [merge_keys(n, [(prior_ref, 0, block)], [(q_ref, 0, block)], caps, states) for n in range(kv_heads)]
+    for n, (highest, total, summed) in enumerate(merged):
         result = (summed / total).astype(jnp.bfloat16)
         lse = highest * score_scale + jnp.log(total)
         for g in range(group):

time: 52.3 us -> 52.3 us (level)
  no operation moved by 1% of the time
where the time goes in v9:
time: 52.3 us; the launch traced here: 52.1 us
  Pallas kernels  17.5 us (33%)
  starting transfers between devices  12.7 us (24%)
  blocking collectives  9.4 us (18%)
  waiting for transfers between devices  8.57 us (16%)
  local copies, waits for them, and re-layouts  3.12 us (6%)
  between operations  0.79 us (2%)
    all_to_all x1, blocking collectives, shards(): recv = lax.all_to_all(send, 'attn', split_axis=0, concat_axis=0, tiled=True)  9.4 us
    pallas_call x1, Pallas kernels, local_part(): pl.pallas_call(local_kernel, out_shape=(pltpu.VMEM((rows, q_width), jnp.f...  7 us
    ppermute x3, waiting for transfers between devices, shards(): lax.ppermute(piece, 'proj', across(d))  5.67 us
    ppermute x3, starting transfers between devices, shards(): prior.append(lax.ppermute(kv, 'attn', onward))  5.34 us
    ppermute x3, starting transfers between devices, shards(): lax.ppermute(piece, 'proj', across(d))  4.61 us
    pallas_call x3, Pallas kernels, project(): pl.pallas_call(functools.partial(chunk_kernel, [len(group) for group in g...  4.16 us
    slice x2, local copies, waits for them, and re-layouts, shards(): piece = rest[low:high]  2.93 us
    pallas_call x1, Pallas kernels, shards(): pl.pallas_call(functools.partial(high_attention_kernel, chunks, list(rang...  2.77 us
  transfers between devices with their start and end apart: 15, of which 6 were waited for; matrix products, arithmetic and copies ran while one was open for 6% of the time, Pallas kernels for 31%

profile of v9, /device:TPU:0, one launch (start us, length us, event | category | flops | bytes accessed | tf_op | source)
XLA Modules:
  0.0 52.1 jit_solution(14092288165392280894)
XLA Ops:
  0.7 0.5 collective-permute-start.1
  1.2 1.1 %slice.33 = bf16[256,1024]{1,0:T(8,128)(2,1)S(1)} slice(bf16[512,1024]{1,0:T(8,128)(2,1)} %x_ref.1), slice={[256:512], [0:1024]} | slice | bytes 1048576 | tf_op jit(solution)/shard_map/slice | solution.py:378
  2.3 2.6 %collective-permute-start = (bf16[256,1024]{1,0:T(8,128)(2,1)S(1)}, bf16[256,1024]{1,0:T(8,128)(2,1)S(1)}, u32[]{:S(2)}, u32[]{:S(2)}) collective-permute-start(bf16[256,1024]{1,0:T(8,128)(2,1)S(1)} %slice.33), channel_id=1, source_target_pairs={{0,2},{1,3},{2,0},{3,1},{4,6},{5,7},{6,4},{7,5},{8,10},{9,11},{10,... | collective-permute-start | bytes 1572872 | tf_op jit(solution)/shard_map/ppermute | solution.py:381
  4.9 1.9 %fusion = (bf16[128,1024]{1,0:T(8,128)(2,1)}, bf16[128,1024]{1,0:T(8,128)(2,1)}) fusion(bf16[512,1024]{1,0:T(8,128)(2,1)} %x_ref.1), kind=kLoop, calls=%fused_computation | loop fusion | bytes 1048576 | tf_op jit(solution)/shard_map/slice | solution.py:378
  6.8 0.1 stack.23.order_ref
  6.9 7.0 %shard_map.86 = (f32[512,1024]{1,0:T(8,128)S(1)}, f32[512,512]{1,0:T(8,128)S(1)}, f32[512,1]{1,0:T(8,128)S(1)}, s32[4,128]{1,0:T(4,128)S(1)}, s32[4,8,128]{2,1,0...) custom-call(s32[5]{0:T(128)S(1)} %stack.23.order_ref, ...), custom_call_target="tpu_custom_call" | custom-call | flops 1024 | bytes 1024 | tf_op jit(solution)/shard_map/pallas_call | solution.py:93
  13.9 3.8 %collective-permute-done.refs_0_ = bf16[256,1024]{1,0:T(8,128)(2,1)S(1)} collective-permute-done((bf16[256,1024]{1,0:T(8,128)(2,1)S(1)}, bf16[256,1024]{1,0:T(8,128)(2,1)S(1)}, u32[]{:S(2)}, u32[]{:S(2)}) %collective-permute-start) | collective-permute-done | bytes 524320 | tf_op jit(solution)/shard_map/ppermute | solution.py:381
  17.7 0.1 collective-permute-start.2
  17.8 0.5 collective-permute-start.3
  18.3 0.1 collective-permute-start.4
  18.4 0.4 collective-permute-start.5
  18.8 0.3 collective-permute-done.2.refs_1_
  19.1 2.0 %collective-permute-start.9 = (bf16[128,1024]{1,0:T(8,128)(2,1)S(1)}, bf16[128,1024]{1,0:T(8,128)(2,1)S(1)}, u32[]{:S(2)}, u32[]{:S(2)}) collective-permute-start(bf16[128,1024]{1,0:T(8,128)(2,1)S(1)} %copy-done.3), channel_id=1, source_target_pairs={{0,2},{1,3},{2,0},{3,1},{4,6},{5,7},{6,4},{7,5},{8,10},{9,11},{10,... | collective-permute-start | bytes 786440 | tf_op jit(solution)/shard_map/ppermute | solution.py:381
  21.1 1.9 %shard_map.87 = (bf16[256,512]{1,0:T(8,128)(2,1)S(1)}, bf16[256,1024]{1,0:T(8,128)(2,1)S(1)}) custom-call(bf16[256,1024]{1,0:T(8,128)(2,1)S(1)} %collective-permute-done.refs_0_, bf16[64,1024]{1,0:T(8,128)(2,1)S(1)} %collective-permute-done.2.refs_1_, bf16[64,1024]{1,0:T(8,128)(2,1)S(1)} %collective-permute-done.3.refs_2_, ...), custom_call_target="tpu_custom_call" | custom-call | flops 1024 | bytes 1024 | tf_op jit(solution)/shard_map/pallas_call | solution.py:142
  23.1 0.2 collective-permute-done.6.refs_0_
  23.3 0.1 collective-permute-start.7
  23.4 0.5 collective-permute-start.8
  23.9 2.0 %collective-permute-start.13 = (bf16[256,512]{1,0:T(8,128)(2,1)S(1)}, bf16[256,512]{1,0:T(8,128)(2,1)S(1)}, u32[]{:S(2)}, u32[]{:S(2)}) collective-permute-start(bf16[256,512]{1,0:T(8,128)(2,1)S(1)} %get-tuple-element.58.refs_3_), channel_id=1, source_target_pairs={{0,4},{4,8},{8,12},{12,16},{16,20},{20,24},{24,28},{28,0},{1,5},{5... | collective-permute-start | bytes 786440 | tf_op jit(solution)/shard_map/ppermute | solution.py:411
  25.9 1.1 %shard_map.88 = (bf16[128,512]{1,0:T(8,128)(2,1)S(1)}, bf16[128,1024]{1,0:T(8,128)(2,1)S(1)}) custom-call(bf16[128,1024]{1,0:T(8,128)(2,1)S(1)} %collective-permute-done.6.refs_0_, bf16[64,1024]{1,0:T(8,128)(2,1)S(1)} %collective-permute-done.7.refs_1_, bf16[64,1024]{1,0:T(8,128)(2,1)S(1)} %collective-permute-done.8.refs_2_, ...), custom_call_target="tpu_custom_call" | custom-call | flops 1024 | bytes 1024 | tf_op jit(solution)/shard_map/pallas_call | solution.py:142
  27.0 1.7 %collective-permute-done.9.refs_0_ = bf16[128,1024]{1,0:T(8,128)(2,1)S(1)} collective-permute-done((bf16[128,1024]{1,0:T(8,128)(2,1)S(1)}, bf16[128,1024]{1,0:T(8,128)(2,1)S(1)}, u32[]{:S(2)}, u32[]{:S(2)}) %collective-permute-start.9) | collective-permute-done | bytes 262176 | tf_op jit(solution)/shard_map/ppermute | solution.py:381
  28.7 0.1 collective-permute-start.10
  28.8 0.5 collective-permute-start.11
  29.3 1.8 %collective-permute-start.14 = (bf16[128,512]{1,0:T(8,128)(2,1)S(1)}, bf16[128,512]{1,0:T(8,128)(2,1)S(1)}, u32[]{:S(2)}, u32[]{:S(2)}) collective-permute-start(bf16[128,512]{1,0:T(8,128)(2,1)S(1)} %get-tuple-element.59.refs_4_), channel_id=1, source_target_pairs={{0,4},{4,8},{8,12},{12,16},{16,20},{20,24},{24,28},{28,0},{1,5},{5... | collective-permute-start | bytes 393224 | tf_op jit(solution)/shard_map/ppermute | solution.py:411
  31.0 1.1 %shard_map.89 = (bf16[128,512]{1,0:T(8,128)(2,1)S(1)}, bf16[128,1024]{1,0:T(8,128)(2,1)S(1)}) custom-call(bf16[128,1024]{1,0:T(8,128)(2,1)S(1)} %collective-permute-done.9.refs_0_, bf16[64,1024]{1,0:T(8,128)(2,1)S(1)} %collective-permute-done.10.refs_1_, bf16[64,1024]{1,0:T(8,128)(2,1)S(1)} %collective-permute-done.11.refs_2_, ...), custom_call_target="tpu_custom_call" | custom-call | flops 1024 | bytes 1024 | tf_op jit(solution)/shard_map/pallas_call | solution.py:142
  32.2 1.6 %collective-permute-start.12 = (bf16[128,512]{1,0:T(8,128)(2,1)S(1)}, bf16[128,512]{1,0:T(8,128)(2,1)S(1)}, u32[]{:S(2)}, u32[]{:S(2)}) collective-permute-start(bf16[128,512]{1,0:T(8,128)(2,1)S(1)} %get-tuple-element.54.refs_5_), channel_id=1, source_target_pairs={{0,4},{4,8},{8,12},{12,16},{16,20},{20,24},{24,28},{28,0},{1,5},{5... | collective-permute-start | bytes 393224 | tf_op jit(solution)/shard_map/ppermute | solution.py:411
  33.7 2.1 %collective-permute-done.13.refs_6_ = bf16[256,512]{1,0:T(8,128)(2,1)S(1)} collective-permute-done((bf16[256,512]{1,0:T(8,128)(2,1)S(1)}, bf16[256,512]{1,0:T(8,128)(2,1)S(1)}, u32[]{:S(2)}, u32[]{:S(2)}) %collective-permute-start.13) | collective-permute-done | bytes 262176 | tf_op jit(solution)/shard_map/ppermute | solution.py:411
  35.9 2.8 %shard_map.90 = (bf16[256,1024]{1,0:T(8,128)(2,1)S(1)}, f32[2,8,128]{2,1,0:T(8,128)S(1)}, f32[2,1,512]{2,1,0:T(1,128)S(1)}, f32[2,1,512]{2,1,0:T(1,128)S(1)}, f32[2,128,512]{2,1,0:T(8,128)S(1)}) custom-call(bf16[256,1024]{1,0:T(8,128)(2,1)S(1)} %get-tuple-element.56.refs_0_, bf16[128,1024]{1,0:T(8,128)(2,1)S(1)} %get-tuple-element.57.refs_1_, ...), custom_call_target="tpu_custom_call" | custom-call | flops 1024 | bytes 1024 | tf_op jit(solution)/shard_map/pallas_call | solution.py:430
  38.7 2.0 %shard_map.91 = (bf16[128,1024]{1,0:T(8,128)(2,1)S(1)}, f32[1,8,128]{2,1,0:T(8,128)S(1)}, f32[2,1,512]{2,1,0:T(1,128)S(1)}, f32[2,1,512]{2,1,0:T(1,128)S(1)}, f3...) custom-call(bf16[256,1024]{1,0:T(8,128)(2,1)S(1)} %get-tuple-element.56.refs_0_, ...), custom_call_target="tpu_custom_call" | custom-call | flops 1024 | bytes 1024 | tf_op jit(solution)/shard_map/pallas_call | solution.py:438
  40.7 0.4 collective-permute-done.12.prior_ref
  41.1 0.8 %shard_map.92 = (bf16[128,1024]{1,0:T(8,128)(2,1)S(1)}, bf16[8,8,128]{2,1,0:T(8,128)(2,1)S(1)}) custom-call(bf16[128,1024]{1,0:T(8,128)(2,1)S(1)} %get-tuple-element.53.refs_2_.q_ref, bf16[128,512]{1,0:T(8,128)(2,1)S(1)} %collective-permute-done.12.prior_ref, s32[4,128]{1,0:T(4,128)S(1)} %get-tuple-element.55.refs_7_.refs_8_.bounds_ref, ...), custom_call_target="tpu_custom_call" | custom-call | flops 1024 | bytes 1024 | tf_op jit(solution)/shard_map/pallas_call | solution.py:447
  41.8 9.4 %all_to_all.5.recv_ref = bf16[8,8,128]{2,1,0:T(8,128)(2,1)S(1)} all-to-all(bf16[8,8,128]{2,1,0:T(8,128)(2,1)S(1)} %get-tuple-element.70), channel_id=1, replica_groups=mesh['attn'=8,'proj'=4] {'attn'}, dimensions={0} | all-to-all | bytes 32768 | tf_op jit(solution)/shard_map/all_to_all | solution.py:456
  51.2 0.8 %shard_map.93 = (f32[4,8,128]{2,1,0:T(8,128)}, bf16[512,1024]{1,0:T(8,128)(2,1)}) custom-call(bf16[8,8,128]{2,1,0:T(8,128)(2,1)S(1)} %all_to_all.5.recv_ref, bf16[128,1024]{1,0:T(8,128)(2,1)S(1)} %get-tuple-element.71.here_ref, bf16[128,1024]{1,0:T(8,128)(2,1)S(1)} %get-tuple-element.72.below_ref, ...), custom_call_target="tpu_custom_call", output_to_operand_aliasing={{1}: (3, {})} | custom-call | tf_op jit(solution)/shard_map/pallas_call | solution.py:457
  (24 shorter events, 0.2 us)
Async XLA Ops:
  0.6 6.3 %copy-start = (bf16[512,1024]{1,0:T(8,128)(2,1)S(1)}, bf16[512,1024]{1,0:T(8,128)(2,1)}, u32[]{:S(2)}) copy-start(bf16[512,1024]{1,0:T(8,128)(2,1)} %x_ref.1) | copy-start | bytes 3145732
  0.6 6.1 %copy-start.4 = (f32[4096]{0:T(1024)S(1)}, f32[4096]{0:T(1024)}, u32[]{:S(2)}) copy-start(f32[4096]{0:T(1024)} %param.8) | copy-start | bytes 49156
  0.7 6.2 %copy-start.1 = (s32[32]{0:T(128)S(1)}, s32[32]{0:T(128)}, u32[]{:S(2)}) copy-start(s32[32]{0:T(128)} %docs_ref.1) | copy-start | bytes 388
  0.7 6.2 %copy-start.2 = (s32[4]{0:T(128)S(1)}, s32[4]{0:T(128)}, u32[]{:S(2)}) copy-start(s32[4]{0:T(128)} %server_ref.1) | copy-start | bytes 52
  0.7 6.2 %collective-permute-start.1 = (bf16[512,1024]{1,0:T(8,128)(2,1)}, bf16[512,1024]{1,0:T(8,128)(2,1)S(1)}, u32[]{:S(2)}, u32[]{:S(2)}) collective-permute-start(bf16[512,1024]{1,0:T(8,128)(2,1)} %x_ref.1), channel_id=1, source_target_pairs={{0,1},{1,0},{2,3},{3,2},{4,5},{5,4},{6,7},{7,6},{8,9},{9,8},{10,11... | collective-permute-start | bytes 3145736 | tf_op jit(solution)/shard_map/ppermute | solution.py:382
  2.3 15.4 %collective-permute-start = (bf16[256,1024]{1,0:T(8,128)(2,1)S(1)}, bf16[256,1024]{1,0:T(8,128)(2,1)S(1)}, u32[]{:S(2)}, u32[]{:S(2)}) collective-permute-start(bf16[256,1024]{1,0:T(8,128)(2,1)S(1)} %slice.33), channel_id=1, source_target_pairs={{0,2},{1,3},{2,0},{3,1},{4,6},{5,7},{6,4},{7,5},{8,10},{9,11},{10,... | collective-permute-start | bytes 1572872 | tf_op jit(solution)/shard_map/ppermute | solution.py:381
  6.8 16.5 %collective-permute-start.6 = (bf16[128,1024]{1,0:T(8,128)(2,1)}, bf16[128,1024]{1,0:T(8,128)(2,1)S(1)}, u32[]{:S(2)}, u32[]{:S(2)}) collective-permute-start(bf16[128,1024]{1,0:T(8,128)(2,1)} %get-tuple-element.77), channel_id=1, source_target_pairs={{0,2},{1,3},{2,0},{3,1},{4,6},{5,7},{6,4},{7,5},{8,10},{9,11},{10,... | collective-permute-start | bytes 786440 | tf_op jit(solution)/shard_map/ppermute | solution.py:381
  6.9 12.3 %copy-start.3 = (bf16[128,1024]{1,0:T(8,128)(2,1)S(1)}, bf16[128,1024]{1,0:T(8,128)(2,1)}, u32[]{:S(2)}) copy-start(bf16[128,1024]{1,0:T(8,128)(2,1)} %get-tuple-element.76) | copy-start | bytes 786436
  17.7 1.4 %collective-permute-start.2 = (bf16[64,1024]{1,0:T(8,128)(2,1)S(1)}, bf16[64,1024]{1,0:T(8,128)(2,1)S(1)}, u32[]{:S(2)}, u32[]{:S(2)}) collective-permute-start(bf16[64,1024]{1,0:T(8,128)(2,1)S(1)} %get-tuple-element.81), channel_id=1, source_target_pairs={{0,1},{1,0},{2,3},{3,2},{4,5},{5,4},{6,7},{7,6},{8,9},{9,8},{10,11... | collective-permute-start | bytes 393224 | tf_op jit(solution)/shard_map/ppermute | solution.py:407
  17.8 3.3 %collective-permute-start.3 = (bf16[64,1024]{1,0:T(8,128)(2,1)S(1)}, bf16[64,1024]{1,0:T(8,128)(2,1)S(1)}, u32[]{:S(2)}, u32[]{:S(2)}) collective-permute-start(bf16[64,1024]{1,0:T(8,128)(2,1)S(1)} %get-tuple-element.80), channel_id=1, source_target_pairs={{0,1},{1,0},{2,3},{3,2},{4,5},{5,4},{6,7},{7,6},{8,9},{9,8},{10,11... | collective-permute-start | bytes 393224 | tf_op jit(solution)/shard_map/ppermute | solution.py:407
  18.3 2.8 %collective-permute-start.4 = (bf16[64,1024]{1,0:T(8,128)(2,1)S(1)}, bf16[64,1024]{1,0:T(8,128)(2,1)S(1)}, u32[]{:S(2)}, u32[]{:S(2)}) collective-permute-start(bf16[64,1024]{1,0:T(8,128)(2,1)S(1)} %get-tuple-element.79), channel_id=1, source_target_pairs={{0,1},{1,0},{2,3},{3,2},{4,5},{5,4},{6,7},{7,6},{8,9},{9,8},{10,11... | collective-permute-start | bytes 393224 | tf_op jit(solution)/shard_map/ppermute | solution.py:407
  18.4 2.7 %collective-permute-start.5 = (bf16[64,1024]{1,0:T(8,128)(2,1)S(1)}, bf16[64,1024]{1,0:T(8,128)(2,1)S(1)}, u32[]{:S(2)}, u32[]{:S(2)}) collective-permute-start(bf16[64,1024]{1,0:T(8,128)(2,1)S(1)} %get-tuple-element.78), channel_id=1, source_target_pairs={{0,1},{1,0},{2,3},{3,2},{4,5},{5,4},{6,7},{7,6},{8,9},{9,8},{10,11... | collective-permute-start | bytes 393224 | tf_op jit(solution)/shard_map/ppermute | solution.py:407
  19.1 9.5 %collective-permute-start.9 = (bf16[128,1024]{1,0:T(8,128)(2,1)S(1)}, bf16[128,1024]{1,0:T(8,128)(2,1)S(1)}, u32[]{:S(2)}, u32[]{:S(2)}) collective-permute-start(bf16[128,1024]{1,0:T(8,128)(2,1)S(1)} %copy-done.3), channel_id=1, source_target_pairs={{0,2},{1,3},{2,0},{3,1},{4,6},{5,7},{6,4},{7,5},{8,10},{9,11},{10,... | collective-permute-start | bytes 786440 | tf_op jit(solution)/shard_map/ppermute | solution.py:381
  23.3 2.6 %collective-permute-start.7 = (bf16[64,1024]{1,0:T(8,128)(2,1)S(1)}, bf16[64,1024]{1,0:T(8,128)(2,1)S(1)}, u32[]{:S(2)}, u32[]{:S(2)}) collective-permute-start(bf16[64,1024]{1,0:T(8,128)(2,1)S(1)} %get-tuple-element.85), channel_id=1, source_target_pairs={{0,1},{1,0},{2,3},{3,2},{4,5},{5,4},{6,7},{7,6},{8,9},{9,8},{10,11... | collective-permute-start | bytes 393224 | tf_op jit(solution)/shard_map/ppermute | solution.py:407
  23.4 2.5 %collective-permute-start.8 = (bf16[64,1024]{1,0:T(8,128)(2,1)S(1)}, bf16[64,1024]{1,0:T(8,128)(2,1)S(1)}, u32[]{:S(2)}, u32[]{:S(2)}) collective-permute-start(bf16[64,1024]{1,0:T(8,128)(2,1)S(1)} %get-tuple-element.84), channel_id=1, source_target_pairs={{0,1},{1,0},{2,3},{3,2},{4,5},{5,4},{6,7},{7,6},{8,9},{9,8},{10,11... | collective-permute-start | bytes 393224 | tf_op jit(solution)/shard_map/ppermute | solution.py:407
  23.9 12.0 %collective-permute-start.13 = (bf16[256,512]{1,0:T(8,128)(2,1)S(1)}, bf16[256,512]{1,0:T(8,128)(2,1)S(1)}, u32[]{:S(2)}, u32[]{:S(2)}) collective-permute-start(bf16[256,512]{1,0:T(8,128)(2,1)S(1)} %get-tuple-element.58.refs_3_), channel_id=1, source_target_pairs={{0,4},{4,8},{8,12},{12,16},{16,20},{20,24},{24,28},{28,0},{1,5},{5... | collective-permute-start | bytes 786440 | tf_op jit(solution)/shard_map/ppermute | solution.py:411
  28.7 2.4 %collective-permute-start.10 = (bf16[64,1024]{1,0:T(8,128)(2,1)S(1)}, bf16[64,1024]{1,0:T(8,128)(2,1)S(1)}, u32[]{:S(2)}, u32[]{:S(2)}) collective-permute-start(bf16[64,1024]{1,0:T(8,128)(2,1)S(1)} %get-tuple-element.83), channel_id=1, source_target_pairs={{0,1},{1,0},{2,3},{3,2},{4,5},{5,4},{6,7},{7,6},{8,9},{9,8},{10,11... | collective-permute-start | bytes 393224 | tf_op jit(solution)/shard_map/ppermute | solution.py:407
  28.8 2.3 %collective-permute-start.11 = (bf16[64,1024]{1,0:T(8,128)(2,1)S(1)}, bf16[64,1024]{1,0:T(8,128)(2,1)S(1)}, u32[]{:S(2)}, u32[]{:S(2)}) collective-permute-start(bf16[64,1024]{1,0:T(8,128)(2,1)S(1)} %get-tuple-element.82), channel_id=1, source_target_pairs={{0,1},{1,0},{2,3},{3,2},{4,5},{5,4},{6,7},{7,6},{8,9},{9,8},{10,11... | collective-permute-start | bytes 393224 | tf_op jit(solution)/shard_map/ppermute | solution.py:407
  29.3 9.4 %collective-permute-start.14 = (bf16[128,512]{1,0:T(8,128)(2,1)S(1)}, bf16[128,512]{1,0:T(8,128)(2,1)S(1)}, u32[]{:S(2)}, u32[]{:S(2)}) collective-permute-start(bf16[128,512]{1,0:T(8,128)(2,1)S(1)} %get-tuple-element.59.refs_4_), channel_id=1, source_target_pairs={{0,4},{4,8},{8,12},{12,16},{16,20},{20,24},{24,28},{28,0},{1,5},{5... | collective-permute-start | bytes 393224 | tf_op jit(solution)/shard_map/ppermute | solution.py:411
  32.2 8.9 %collective-permute-start.12 = (bf16[128,512]{1,0:T(8,128)(2,1)S(1)}, bf16[128,512]{1,0:T(8,128)(2,1)S(1)}, u32[]{:S(2)}, u32[]{:S(2)}) collective-permute-start(bf16[128,512]{1,0:T(8,128)(2,1)S(1)} %get-tuple-element.54.refs_5_), channel_id=1, source_target_pairs={{0,4},{4,8},{8,12},{12,16},{16,20},{20,24},{24,28},{28,0},{1,5},{5... | collective-permute-start | bytes 393224 | tf_op jit(solution)/shard_map/ppermute | solution.py:411
